TPU v7x, 32 devices: a whole 2x2x4 slice. The times are simulated.
32 devices in a mesh: dp: 4 (over y, x), fsdp: 8 (over z, core).
Axes of the slice: x: 2, y: 2, z: 4, core: 2. Of those that a mesh axis runs over, the one named last changes fastest.
Arguments:
- unit_states: bfloat16 [32, 1024, 1024], P(('dp', 'fsdp')), may hold values from -6 to 6
- dec_states: bfloat16 [32, 256, 1024], P(('dp', 'fsdp')), may hold values from -6 to 6
- enc_states: bfloat16 [32, 256, 1024], P(('dp', 'fsdp')), may hold values from -6 to 6
- unit_len: int32 [32], P(('dp', 'fsdp')), may hold values from 512 to 1024, as said below
- text_len: int32 [32], P(('dp', 'fsdp')), may hold values from 64 to 256, as said below
- task_flag: int32 [32], P(('dp', 'fsdp')), may hold values from 0 to 1
- cotangent: bfloat16 [32, 1024, 1024], P(('dp', 'fsdp')), may hold values from -6 to 6
- ln1_gain: bfloat16 [1024], P(('dp', 'fsdp')), may hold values from 0.25 to 1.75
- ln1_shift: bfloat16 [1024], P(('dp', 'fsdp')), may hold values from -2 to 2
- self_wq: bfloat16 [1024, 1024], P(('dp', 'fsdp')), may hold values from -0.1875 to 0.1875
- self_bq: bfloat16 [1024], P(('dp', 'fsdp')), may hold values from -2 to 2
- self_wk: bfloat16 [1024, 1024], P(('dp', 'fsdp')), may hold values from -0.1875 to 0.1875
- self_wv: bfloat16 [1024, 1024], P(('dp', 'fsdp')), may hold values from -0.1875 to 0.1875
- self_bv: bfloat16 [1024], P(('dp', 'fsdp')), may hold values from -2 to 2
- self_wo: bfloat16 [1024, 1024], P(('dp', 'fsdp')), may hold values from -0.75 to 0.75
- self_bo: bfloat16 [1024], P(('dp', 'fsdp')), may hold values from -2 to 2
- ln2_gain: bfloat16 [1024], P(('dp', 'fsdp')), may hold values from 0.25 to 1.75
- ln2_shift: bfloat16 [1024], P(('dp', 'fsdp')), may hold values from -2 to 2
- cross_wq: bfloat16 [1024, 1024], P(('dp', 'fsdp')), may hold values from -0.1875 to 0.1875
- cross_bq: bfloat16 [1024], P(('dp', 'fsdp')), may hold values from -2 to 2
- cross_wk: bfloat16 [1024, 1024], P(('dp', 'fsdp')), may hold values from -0.1875 to 0.1875
- cross_wv: bfloat16 [1024, 1024], P(('dp', 'fsdp')), may hold values from -0.1875 to 0.1875
- cross_bv: bfloat16 [1024], P(('dp', 'fsdp')), may hold values from -2 to 2
- cross_wo: bfloat16 [1024, 1024], P(('dp', 'fsdp')), may hold values from -0.75 to 0.75
- cross_bo: bfloat16 [1024], P(('dp', 'fsdp')), may hold values from -2 to 2
- ln3_gain: bfloat16 [1024], P(('dp', 'fsdp')), may hold values from 0.25 to 1.75
- ln3_shift: bfloat16 [1024], P(('dp', 'fsdp')), may hold values from -2 to 2
- ffn_w1: bfloat16 [1024, 4096], P(('dp', 'fsdp')), may hold values from -0.1875 to 0.1875
- ffn_b1: bfloat16 [4096], P(('dp', 'fsdp')), may hold values from -2 to 2
- ffn_w2: bfloat16 [4096, 1024], P(('dp', 'fsdp')), may hold values from -0.09375 to 0.09375
- ffn_b2: bfloat16 [1024], P(('dp', 'fsdp')), may hold values from -2 to 2
Outputs:
- mixed: bfloat16 [32, 1024, 1024], P(('dp', 'fsdp'))
- grad_units: float32 [32, 1024, 1024], P(('dp', 'fsdp'))
- grad_dec_states: float32 [32, 256, 1024], P(('dp', 'fsdp'))
- grad_enc_states: float32 [32, 256, 1024], P(('dp', 'fsdp'))
- grad_ln1_gain: float32 [1024], P(('dp', 'fsdp'))
- grad_ln1_shift: float32 [1024], P(('dp', 'fsdp'))
- grad_self_wq: float32 [1024, 1024], P(('dp', 'fsdp'))
- grad_self_bq: float32 [1024], P(('dp', 'fsdp'))
- grad_self_wk: float32 [1024, 1024], P(('dp', 'fsdp'))
- grad_self_wv: float32 [1024, 1024], P(('dp', 'fsdp'))
- grad_self_bv: float32 [1024], P(('dp', 'fsdp'))
- grad_self_wo: float32 [1024, 1024], P(('dp', 'fsdp'))
- grad_self_bo: float32 [1024], P(('dp', 'fsdp'))
- grad_ln2_gain: float32 [1024], P(('dp', 'fsdp'))
- grad_ln2_shift: float32 [1024], P(('dp', 'fsdp'))
- grad_cross_wq: float32 [1024, 1024], P(('dp', 'fsdp'))
- grad_cross_bq: float32 [1024], P(('dp', 'fsdp'))
- grad_cross_wk: float32 [1024, 1024], P(('dp', 'fsdp'))
- grad_cross_wv: float32 [1024, 1024], P(('dp', 'fsdp'))
- grad_cross_bv: float32 [1024], P(('dp', 'fsdp'))
- grad_cross_wo: float32 [1024, 1024], P(('dp', 'fsdp'))
- grad_cross_bo: float32 [1024], P(('dp', 'fsdp'))
- grad_ln3_gain: float32 [1024], P(('dp', 'fsdp'))
- grad_ln3_shift: float32 [1024], P(('dp', 'fsdp'))
- grad_ffn_w1: float32 [1024, 4096], P(('dp', 'fsdp'))
- grad_ffn_b1: float32 [4096], P(('dp', 'fsdp'))
- grad_ffn_w2: float32 [4096, 1024], P(('dp', 'fsdp'))
- grad_ffn_b2: float32 [1024], P(('dp', 'fsdp'))
Inputs may be any that keep to these rules, and one draw needn't show every extreme that they name: `unit_len`: at least half of 1024; some item has exactly 1024. `text_len`: at least a quarter of 256; some item has exactly 256.
All inputs are finite; a program needn't handle non-finite values.
Results may differ from a plain program's by a relative error of at most 0.02.
Values may be sent and summed in bfloat16 or wider, within the bound.
A program may use at most 384 MiB of HBM per device.

v0:
```python
from functools import partial

import jax
import jax.numpy as jnp
from jax import lax
from jax.sharding import PartitionSpec as P

HEADS = 16


EPSILON = 1e-05
NEGATIVE = -1e30


def matmul(left_side, right_side):
    return jnp.dot(left_side, right_side, preferred_element_type=jnp.float32)


def inner_rows(left_side, right_side):
    return lax.dot_general(
        left_side, right_side, (((0,), (0,)), ((), ())), preferred_element_type=jnp.float32
    )


def inner_cols(left_side, right_side):
    return lax.dot_general(
        left_side, right_side, (((1,), (1,)), ((), ())), preferred_element_type=jnp.float32
    )


def layer_norm(tensor, norm_gain, norm_shift):
    centre = tensor - jnp.mean(tensor, axis=-1, keepdims=True)
    spread = jnp.mean(centre * centre, axis=-1, keepdims=True)
    return centre * lax.rsqrt(spread + EPSILON) * norm_gain + norm_shift


def split_heads(tensor):
    return tensor.reshape(tensor.shape[0], HEADS, -1)


def merge_heads(tensor):
    return tensor.reshape(tensor.shape[0], -1)


def causal_allowed(seq_rows, first_row, count_rows):
    positions = first_row + jnp.arange(count_rows, dtype=jnp.int32)
    return jnp.arange(seq_rows, dtype=jnp.int32)[None, :] <= positions[:, None]


def text_allowed(text_cols, first_row, count_rows):
    return jnp.broadcast_to(text_cols[None, :], (count_rows, text_cols.shape[0]))


def block_scores(query_part, key_rows, allowed_fn, first_row):
    scaling = query_part.shape[-1] ** (-0.5)
    scores = (
        jnp.einsum("qhe,khe->hqk", query_part, key_rows, preferred_element_type=jnp.float32)
        * scaling
    )
    return jnp.where(allowed_fn(first_row, query_part.shape[0])[None], scores, NEGATIVE)


def attend_forward(queries, key_rows, value_rows, allowed_fn, block_rows):
    contexts = []
    log_totals = []
    for first_row in range(0, queries.shape[0], block_rows):
        query_part = queries[first_row : first_row + block_rows]
        scores = block_scores(query_part, key_rows, allowed_fn, first_row)
        highest = jnp.max(scores, axis=-1, keepdims=True)
        exponents = jnp.exp(scores - highest)
        totals = jnp.sum(exponents, axis=-1, keepdims=True)
        weights = (exponents / totals).astype(jnp.bfloat16)
        contexts.append(
            jnp.einsum(
                "hqk,khe->qhe", weights, value_rows, preferred_element_type=jnp.float32
            ).astype(jnp.bfloat16)
        )
        log_totals.append(highest[..., 0] + jnp.log(totals[..., 0]))
    return (jnp.concatenate(contexts, 0), jnp.concatenate(log_totals, 1))


def attend_backward(
    queries, key_rows, value_rows, allowed_fn, block_rows, log_totals, grad_context
):
    scaling = queries.shape[-1] ** (-0.5)
    grad_queries = []
    grad_keys = jnp.zeros(key_rows.shape, jnp.float32)
    grad_values = jnp.zeros(value_rows.shape, jnp.float32)
    for first_row in range(0, queries.shape[0], block_rows):
        query_part = queries[first_row : first_row + block_rows]
        grad_part = grad_context[first_row : first_row + block_rows]
        scores = block_scores(query_part, key_rows, allowed_fn, first_row)
        probs = jnp.exp(scores - log_totals[:, first_row : first_row + block_rows, None])
        grad_probs = jnp.einsum(
            "qhe,khe->hqk", grad_part, value_rows, preferred_element_type=jnp.float32
        )
        centre = jnp.sum(grad_probs * probs, axis=-1, keepdims=True)
        grad_scores = (probs * (grad_probs - centre)).astype(jnp.bfloat16)
        grad_queries.append(
            jnp.einsum("hqk,khe->qhe", grad_scores, key_rows, preferred_element_type=jnp.float32)
            * scaling
        )
        grad_keys = (
            grad_keys
            + jnp.einsum(
                "hqk,qhe->khe", grad_scores, query_part, preferred_element_type=jnp.float32
            )
            * scaling
        )
        grad_values = grad_values + jnp.einsum(
            "hqk,qhe->khe",
            probs.astype(jnp.bfloat16),
            grad_part,
            preferred_element_type=jnp.float32,
        )
    return (jnp.concatenate(grad_queries, 0), grad_keys, grad_values)


def attention_forward(residual, sources, params, allowed_fn, block_rows):
    (
        norm_gain,
        norm_shift,
        query_weight,
        query_bias,
        key_weight,
        value_weight,
        value_bias,
        out_weight,
        out_bias,
    ) = params
    normed = layer_norm(
        residual, norm_gain.astype(jnp.float32), norm_shift.astype(jnp.float32)
    ).astype(jnp.bfloat16)
    if sources is None:
        sources = normed
    queries = (matmul(normed, query_weight) + query_bias).astype(jnp.bfloat16)
    key_rows = matmul(sources, key_weight).astype(jnp.bfloat16)
    value_rows = (matmul(sources, value_weight) + value_bias).astype(jnp.bfloat16)
    contexts, log_totals = attend_forward(
        split_heads(queries), split_heads(key_rows), split_heads(value_rows), allowed_fn, block_rows
    )
    contexts = merge_heads(contexts)
    output = residual + (matmul(contexts, out_weight) + out_bias)
    return (output, (normed, sources, queries, key_rows, value_rows, contexts, log_totals))


def attention_backward(residual, saved, params, allowed_fn, block_rows, grad_output, is_self):
    (
        norm_gain,
        norm_shift,
        query_weight,
        query_bias,
        key_weight,
        value_weight,
        value_bias,
        out_weight,
        out_bias,
    ) = params
    normed, sources, queries, key_rows, value_rows, contexts, log_totals = saved
    grad_branch = grad_output.astype(jnp.bfloat16)
    grad_out_weight = inner_rows(contexts, grad_branch)
    grad_out_bias = jnp.sum(grad_branch.astype(jnp.float32), axis=0)
    grad_context = inner_cols(grad_branch, out_weight).astype(jnp.bfloat16)
    grad_q, grad_k, grad_v = attend_backward(
        split_heads(queries),
        split_heads(key_rows),
        split_heads(value_rows),
        allowed_fn,
        block_rows,
        log_totals,
        split_heads(grad_context),
    )
    grad_q = merge_heads(grad_q).astype(jnp.bfloat16)
    grad_k = merge_heads(grad_k).astype(jnp.bfloat16)
    grad_v = merge_heads(grad_v).astype(jnp.bfloat16)
    grad_query_weight = inner_rows(normed, grad_q)
    grad_query_bias = jnp.sum(grad_q.astype(jnp.float32), axis=0)
    grad_key_weight = inner_rows(sources, grad_k)
    grad_value_weight = inner_rows(sources, grad_v)
    grad_value_bias = jnp.sum(grad_v.astype(jnp.float32), axis=0)
    grad_normed = inner_cols(grad_q, query_weight)
    grad_sources = inner_cols(grad_k, key_weight) + inner_cols(grad_v, value_weight)
    if is_self:
        grad_normed = grad_normed + grad_sources
    _, norm_pull = jax.vjp(
        layer_norm, residual, norm_gain.astype(jnp.float32), norm_shift.astype(jnp.float32)
    )
    grad_residual, grad_gain, grad_shift = norm_pull(grad_normed)
    grads = (
        grad_gain,
        grad_shift,
        grad_query_weight,
        grad_query_bias,
        grad_key_weight,
        grad_value_weight,
        grad_value_bias,
        grad_out_weight,
        grad_out_bias,
    )
    return (grad_output + grad_residual, grad_sources, grads)


def feed_forward(residual, params, valid_rows):
    norm_gain, norm_shift, first_weight, first_bias, second_weight, second_bias = params
    normed = layer_norm(
        residual, norm_gain.astype(jnp.float32), norm_shift.astype(jnp.float32)
    ).astype(jnp.bfloat16)
    before = matmul(normed, first_weight) + first_bias
    hidden = jax.nn.gelu(before, approximate=True).astype(jnp.bfloat16)
    output = (residual + (matmul(hidden, second_weight) + second_bias)) * valid_rows
    return (output, (normed, before, hidden))


def feed_backward(residual, saved, params, grad_output):
    norm_gain, norm_shift, first_weight, first_bias, second_weight, second_bias = params
    normed, before, hidden = saved
    grad_branch = grad_output.astype(jnp.bfloat16)
    grad_second = inner_rows(hidden, grad_branch)
    grad_second_bias = jnp.sum(grad_branch.astype(jnp.float32), axis=0)
    grad_hidden = inner_cols(grad_branch, second_weight).astype(jnp.bfloat16)
    _, gelu_pull = jax.vjp(partial(jax.nn.gelu, approximate=True), before)
    grad_before = gelu_pull(grad_hidden.astype(jnp.float32))[0].astype(jnp.bfloat16)
    grad_first = inner_rows(normed, grad_before)
    grad_first_bias = jnp.sum(grad_before.astype(jnp.float32), axis=0)
    grad_normed = inner_cols(grad_before, first_weight)
    _, norm_pull = jax.vjp(
        layer_norm, residual, norm_gain.astype(jnp.float32), norm_shift.astype(jnp.float32)
    )
    grad_residual, grad_gain, grad_shift = norm_pull(grad_normed)
    grads = (grad_gain, grad_shift, grad_first, grad_first_bias, grad_second, grad_second_bias)
    return (grad_output + grad_residual, grads)


def shards(
    unit_states,
    dec_states,
    enc_states,
    unit_len,
    text_len,
    task_flag,
    cotangent,
    ln1_gain,
    ln1_shift,
    self_wq,
    self_bq,
    self_wk,
    self_wv,
    self_bv,
    self_wo,
    self_bo,
    ln2_gain,
    ln2_shift,
    cross_wq,
    cross_bq,
    cross_wk,
    cross_wv,
    cross_bv,
    cross_wo,
    cross_bo,
    ln3_gain,
    ln3_shift,
    ffn_w1,
    ffn_b1,
    ffn_w2,
    ffn_b2,
):
    seq_rows = unit_states.shape[1]
    block_rows = min(512, seq_rows)
    causal = partial(causal_allowed, seq_rows)
    row_numbers = jnp.arange(seq_rows, dtype=jnp.int32)
    attention_whole = (
        lax.all_gather(ln1_gain, ("dp", "fsdp"), axis=0, tiled=True),
        lax.all_gather(ln1_shift, ("dp", "fsdp"), axis=0, tiled=True),
        lax.all_gather(self_wq, ("dp", "fsdp"), axis=0, tiled=True),
        lax.all_gather(self_bq, ("dp", "fsdp"), axis=0, tiled=True),
        lax.all_gather(self_wk, ("dp", "fsdp"), axis=0, tiled=True),
        lax.all_gather(self_wv, ("dp", "fsdp"), axis=0, tiled=True),
        lax.all_gather(self_bv, ("dp", "fsdp"), axis=0, tiled=True),
        lax.all_gather(self_wo, ("dp", "fsdp"), axis=0, tiled=True),
        lax.all_gather(self_bo, ("dp", "fsdp"), axis=0, tiled=True),
        lax.all_gather(ln2_gain, ("dp", "fsdp"), axis=0, tiled=True),
        lax.all_gather(ln2_shift, ("dp", "fsdp"), axis=0, tiled=True),
        lax.all_gather(cross_wq, ("dp", "fsdp"), axis=0, tiled=True),
        lax.all_gather(cross_bq, ("dp", "fsdp"), axis=0, tiled=True),
        lax.all_gather(cross_wk, ("dp", "fsdp"), axis=0, tiled=True),
        lax.all_gather(cross_wv, ("dp", "fsdp"), axis=0, tiled=True),
        lax.all_gather(cross_bv, ("dp", "fsdp"), axis=0, tiled=True),
        lax.all_gather(cross_wo, ("dp", "fsdp"), axis=0, tiled=True),
        lax.all_gather(cross_bo, ("dp", "fsdp"), axis=0, tiled=True),
    )
    item_index = 0
    residual = unit_states[item_index].astype(jnp.float32)
    memory = jnp.where(task_flag[item_index] == 1, dec_states[item_index], enc_states[item_index])
    text_mask = partial(
        text_allowed, jnp.arange(memory.shape[0], dtype=jnp.int32) < text_len[item_index]
    )
    after_self, self_saved = attention_forward(
        residual, None, attention_whole[:9], causal, block_rows
    )
    after_cross, cross_saved = attention_forward(
        after_self, memory, attention_whole[9:], text_mask, block_rows
    )
    saved_items = [(residual, after_self, after_cross, text_mask, self_saved, cross_saved)]
    ffn_whole = (
        lax.all_gather(ln3_gain, ("dp", "fsdp"), axis=0, tiled=True),
        lax.all_gather(ln3_shift, ("dp", "fsdp"), axis=0, tiled=True),
        lax.all_gather(ffn_w1, ("dp", "fsdp"), axis=0, tiled=True),
        lax.all_gather(ffn_b1, ("dp", "fsdp"), axis=0, tiled=True),
        lax.all_gather(ffn_w2, ("dp", "fsdp"), axis=0, tiled=True),
        lax.all_gather(ffn_b2, ("dp", "fsdp"), axis=0, tiled=True),
    )
    item_index = 0
    valid_rows = (row_numbers < unit_len[item_index]).astype(jnp.float32)[:, None]
    output, feed_saved = feed_forward(saved_items[item_index][2], ffn_whole, valid_rows)
    outputs = [output.astype(jnp.bfloat16)]
    ffn_saved = [(feed_saved, valid_rows)]
    ffn_back = (
        lax.all_gather(ln3_gain, ("dp", "fsdp"), axis=0, tiled=True),
        lax.all_gather(ln3_shift, ("dp", "fsdp"), axis=0, tiled=True),
        lax.all_gather(ffn_w1, ("dp", "fsdp"), axis=0, tiled=True),
        lax.all_gather(ffn_b1, ("dp", "fsdp"), axis=0, tiled=True),
        lax.all_gather(ffn_w2, ("dp", "fsdp"), axis=0, tiled=True),
        lax.all_gather(ffn_b2, ("dp", "fsdp"), axis=0, tiled=True),
    )
    item_index = 0
    feed_saved, valid_rows = ffn_saved[item_index]
    grad_top = cotangent[item_index].astype(jnp.float32) * valid_rows
    grad_after_cross, fresh = feed_backward(
        saved_items[item_index][2], feed_saved, ffn_back, grad_top
    )
    grad_cross_rows = [grad_after_cross]
    ffn_totals = (
        lax.psum_scatter(fresh[0], ("dp", "fsdp"), scatter_dimension=0, tiled=True),
        lax.psum_scatter(fresh[1], ("dp", "fsdp"), scatter_dimension=0, tiled=True),
        lax.psum_scatter(fresh[2], ("dp", "fsdp"), scatter_dimension=0, tiled=True),
        lax.psum_scatter(fresh[3], ("dp", "fsdp"), scatter_dimension=0, tiled=True),
        lax.psum_scatter(fresh[4], ("dp", "fsdp"), scatter_dimension=0, tiled=True),
        lax.psum_scatter(fresh[5], ("dp", "fsdp"), scatter_dimension=0, tiled=True),
    )
    attention_back = (
        lax.all_gather(ln1_gain, ("dp", "fsdp"), axis=0, tiled=True),
        lax.all_gather(ln1_shift, ("dp", "fsdp"), axis=0, tiled=True),
        lax.all_gather(self_wq, ("dp", "fsdp"), axis=0, tiled=True),
        lax.all_gather(self_bq, ("dp", "fsdp"), axis=0, tiled=True),
        lax.all_gather(self_wk, ("dp", "fsdp"), axis=0, tiled=True),
        lax.all_gather(self_wv, ("dp", "fsdp"), axis=0, tiled=True),
        lax.all_gather(self_bv, ("dp", "fsdp"), axis=0, tiled=True),
        lax.all_gather(self_wo, ("dp", "fsdp"), axis=0, tiled=True),
        lax.all_gather(self_bo, ("dp", "fsdp"), axis=0, tiled=True),
        lax.all_gather(ln2_gain, ("dp", "fsdp"), axis=0, tiled=True),
        lax.all_gather(ln2_shift, ("dp", "fsdp"), axis=0, tiled=True),
        lax.all_gather(cross_wq, ("dp", "fsdp"), axis=0, tiled=True),
        lax.all_gather(cross_bq, ("dp", "fsdp"), axis=0, tiled=True),
        lax.all_gather(cross_wk, ("dp", "fsdp"), axis=0, tiled=True),
        lax.all_gather(cross_wv, ("dp", "fsdp"), axis=0, tiled=True),
        lax.all_gather(cross_bv, ("dp", "fsdp"), axis=0, tiled=True),
        lax.all_gather(cross_wo, ("dp", "fsdp"), axis=0, tiled=True),
        lax.all_gather(cross_bo, ("dp", "fsdp"), axis=0, tiled=True),
    )
    attention_grads = None
    item_index = 0
    residual, after_self, after_cross, text_mask, self_saved, cross_saved = saved_items[item_index]
    grad_after_self, grad_memory, cross_fresh = attention_backward(
        after_self,
        cross_saved,
        attention_back[9:],
        text_mask,
        block_rows,
        grad_cross_rows[item_index],
        False,
    )
    grad_residual, _, self_fresh = attention_backward(
        residual, self_saved, attention_back[:9], causal, block_rows, grad_after_self, True
    )
    attention_grads = self_fresh + cross_fresh
    grad_unit_rows = [grad_residual]
    flag_weight = (task_flag[item_index] == 1).astype(jnp.float32)
    grad_dec_rows = [grad_memory * flag_weight]
    grad_enc_rows = [grad_memory * (1.0 - flag_weight)]
    attention_totals = (
        lax.psum_scatter(attention_grads[0], ("dp", "fsdp"), scatter_dimension=0, tiled=True),
        lax.psum_scatter(attention_grads[1], ("dp", "fsdp"), scatter_dimension=0, tiled=True),
        lax.psum_scatter(attention_grads[2], ("dp", "fsdp"), scatter_dimension=0, tiled=True),
        lax.psum_scatter(attention_grads[3], ("dp", "fsdp"), scatter_dimension=0, tiled=True),
        lax.psum_scatter(attention_grads[4], ("dp", "fsdp"), scatter_dimension=0, tiled=True),
        lax.psum_scatter(attention_grads[5], ("dp", "fsdp"), scatter_dimension=0, tiled=True),
        lax.psum_scatter(attention_grads[6], ("dp", "fsdp"), scatter_dimension=0, tiled=True),
        lax.psum_scatter(attention_grads[7], ("dp", "fsdp"), scatter_dimension=0, tiled=True),
        lax.psum_scatter(attention_grads[8], ("dp", "fsdp"), scatter_dimension=0, tiled=True),
        lax.psum_scatter(attention_grads[9], ("dp", "fsdp"), scatter_dimension=0, tiled=True),
        lax.psum_scatter(attention_grads[10], ("dp", "fsdp"), scatter_dimension=0, tiled=True),
        lax.psum_scatter(attention_grads[11], ("dp", "fsdp"), scatter_dimension=0, tiled=True),
        lax.psum_scatter(attention_grads[12], ("dp", "fsdp"), scatter_dimension=0, tiled=True),
        lax.psum_scatter(attention_grads[13], ("dp", "fsdp"), scatter_dimension=0, tiled=True),
        lax.psum_scatter(attention_grads[14], ("dp", "fsdp"), scatter_dimension=0, tiled=True),
        lax.psum_scatter(attention_grads[15], ("dp", "fsdp"), scatter_dimension=0, tiled=True),
        lax.psum_scatter(attention_grads[16], ("dp", "fsdp"), scatter_dimension=0, tiled=True),
        lax.psum_scatter(attention_grads[17], ("dp", "fsdp"), scatter_dimension=0, tiled=True),
    )
    all_totals = tuple(attention_totals) + tuple(ffn_totals)
    heads_out = (
        jnp.stack(outputs),
        jnp.stack(grad_unit_rows),
        jnp.stack(grad_dec_rows),
        jnp.stack(grad_enc_rows),
    )
    return heads_out + all_totals


def solution(mesh):
    placed = (
        P(("dp", "fsdp"), None, None),
        P(("dp", "fsdp"), None, None),
        P(("dp", "fsdp"), None, None),
        P(("dp", "fsdp")),
        P(("dp", "fsdp")),
        P(("dp", "fsdp")),
        P(("dp", "fsdp"), None, None),
        P(("dp", "fsdp")),
        P(("dp", "fsdp")),
        P(("dp", "fsdp"), None),
        P(("dp", "fsdp")),
        P(("dp", "fsdp"), None),
        P(("dp", "fsdp"), None),
        P(("dp", "fsdp")),
        P(("dp", "fsdp"), None),
        P(("dp", "fsdp")),
        P(("dp", "fsdp")),
        P(("dp", "fsdp")),
        P(("dp", "fsdp"), None),
        P(("dp", "fsdp")),
        P(("dp", "fsdp"), None),
        P(("dp", "fsdp"), None),
        P(("dp", "fsdp")),
        P(("dp", "fsdp"), None),
        P(("dp", "fsdp")),
        P(("dp", "fsdp")),
        P(("dp", "fsdp")),
        P(("dp", "fsdp"), None),
        P(("dp", "fsdp")),
        P(("dp", "fsdp"), None),
        P(("dp", "fsdp")),
    )
    return jax.shard_map(
        shards,
        mesh=mesh,
        in_specs=placed,
        out_specs=(
            P(("dp", "fsdp"), None, None),
            P(("dp", "fsdp"), None, None),
            P(("dp", "fsdp"), None, None),
            P(("dp", "fsdp"), None, None),
            P(("dp", "fsdp")),
            P(("dp", "fsdp")),
            P(("dp", "fsdp"), None),
            P(("dp", "fsdp")),
            P(("dp", "fsdp"), None),
            P(("dp", "fsdp"), None),
            P(("dp", "fsdp")),
            P(("dp", "fsdp"), None),
            P(("dp", "fsdp")),
            P(("dp", "fsdp")),
            P(("dp", "fsdp")),
            P(("dp", "fsdp"), None),
            P(("dp", "fsdp")),
            P(("dp", "fsdp"), None),
            P(("dp", "fsdp"), None),
            P(("dp", "fsdp")),
            P(("dp", "fsdp"), None),
            P(("dp", "fsdp")),
            P(("dp", "fsdp")),
            P(("dp", "fsdp")),
            P(("dp", "fsdp"), None),
            P(("dp", "fsdp")),
            P(("dp", "fsdp"), None),
            P(("dp", "fsdp")),
        ),
        check_vma=False,
    )
```

profile of v0, /device:TPU:0, one launch (start us, length us, event | category | flops | bytes accessed | tf_op | source)
XLA Modules:
  0.0 2606.6 jit_solution(10173327577952202450)
XLA Ops:
  28.3 42.7 %all-reduce.28 = (bf16[1024]{0:T(1024)(128)(2,1)S(1)}, bf16[1024]{0:T(1024)(128)(2,1)S(1)}, bf16[1024]{0:T(1024)(128)(2,1)S(1)}, bf16[1024]{0:T(1024)(128)(2,1)S...) all-reduce(bf16[1024]{0:T(1024)(128)(2,1)S(1)} %dynamic-update-slic, ...), channel_id=1, replica_groups=mesh['dp'=4,'fsdp'=8] {'dp','fsdp'}, use_global_device_ids=true, to_apply=%add.4 | all-reduce | flops 13312 | bytes 53248
  75.8 39.9 %all-gather = bf16[32,1,128]{2,1,0:T(2,128)(2,1)S(1)} all-gather(bf16[1,1,128]{2,1,0:T(2,128)(2,1)} %bitcast.264), channel_id=1, replica_groups=mesh['dp'=4,'fsdp'=8] {'dp','fsdp'}, dimensions={0}, use_global_device_ids=true | all-gather | bytes 8448 | tf_op jit(solution)/shard_map/all_gather | solution.py:308
  249.8 53.9 %all-gather.24.cloned.1.call-done = bf16[1024,1024]{1,0:T(8,128)(2,1)} async-done(((bf16[32,1024]{1,0:T(8,128)(2,1)}), bf16[1024,1024]{1,0:T(8,128)(2,1)}) %all-gather.24.cloned.1.call-update) | async-done | bytes 2097168 | tf_op jit(solution)/shard_map/all_gather | solution.py:285
  322.8 39.0 %all-gather.18.cloned.1.call-done = bf16[1024,1024]{1,0:T(8,128)(2,1)} async-done(((bf16[32,1024]{1,0:T(8,128)(2,1)}), bf16[1024,1024]{1,0:T(8,128)(2,1)}) %all-gather.18.cloned.1.call-update) | async-done | bytes 2097168 | tf_op jit(solution)/shard_map/all_gather | solution.py:279
  369.4 50.8 %all-gather.22.cloned.1.call-done = bf16[1024,1024]{1,0:T(8,128)(2,1)} async-done(((bf16[32,1024]{1,0:T(8,128)(2,1)}), bf16[1024,1024]{1,0:T(8,128)(2,1)}) %all-gather.22.cloned.1.call-update) | async-done | bytes 2097168 | tf_op jit(solution)/shard_map/all_gather | solution.py:283
  437.0 41.5 %all-gather.26.cloned.1.call-done = bf16[1024,1024]{1,0:T(8,128)(2,1)} async-done(((bf16[32,1024]{1,0:T(8,128)(2,1)}), bf16[1024,1024]{1,0:T(8,128)(2,1)}) %all-gather.26.cloned.1.call-update) | async-done | bytes 2097168 | tf_op jit(solution)/shard_map/all_gather | solution.py:288
  487.2 70.6 %all-gather.28.cloned.1.call-done = bf16[1024,4096]{1,0:T(8,128)(2,1)} async-done(((bf16[32,4096]{1,0:T(8,128)(2,1)}), bf16[1024,4096]{1,0:T(8,128)(2,1)}) %all-gather.28.cloned.1.call-update) | async-done | bytes 8388624 | tf_op jit(solution)/shard_map/all_gather | solution.py:307
  574.7 61.9 %all-gather.30.cloned.1.call-done = bf16[4096,1024]{1,0:T(8,128)(2,1)} async-done(((bf16[128,1024]{1,0:T(8,128)(2,1)}), bf16[4096,1024]{1,0:T(8,128)(2,1)}) %all-gather.30.cloned.1.call-update) | async-done | bytes 8388624 | tf_op jit(solution)/shard_map/all_gather | solution.py:309
  636.6 25.2 convert_reduce_fusion
  748.6 22.4 multiply_reduce_fusion.1
  771.0 28.0 %multiply_convert_fusion.1 = bf16[16,512,1024]{2,1,0:T(8,128)(2,1)} fusion(f32[16,512,1024]{2,1,0:T(8,128)} %get-tuple-element.187, f32[16,512,1024]{2,1,0:T(8,128)} %get-tuple-element.171, f32[16,512]{1,0:T(8,128)S(1)} %get-tuple-element.186, f32[16,512]{1,0:T(8,128)S(1)} %log_add_fusion.1), kind=kLoop, calls=%fused_computation.3 | loop fusion | flops 33554432 | bytes 83951616 | tf_op jit(solution)/shard_map/convert_element_type | solution.py:98
  837.9 24.7 multiply_reduce_fusion
  883.0 28.2 %multiply_convert_fusion = bf16[16,512,1024]{2,1,0:T(8,128)(2,1)} fusion(f32[16,512,1024]{2,1,0:T(8,128)} %get-tuple-element.185, f32[16,512,1024]{2,1,0:T(8,128)} %get-tuple-element.169, f32[16,512]{1,0:T(8,128)S(1)} %get-tuple-element.184, f32[16,512]{1,0:T(8,128)S(1)} %copy-done.53), kind=kLoop, calls=%fused_computation | loop fusion | flops 33554432 | bytes 83951616 | tf_op jit(solution)/shard_map/convert_element_type | solution.py:98
  1006.5 21.1 fusion.62
  1101.3 127.8 %reduce-scatter.25.cloned.1.call-done = f32[32,1024]{1,0:T(8,128)} async-done(((f32[1024,1024]{1,0:T(8,128)}), f32[32,1024]{1,0:T(8,128)}) %reduce-scatter.25.cloned.1.call-update) | async-done | bytes 131088 | tf_op jit(solution)/shard_map/reduce_scatter | solution.py:397
  1229.1 142.5 %reduce-scatter.23.cloned.1.call-done = f32[32,1024]{1,0:T(8,128)} async-done(((f32[1024,1024]{1,0:T(8,128)}), f32[32,1024]{1,0:T(8,128)}) %reduce-scatter.23.cloned.1.call-update) | async-done | bytes 131088 | tf_op jit(solution)/shard_map/reduce_scatter | solution.py:395
  1371.5 141.8 %reduce-scatter.19.cloned.1.call-done = f32[32,1024]{1,0:T(8,128)} async-done(((f32[1024,1024]{1,0:T(8,128)}), f32[32,1024]{1,0:T(8,128)}) %reduce-scatter.19.cloned.1.call-update) | async-done | bytes 131088 | tf_op jit(solution)/shard_map/reduce_scatter | solution.py:392
  1513.3 142.8 %reduce-scatter.21.cloned.1.call-done = f32[32,1024]{1,0:T(8,128)} async-done(((f32[1024,1024]{1,0:T(8,128)}), f32[32,1024]{1,0:T(8,128)}) %reduce-scatter.21.cloned.1.call-update) | async-done | bytes 131088 | tf_op jit(solution)/shard_map/reduce_scatter | solution.py:394
  1656.1 142.4 %reduce-scatter.17.cloned.1.call-done = f32[32,1024]{1,0:T(8,128)} async-done(((f32[1024,1024]{1,0:T(8,128)}), f32[32,1024]{1,0:T(8,128)}) %reduce-scatter.17.cloned.1.call-update) | async-done | bytes 131088 | tf_op jit(solution)/shard_map/reduce_scatter | solution.py:388
  1798.5 142.3 %reduce-scatter.15.cloned.1.call-done = f32[32,1024]{1,0:T(8,128)} async-done(((f32[1024,1024]{1,0:T(8,128)}), f32[32,1024]{1,0:T(8,128)}) %reduce-scatter.15.cloned.1.call-update) | async-done | bytes 131088 | tf_op jit(solution)/shard_map/reduce_scatter | solution.py:386
  1940.8 142.4 %reduce-scatter.13.cloned.1.call-done = f32[32,1024]{1,0:T(8,128)} async-done(((f32[1024,1024]{1,0:T(8,128)}), f32[32,1024]{1,0:T(8,128)}) %reduce-scatter.13.cloned.1.call-update) | async-done | bytes 131088 | tf_op jit(solution)/shard_map/reduce_scatter | solution.py:385
  2083.2 142.3 %reduce-scatter.11.cloned.1.call-done = f32[32,1024]{1,0:T(8,128)} async-done(((f32[1024,1024]{1,0:T(8,128)}), f32[32,1024]{1,0:T(8,128)}) %reduce-scatter.11.cloned.1.call-update) | async-done | bytes 131088 | tf_op jit(solution)/shard_map/reduce_scatter | solution.py:383
  2225.5 186.5 %reduce-scatter.29.cloned.1.call-done = f32[128,1024]{1,0:T(8,128)} async-done(((f32[4096,1024]{1,0:T(8,128)}), f32[128,1024]{1,0:T(8,128)}) %reduce-scatter.29.cloned.1.call-update) | async-done | bytes 524304 | tf_op jit(solution)/shard_map/reduce_scatter | solution.py:337
  2412.0 187.3 %reduce-scatter.27.cloned.1.call-done = f32[32,4096]{1,0:T(8,128)} async-done(((f32[1024,4096]{1,0:T(8,128)}), f32[32,4096]{1,0:T(8,128)}) %reduce-scatter.27.cloned.1.call-update) | async-done | bytes 524304 | tf_op jit(solution)/shard_map/reduce_scatter | solution.py:335
  (440 shorter events, 540.5 us)
Async XLA Ops:
  7.2 119.8 %all-gather.14.cloned.1.call-start = ((), (), s32[]{:S(2)}) async-start(), calls=%async_computation.11 | async-start | bytes 2162688 | tf_op jit(solution)/shard_map/all_gather | solution.py:274
  7.9 124.5 %all-gather.16.cloned.1.call-start = ((), (), s32[]{:S(2)}) async-start(), calls=%async_computation.12 | async-start | bytes 2162688 | tf_op jit(solution)/shard_map/all_gather | solution.py:276
  8.7 178.5 %all-gather.12.cloned.1.call-start = ((), (), s32[]{:S(2)}) async-start(), calls=%async_computation.10 | async-start | bytes 2162688 | tf_op jit(solution)/shard_map/all_gather | solution.py:277
  9.4 236.0 %all-gather.20.cloned.1.call-start = ((), (), s32[]{:S(2)}) async-start(), calls=%async_computation.14 | async-start | bytes 2162688 | tf_op jit(solution)/shard_map/all_gather | solution.py:286
  10.0 293.7 %all-gather.24.cloned.1.call-start = ((), (), s32[]{:S(2)}) async-start(), calls=%async_computation.16 | async-start | bytes 2162688 | tf_op jit(solution)/shard_map/all_gather | solution.py:285
  10.6 351.3 %all-gather.18.cloned.1.call-start = ((), (), s32[]{:S(2)}) async-start(), calls=%async_computation.13 | async-start | bytes 2162688 | tf_op jit(solution)/shard_map/all_gather | solution.py:279
  11.2 409.1 %all-gather.22.cloned.1.call-start = ((), (), s32[]{:S(2)}) async-start(), calls=%async_computation.15 | async-start | bytes 2162688 | tf_op jit(solution)/shard_map/all_gather | solution.py:283
  11.9 466.7 %all-gather.26.cloned.1.call-start = ((), (), s32[]{:S(2)}) async-start(), calls=%async_computation.17 | async-start | bytes 2162688 | tf_op jit(solution)/shard_map/all_gather | solution.py:288
  12.7 545.2 %all-gather.28.cloned.1.call-start = ((), (), s32[]{:S(2)}) async-start(), calls=%async_computation.18 | async-start | bytes 8650752 | tf_op jit(solution)/shard_map/all_gather | solution.py:307
  13.4 623.2 %all-gather.30.cloned.1.call-start = ((), (), s32[]{:S(2)}) async-start(), calls=%async_computation.19 | async-start | bytes 8650752 | tf_op jit(solution)/shard_map/all_gather | solution.py:309
  14.0 1069.7 %all-reduce.31.cloned.1.call-start = ((), (), s32[]{:S(2)}) async-start(), calls=%async_computation.30 | async-start | bytes 139264
  484.0 204.5 %copy-start.70 = (f32[1024]{0:T(1024)}, f32[1024]{0:T(1024)S(1)}, u32[]{:S(2)}) copy-start(f32[1024]{0:T(1024)S(1)} %broadcast_multiply_fusion) | copy-start | bytes 12292
  486.5 202.0 %copy-start.83 = (f32[1024]{0:T(1024)}, f32[1024]{0:T(1024)S(1)}, u32[]{:S(2)}) copy-start(f32[1024]{0:T(1024)S(1)} %fusion.92) | copy-start | bytes 12292
  487.2 149.4 %copy-start.22 = (bf16[1,1024,1024]{1,2,0:T(8,128)(2,1)S(1)}, bf16[1,1024,1024]{1,2,0:T(8,128)(2,1)}, u32[]{:S(2)}) copy-start(bf16[1,1024,1024]{1,2,0:T(8,128)(2,1)} %copy.115) | copy-start | bytes 6291460
  951.9 277.2 %reduce-scatter.25.cloned.1.call-start = ((), (), s32[]{:S(2)}) async-start(), calls=%async_computation.27 | async-start | bytes 4325376 | tf_op jit(solution)/shard_map/reduce_scatter | solution.py:397
  958.5 413.0 %reduce-scatter.23.cloned.1.call-start = ((), (), s32[]{:S(2)}) async-start(), calls=%async_computation.26 | async-start | bytes 4325376 | tf_op jit(solution)/shard_map/reduce_scatter | solution.py:395
  962.5 550.9 %reduce-scatter.19.cloned.1.call-start = ((), (), s32[]{:S(2)}) async-start(), calls=%async_computation.24 | async-start | bytes 4325376 | tf_op jit(solution)/shard_map/reduce_scatter | solution.py:392
  969.9 686.3 %reduce-scatter.21.cloned.1.call-start = ((), (), s32[]{:S(2)}) async-start(), calls=%async_computation.25 | async-start | bytes 4325376 | tf_op jit(solution)/shard_map/reduce_scatter | solution.py:394
  979.0 819.6 %reduce-scatter.17.cloned.1.call-start = ((), (), s32[]{:S(2)}) async-start(), calls=%async_computation.23 | async-start | bytes 4325376 | tf_op jit(solution)/shard_map/reduce_scatter | solution.py:388
  986.3 954.5 %reduce-scatter.15.cloned.1.call-start = ((), (), s32[]{:S(2)}) async-start(), calls=%async_computation.22 | async-start | bytes 4325376 | tf_op jit(solution)/shard_map/reduce_scatter | solution.py:386
  992.9 1090.3 %reduce-scatter.13.cloned.1.call-start = ((), (), s32[]{:S(2)}) async-start(), calls=%async_computation.21 | async-start | bytes 4325376 | tf_op jit(solution)/shard_map/reduce_scatter | solution.py:385
  999.0 1226.5 %reduce-scatter.11.cloned.1.call-start = ((), (), s32[]{:S(2)}) async-start(), calls=%async_computation.20 | async-start | bytes 4325376 | tf_op jit(solution)/shard_map/reduce_scatter | solution.py:383
  1005.9 1406.1 %reduce-scatter.29.cloned.1.call-start = ((), (), s32[]{:S(2)}) async-start(), calls=%async_computation.29 | async-start | bytes 17301504 | tf_op jit(solution)/shard_map/reduce_scatter | solution.py:337
  1027.7 1571.6 %reduce-scatter.27.cloned.1.call-start = ((), (), s32[]{:S(2)}) async-start(), calls=%async_computation.28 | async-start | bytes 17301504 | tf_op jit(solution)/shard_map/reduce_scatter | solution.py:335
  (110 other events, 2076.0 us)
Sparse Core Ops, SparseCore 0:
  11.0 59.4 all-gather.13
  73.5 55.3 all-gather.15
  131.9 55.3 all-gather.11
  190.1 55.3 all-gather.19
  248.3 55.3 all-gather.23
  306.5 55.3 all-gather.17
  364.9 55.3 all-gather.21
  423.2 55.3 all-gather.25
  481.6 76.2 all-gather.27
  560.7 75.8 all-gather.29
  952.0 129.1 all-reduce.30
  1083.8 145.1 reduce-scatter.24
  1231.9 139.5 reduce-scatter.22
  1374.2 139.0 reduce-scatter.18
  1516.0 140.0 reduce-scatter.20
  1658.8 139.6 reduce-scatter.16
  1801.2 139.5 reduce-scatter.14
  1943.5 139.6 reduce-scatter.12
  2086.1 139.4 reduce-scatter.10
  2228.2 183.6 reduce-scatter.28
  2414.9 184.3 reduce-scatter.26
where the time goes:
time: 2610 us
  waiting for transfers between devices  1850 us (71%)
  matrix products  425 us (16%)
  other arithmetic  139 us (5%)
  local copies, waits for them, and re-layouts  87.3 us (3%)
  blocking collectives  82.6 us (3%)
    reduce_scatter x1, waiting for transfers between devices, shards(): lax.psum_scatter(fresh[2], ('dp', 'fsdp'), scatter_dimension=0, tiled=True)  187 us
    reduce_scatter x1, waiting for transfers between devices, shards(): lax.psum_scatter(fresh[4], ('dp', 'fsdp'), scatter_dimension=0, tiled=True)  186 us
    reduce_scatter x1, waiting for transfers between devices, shards(): lax.psum_scatter(attention_grads[13], ('dp', 'fsdp'), scatter_dimension=0...  143 us
    reduce_scatter x1, waiting for transfers between devices, shards(): lax.psum_scatter(attention_grads[14], ('dp', 'fsdp'), scatter_dimension=0...  142 us
    reduce_scatter x1, waiting for transfers between devices, shards(): lax.psum_scatter(attention_grads[4], ('dp', 'fsdp'), scatter_dimension=0,...  142 us
    reduce_scatter x1, waiting for transfers between devices, shards(): lax.psum_scatter(attention_grads[7], ('dp', 'fsdp'), scatter_dimension=0,...  142 us
    reduce_scatter x1, waiting for transfers between devices, shards(): lax.psum_scatter(attention_grads[2], ('dp', 'fsdp'), scatter_dimension=0,...  142 us
    reduce_scatter x1, waiting for transfers between devices, shards(): lax.psum_scatter(attention_grads[5], ('dp', 'fsdp'), scatter_dimension=0,...  142 us
  transfers between devices with their start and end apart: 21, of which 18 were waited for; matrix products, arithmetic and copies ran while one was open for 13% of the time, Pallas kernels for 0%

commit v1 on v0

v1 whole, which is shorter than its diff:
```python
import functools

import jax
import jax.numpy as jnp
from jax import lax
from jax.experimental import pallas as pl
from jax.experimental.pallas import tpu as pltpu
from jax.sharding import PartitionSpec as P

MIB=1<<20
NEGATIVE=-1e30
NN=(((1,),(0,)),((),()))
NT=(((1,),(1,)),((),()))
TN=(((0,),(0,)),((),()))
def dot(a,b,dims=NN):
    return lax.dot_general(a,b,dims,preferred_element_type=jnp.float32)

def head_masks(width):
    lane=lax.broadcasted_iota(jnp.int32,(1,128),1)
    return [((lane//width)==h) for h in range(128//width)]

def allowed(scores, first_row, first_col, causal, limit):
    cols=first_col+lax.broadcasted_iota(jnp.int32,scores.shape,1)
    if causal:
        rows=first_row+lax.broadcasted_iota(jnp.int32,scores.shape,0)
        keep=cols<=rows
    else:
        keep=cols<limit
    return jnp.where(keep,scores,NEGATIVE)

def fwd_kernel(causal, block, width, lim_ref, q_ref, k_ref, v_ref, ctx_ref, lse_ref):
    rows=q_ref.shape[0]; keys=k_ref.shape[0]
    masks=head_masks(width)
    k=k_ref[...]
    v=v_ref[...]
    vm=[jnp.where(m,v,jnp.zeros_like(v)) for m in masks]
    for i in range(rows//block):
        kend=(i+1)*block if causal else keys
        q=q_ref[pl.ds(i*block,block),:]*jnp.bfloat16(width**-0.5)
        ctx=None
        for h,m in enumerate(masks):
            s=dot(jnp.where(m,q,jnp.zeros_like(q)),k[:kend],NT)
            if causal:
                tail=allowed(s[:,kend-block:],0,0,True,None)
                s=tail if kend==block else jnp.concatenate([s[:,:kend-block],tail],1)
            else:
                s=allowed(s,0,0,False,lim_ref[0])
            top=jnp.max(s,axis=1,keepdims=True)
            p=jnp.exp(s-top)
            total=jnp.sum(p,axis=1,keepdims=True)
            part=dot(p.astype(jnp.bfloat16),vm[h][:kend])*(1.0/total)
            ctx=part if ctx is None else ctx+part
            lse=jnp.broadcast_to(top+jnp.log(total),(block,128))
            lse_ref[0,pl.ds(h,1),pl.ds(i*block,block)]=jnp.transpose(lse)[:1]
        ctx_ref[pl.ds(i*block,block),:]=ctx.astype(jnp.bfloat16)

def flash_fwd(q,k,v,limit,causal,block=256,width=64):
    rows,d=q.shape; keys=k.shape[0]
    pairs=d//128
    per=128//width
    spec=lambda n: pl.BlockSpec((n,128),lambda i,lim:(0,i))
    return pl.pallas_call(
        functools.partial(fwd_kernel,causal,block,width),
        grid_spec=pltpu.PrefetchScalarGridSpec(
            num_scalar_prefetch=1, grid=(pairs,),
            in_specs=[spec(rows),spec(keys),spec(keys)],
            out_specs=[spec(rows),pl.BlockSpec((1,per,rows),lambda i,lim:(i,0,0))]),
        out_shape=[jax.ShapeDtypeStruct((rows,d),jnp.bfloat16),jax.ShapeDtypeStruct((pairs,per,rows),jnp.float32)],
        compiler_params=pltpu.CompilerParams(vmem_limit_bytes=48*MIB),
        cost_estimate=pl.CostEstimate(flops=4*rows*keys*d//(2 if causal else 1),bytes_accessed=4*rows*d*2,transcendentals=rows*keys*16//(2 if causal else 1)),
        name="attend_causal" if causal else "attend_text",
    )(limit,q,k,v)

def bwd_kernel(causal, block, width, lim_ref, q_ref,k_ref,v_ref,g_ref,ctx_ref,lse_ref,dq_ref,dk_ref,dv_ref,dk_acc,dv_acc):
    rows=q_ref.shape[0]; keys=k_ref.shape[0]
    masks=head_masks(width)
    scale=jnp.bfloat16(width**-0.5)
    k=k_ref[...]; v=v_ref[...]
    km=[jnp.where(m,k*scale,jnp.zeros_like(k)) for m in masks]
    ones=[jnp.where(m,1.0,0.0) for m in masks]
    dk_acc[...]=jnp.zeros_like(dk_acc); dv_acc[...]=jnp.zeros_like(dv_acc)
    for i in range(rows//block):
        kend=(i+1)*block if causal else keys
        sl=pl.ds(i*block,block)
        q=q_ref[sl,:]*scale
        g=g_ref[sl,:]
        prod=g.astype(jnp.float32)*ctx_ref[sl,:].astype(jnp.float32)
        dq=None
        for h,m in enumerate(masks):
            qm=jnp.where(m,q,jnp.zeros_like(q))
            gm=jnp.where(m,g,jnp.zeros_like(g))
            delta=jnp.sum(jnp.where(m,prod,0.0),axis=1,keepdims=True)
            delta=jnp.transpose(jnp.broadcast_to(delta,(block,128)))[:1]
            lse=lse_ref[0,pl.ds(h,1),sl]
            s=dot(k[:kend],qm,NT)
            if causal:
                tail=s[kend-block:]
                r=lax.broadcasted_iota(jnp.int32,tail.shape,0)
                c=lax.broadcasted_iota(jnp.int32,tail.shape,1)
                tail=jnp.where(r<=c,tail,NEGATIVE)
                s=tail if kend==block else jnp.concatenate([s[:kend-block],tail],0)
            else:
                r=lax.broadcasted_iota(jnp.int32,s.shape,0)
                s=jnp.where(r<lim_ref[0],s,NEGATIVE)
            p=jnp.exp(s-lse)
            dp=dot(v[:kend],gm,NT)
            ds=(p*(dp-delta)).astype(jnp.bfloat16)
            dk_acc[:kend,:]+=dot(ds,qm)
            dv_acc[:kend,:]+=dot(p.astype(jnp.bfloat16),gm)
            part=dot(ds,km[h][:kend],TN)
            dq=part if dq is None else dq+part
        dq_ref[sl,:]=dq.astype(jnp.bfloat16)
    dk_ref[...]=dk_acc[...].astype(jnp.bfloat16)
    dv_ref[...]=dv_acc[...].astype(jnp.bfloat16)

def flash_bwd(q,k,v,g,ctx,lse,limit,causal,block=256,width=64):
    rows,d=q.shape; keys=k.shape[0]
    pairs=d//128; per=128//width
    spec=lambda n: pl.BlockSpec((n,128),lambda i,lim:(0,i))
    return pl.pallas_call(
        functools.partial(bwd_kernel,causal,block,width),
        grid_spec=pltpu.PrefetchScalarGridSpec(
            num_scalar_prefetch=1, grid=(pairs,),
            in_specs=[spec(rows),spec(keys),spec(keys),spec(rows),spec(rows),pl.BlockSpec((1,per,rows),lambda i,lim:(i,0,0))],
            out_specs=[spec(rows),spec(keys),spec(keys)],
            scratch_shapes=[pltpu.VMEM((keys,128),jnp.float32)]*2),
        out_shape=[jax.ShapeDtypeStruct((rows,d),jnp.bfloat16),jax.ShapeDtypeStruct((keys,d),jnp.bfloat16),jax.ShapeDtypeStruct((keys,d),jnp.bfloat16)],
        compiler_params=pltpu.CompilerParams(vmem_limit_bytes=48*MIB),
        cost_estimate=pl.CostEstimate(flops=10*rows*keys*d//(2 if causal else 1),bytes_accessed=8*rows*d*2,transcendentals=rows*keys*16//(2 if causal else 1)),
        name="attend_causal_back" if causal else "attend_text_back",
    )(limit,q,k,v,g,ctx,lse)

MESH=pl.DeviceIdType.MESH

def place():
    dp=lax.axis_index("dp"); fs=lax.axis_index("fsdp")
    return dp,fs,fs//2,fs%2

def turned(index,bit):
    return index+bit-2*bit*((index//bit)%2)

def greet(partners):
    barrier=pltpu.get_barrier_semaphore()
    for device in partners:
        pl.semaphore_signal(barrier,inc=1,device_id=device,device_id_type=MESH)
    pl.semaphore_wait(barrier,len(partners))

def gather_kernel(count,depth,*refs):
    ins,outs=refs[:count],refs[count:2*count]
    local,z_send,z_recv,a_send,a_recv,c_send,c_recv=refs[2*count:]
    dp,fs,z,c=place()
    ups=[((dp),lax.rem(z+k,depth)) for k in range(1,depth)]
    greet([(dp,lax.rem(z+k,depth)*2+c) for k in range(1,depth)]+[(turned(dp,1),fs),(turned(dp,2),fs),(dp,z*2+1-c)])
    sib=(dp,z*2+1-c)
    def line(w,k):
        return pltpu.make_async_remote_copy(ins[w],outs[w].at[dp,z,c],z_send.at[w,k-1],z_recv.at[w,k-1],(dp,lax.rem(z+k,depth)*2+c),MESH)
    def across(w,n,src_dp,bit):
        ref=outs[w].at[src_dp,:,c]
        return pltpu.make_async_remote_copy(ref,ref,a_send.at[w,n],a_recv.at[w,n],(turned(dp,bit),fs),MESH)
    def core(w,n,src_dp):
        ref=outs[w].at[src_dp,:,c]
        return pltpu.make_async_remote_copy(ref,ref,c_send.at[w,n],c_recv.at[w,n],sib,MESH)
    def own(w):
        return pltpu.make_async_copy(ins[w],outs[w].at[dp,z,c],local.at[w])
    for w in range(count):
        own(w).start()
        for k in range(1,depth): line(w,k).start()
    def first_bit(w): return 1+w%2
    def step0(w):
        own(w).wait()
        for k in range(1,depth): line(w,k).wait_recv()
        f,g=first_bit(w),3-first_bit(w)
        across(w,0,dp,f).start()
        across(w,1,dp,g).start()
        core(w,0,dp).start()
    def step1(w):
        f,g=first_bit(w),3-first_bit(w)
        across(w,0,dp,f).wait_recv()
        across(w,2,turned(dp,f),g).start()
        core(w,1,turned(dp,f)).start()
    def step2(w):
        f,g=first_bit(w),3-first_bit(w)
        across(w,1,dp,g).wait_recv()
        core(w,2,turned(dp,g)).start()
    def step3(w):
        f,g=first_bit(w),3-first_bit(w)
        across(w,2,turned(dp,f),g).wait_recv()
        core(w,3,turned(turned(dp,f),g)).start()
    for t in range(count+3):
        for n,step in enumerate((step0,step1,step2,step3)):
            if 0<=t-n<count: step(t-n)
    for w in range(count):
        f,g=first_bit(w),3-first_bit(w)
        for k in range(1,depth): line(w,k).wait_send()
        across(w,0,dp,f).wait_send(); across(w,1,dp,g).wait_send(); across(w,2,dp,g).wait_send()
        for n in range(4):
            core(w,n,dp).wait()

def gather(shards,depth,collective_id):
    count=len(shards)
    sem=pltpu.SemaphoreType.DMA
    outs=pl.pallas_call(
        functools.partial(gather_kernel,count,depth),
        in_specs=[pl.BlockSpec(memory_space=pl.ANY)]*count,
        out_specs=[pl.BlockSpec(memory_space=pl.ANY)]*count,
        out_shape=[jax.ShapeDtypeStruct((4,depth,2)+s.shape,s.dtype) for s in shards],
        scratch_shapes=[sem((count,)),sem((count,depth-1)),sem((count,depth-1)),sem((count,3)),sem((count,3)),sem((count,4)),sem((count,4))],
        compiler_params=pltpu.CompilerParams(collective_id=collective_id,has_side_effects=True),
        name="gather_rows",
    )(*shards)
    return [o.reshape((-1,)+s.shape[1:]) for o,s in zip(outs,shards)]

def reduce_kernel(count,depth,*refs):
    ins,outs=refs[:count],refs[count:2*count]
    held=refs[2*count:3*count]; r0=refs[3*count:4*count]; r1=refs[4*count:5*count]; r2=refs[5*count:6*count]; r3=refs[6*count:7*count]
    local,c_send,c_recv,a_send,a_recv,z_send,z_recv=refs[7*count:]
    dp,fs,z,c=place()
    hi,lo=dp//2,dp%2
    sib=(dp,z*2+1-c)
    greet([(dp,lax.rem(z+k,depth)*2+c) for k in range(1,depth)]+[(turned(dp,1),fs),(turned(dp,2),fs),sib])
    def own(w):
        return pltpu.make_async_copy(ins[w].at[:,:,:,c],held[w],local.at[w])
    def core(w):
        return pltpu.make_async_remote_copy(ins[w].at[:,:,:,1-c],r0[w],c_send.at[w],c_recv.at[w],sib,MESH)
    def first(w):
        if w%2: return pltpu.make_async_remote_copy(held[w].at[1-hi],r1[w],a_send.at[w,0],a_recv.at[w,0],(turned(dp,2),fs),MESH)
        return pltpu.make_async_remote_copy(held[w].at[:,1-lo],r1[w],a_send.at[w,0],a_recv.at[w,0],(turned(dp,1),fs),MESH)
    def second(w):
        if w%2: return pltpu.make_async_remote_copy(held[w].at[hi,1-lo],r2[w],a_send.at[w,1],a_recv.at[w,1],(turned(dp,1),fs),MESH)
        return pltpu.make_async_remote_copy(held[w].at[1-hi,lo],r2[w],a_send.at[w,1],a_recv.at[w,1],(turned(dp,2),fs),MESH)
    def line(w,k):
        return pltpu.make_async_remote_copy(held[w].at[hi,lo,lax.rem(z+k,depth)],r3[w].at[k-1],z_send.at[w,k-1],z_recv.at[w,k-1],(dp,lax.rem(z+k,depth)*2+c),MESH)
    def step0(w):
        own(w).wait(); core(w).wait_recv()
        def add(n,_):
            i,k=n//depth,n%depth
            held[w][i//2,i%2,k]=held[w][i//2,i%2,k]+r0[w][i//2,i%2,k]
            return 0
        lax.fori_loop(0,4*depth,add,0)
        first(w).start()
    def step1(w):
        first(w).wait_recv()
        def add(n,_):
            i,k=n//depth,n%depth
            if w%2: held[w][hi,i,k]=held[w][hi,i,k]+r1[w][i,k]
            else: held[w][i,lo,k]=held[w][i,lo,k]+r1[w][i,k]
            return 0
        lax.fori_loop(0,2*depth,add,0)
        second(w).start()
    def step2(w):
        second(w).wait_recv()
        def add(k,_):
            held[w][hi,lo,k]=held[w][hi,lo,k]+r2[w][k]
            return 0
        lax.fori_loop(0,depth,add,0)
        for k in range(1,depth): line(w,k).start()
    def step3(w):
        total=held[w][hi,lo,z].astype(jnp.float32)
        for k in range(1,depth):
            line(w,k).wait_recv()
            total=total+r3[w][k-1].astype(jnp.float32)
        outs[w][...]=total
    for w in range(count):
        core(w).start(); own(w).start()
    for t in range(count+3):
        for n,step in enumerate((step0,step1,step2,step3)):
            if 0<=t-n<count: step(t-n)
    for w in range(count):
        core(w).wait_send(); first(w).wait_send(); second(w).wait_send()
        for k in range(1,depth): line(w,k).wait_send()

def reduce_rows(partials,depth,collective_id):
    count=len(partials)
    sem=pltpu.SemaphoreType.DMA
    parts=[p.reshape((2,2,depth,2,p.shape[0]//(8*depth),p.shape[1])) for p in partials]
    tails=[p.shape[4:] for p in parts]
    vmem=lambda lead: [pltpu.VMEM(lead+t,p.dtype) for t,p in zip(tails,parts)]
    outs=pl.pallas_call(
        functools.partial(reduce_kernel,count,depth),
        in_specs=[pl.BlockSpec(memory_space=pl.ANY)]*count,
        out_specs=[pl.BlockSpec(memory_space=pltpu.VMEM)]*count,
        out_shape=[jax.ShapeDtypeStruct(t,jnp.float32) for t in tails],
        scratch_shapes=vmem((2,2,depth))+vmem((2,2,depth))+vmem((2,depth))+vmem((depth,))+vmem((depth-1,))
          +[sem((count,)),sem((count,)),sem((count,)),sem((count,2)),sem((count,2)),sem((count,depth-1)),sem((count,depth-1))],
        compiler_params=pltpu.CompilerParams(collective_id=collective_id,has_side_effects=True,vmem_limit_bytes=60*MIB),
        name="reduce_rows",
    )(*parts)
    return outs

AXES=("dp","fsdp")
EPSILON=1e-05

def layer_norm(tensor, gain, shift):
    centre=tensor-jnp.mean(tensor,axis=-1,keepdims=True)
    spread=jnp.mean(centre*centre,axis=-1,keepdims=True)
    return centre*lax.rsqrt(spread+EPSILON)*gain+shift

def layer_norm_back(tensor, gain, grad):
    centre=tensor-jnp.mean(tensor,axis=-1,keepdims=True)
    spread=jnp.mean(centre*centre,axis=-1,keepdims=True)
    inverse=lax.rsqrt(spread+EPSILON)
    hat=centre*inverse
    scaled=grad*gain
    pulled=inverse*(scaled-jnp.mean(scaled,axis=-1,keepdims=True)-hat*jnp.mean(scaled*hat,axis=-1,keepdims=True))
    return pulled,jnp.sum(grad*hat,axis=0),jnp.sum(grad,axis=0)

def low(tensor):
    return tensor.astype(jnp.bfloat16)

def columns(tensor):
    return jnp.sum(tensor.astype(jnp.float32),axis=0)

def gather_all(shards,depth,collective_id):
    if depth: return gather(shards,depth,collective_id)
    return [lax.all_gather(s,AXES,axis=0,tiled=True) for s in shards]

def reduce_all(partials,depth,collective_id):
    if depth: return reduce_rows(partials,depth,collective_id)
    return [lax.psum_scatter(p,AXES,scatter_dimension=0,tiled=True).astype(jnp.float32) for p in partials]

def pack_vectors(vectors,wide):
    flat=jnp.concatenate(list(vectors)+[wide])
    return jnp.pad(flat,(0,2048-flat.shape[0])).reshape(16,128)

def unpack_vectors(whole,devices,count):
    flat=whole.reshape(devices,2048)
    each=1024//devices
    vectors=flat[:,:count*each].reshape(devices,count,each).transpose(1,0,2).reshape(count,1024)
    wide=flat[:,count*each:(count+4)*each].reshape(4096)
    return vectors.astype(jnp.float32),wide.astype(jnp.float32)

def pack_grads(vectors,wide,devices):
    each=1024//devices
    flat=jnp.stack(vectors).reshape(len(vectors),devices,each).transpose(1,0,2).reshape(devices,-1)
    flat=jnp.concatenate([flat,wide.reshape(devices,4*each)],1)
    return jnp.pad(flat,((0,0),(0,1024-flat.shape[1]))).reshape(devices*8,128)

def shards(devices, depth, unit_states, dec_states, enc_states, unit_len, text_len, task_flag, cotangent,
    ln1_gain, ln1_shift, self_wq, self_bq, self_wk, self_wv, self_bv, self_wo, self_bo,
    ln2_gain, ln2_shift, cross_wq, cross_bq, cross_wk, cross_wv, cross_bv, cross_wo, cross_bo,
    ln3_gain, ln3_shift, ffn_w1, ffn_b1, ffn_w2, ffn_b2):
    w1=lax.all_gather(ffn_w1,AXES,axis=0,tiled=True)
    w2=lax.all_gather(ffn_w2,AXES,axis=0,tiled=True)
    small=pack_vectors([ln1_gain,ln1_shift,self_bq,self_bv,self_bo,ln2_gain,ln2_shift,cross_bq,cross_bv,cross_bo,ln3_gain,ln3_shift,ffn_b2],ffn_b1)
    small,wq,wk,wv,wo,cwq,cwk,cwv,cwo=gather_all([small,self_wq,self_wk,self_wv,self_wo,cross_wq,cross_wk,cross_wv,cross_wo],depth,1)
    vectors,b1=unpack_vectors(small,devices,13)
    g1,s1,bq,bv,bo,g2,s2,cbq,cbv,cbo,g3,s3,b2=[vectors[i] for i in range(13)]
    units=unit_states[0].astype(jnp.float32)
    memory=jnp.where(task_flag[0]==1,dec_states[0],enc_states[0])
    valid=(jnp.arange(units.shape[0],dtype=jnp.int32)<unit_len[0]).astype(jnp.float32)[:,None]
    n1=low(layer_norm(units,g1,s1))
    q=low(dot(n1,wq)+bq); k=low(dot(n1,wk)); v=low(dot(n1,wv)+bv)
    ctx,lse=flash_fwd(q,k,v,text_len,True)
    after_self=units+(dot(ctx,wo)+bo)
    n2=low(layer_norm(after_self,g2,s2))
    cq=low(dot(n2,cwq)+cbq); ck=low(dot(memory,cwk)); cv=low(dot(memory,cwv)+cbv)
    cctx,clse=flash_fwd(cq,ck,cv,text_len,False)
    after_cross=after_self+(dot(cctx,cwo)+cbo)
    n3=low(layer_norm(after_cross,g3,s3))
    pre=dot(n3,w1)+b1
    hidden=low(jax.nn.gelu(pre,approximate=True))
    mixed=low((after_cross+(dot(hidden,w2)+b2))*valid)
    top=cotangent[0].astype(jnp.float32)*valid
    gf=low(top)
    dw2=low(dot(hidden,gf,TN))
    _,gelu_pull=jax.vjp(functools.partial(jax.nn.gelu,approximate=True),pre)
    g_pre=low(gelu_pull(low(dot(gf,w2,NT)).astype(jnp.float32))[0])
    dw1=low(dot(n3,g_pre,TN))
    dw1=lax.psum_scatter(dw1,AXES,scatter_dimension=0,tiled=True).astype(jnp.float32)
    dw2=lax.psum_scatter(dw2,AXES,scatter_dimension=0,tiled=True).astype(jnp.float32)
    pulled,dg3,ds3=layer_norm_back(after_cross,g3,dot(g_pre,w1,NT))
    g_cross=top+pulled
    gc=low(g_cross)
    dcwo=low(dot(cctx,gc,TN))
    gcq,gck,gcv=flash_bwd(cq,ck,cv,low(dot(gc,cwo,NT)),cctx,clse,text_len,False)
    dcwq=low(dot(n2,gcq,TN)); dcwk=low(dot(memory,gck,TN)); dcwv=low(dot(memory,gcv,TN))
    g_memory=dot(gck,cwk,NT)+dot(gcv,cwv,NT)
    pulled,dg2,ds2=layer_norm_back(after_self,g2,dot(gcq,cwq,NT))
    g_self=g_cross+pulled
    gs=low(g_self)
    dwo=low(dot(ctx,gs,TN))
    gq,gk,gv=flash_bwd(q,k,v,low(dot(gs,wo,NT)),ctx,lse,text_len,True)
    dwq=low(dot(n1,gq,TN)); dwk=low(dot(n1,gk,TN)); dwv=low(dot(n1,gv,TN))
    pulled,dg1,ds1=layer_norm_back(units,g1,dot(gq,wq,NT)+dot(gk,wk,NT)+dot(gv,wv,NT))
    g_units=g_self+pulled
    is_dec=(task_flag[0]==1).astype(jnp.float32)
    grads=pack_grads([dg1,ds1,columns(gq),columns(gv),columns(gs),dg2,ds2,columns(gcq),columns(gcv),columns(gc),dg3,ds3,columns(gf)],columns(g_pre),devices)
    dcwo,dcwq,dcwk,dcwv,dwo,dwq,dwk,dwv,grads=reduce_all([dcwo,dcwq,dcwk,dcwv,dwo,dwq,dwk,dwv,grads],depth,2)
    each=1024//devices
    grads=grads.reshape(1024)
    ng=[grads[i*each:(i+1)*each] for i in range(13)]
    db1=grads[13*each:17*each]
    return (mixed[None],g_units[None],(g_memory*is_dec)[None],(g_memory*(1.0-is_dec))[None],
        ng[0],ng[1],dwq,ng[2],dwk,dwv,ng[3],dwo,ng[4],ng[5],ng[6],dcwq,ng[7],dcwk,dcwv,ng[8],dcwo,ng[9],ng[10],ng[11],dw1,db1,dw2,ng[12])

def solution(mesh):
    devices=mesh.shape["dp"]*mesh.shape["fsdp"]
    depth=mesh.shape["fsdp"]//2 if mesh.shape["dp"]==4 and (1024//devices)%16==0 else 0
    cube,flat,row=P(AXES,None,None),P(AXES),P(AXES,None)
    return jax.shard_map(
        functools.partial(shards,devices,depth),
        mesh=mesh,
        in_specs=(cube,)*3+(flat,)*3+(cube,flat,flat,row,flat,row,row,flat,row,flat,flat,flat,row,flat,row,row,flat,row,flat,flat,flat,row,flat,row,flat),
        out_specs=(cube,)*4+(flat,flat,row,flat,row,row,flat,row,flat,flat,flat,row,flat,row,row,flat,row,flat,flat,flat,row,flat,row,flat),
        check_vma=False,
    )
```

time: 2610 us -> 644 us (0.25)
  waiting for transfers between devices: 1850 us -> 1.42 us
  Pallas kernels: 0 us -> 339 us
  matrix products: 425 us -> 182 us
  other arithmetic: 139 us -> 30.1 us
  blocking collectives: 82.6 us -> 0 us
    reduce_scatter x10 -> x2, waiting for transfers between devices: 1500 us -> 0.01 us  [the longest x1 0.01 us: shards(): lax.psum_scatter(dw1, AXES, scatter_dimension=0, tiled=True)]
    all_gather x10 -> x2, waiting for transfers between devices: 349 us -> 0.01 us  [the longest x1 0.01 us: shards(): w1 = lax.all_gather(ffn_w1, AXES, axis=0, tiled=True)]
    pallas_call x0 -> x6, Pallas kernels: none -> 339 us  [the longest x1 122 us: reduce_rows(): pl.pallas_call(functools.partial(reduce_kernel, count, depth), in_specs=[...]
    dot_general x54 -> x30, matrix products: 425 us -> 182 us  [dot(): return lax.dot_general(a, b, dims, preferred_element_type=jnp.float32)]
    convert_element_type x19 -> x5, other arithmetic: 69.3 us -> 3.66 us  [the longest x1 1.79 us: shards(): lax.psum_scatter(dw2, AXES, scatter_dimension=0, tiled=True)]
    unnamed x1 -> x0, blocking collectives: 42.7 us -> none
    all_gather x1 -> x0, blocking collectives: 39.9 us -> none  [shards(): lax.all_gather(ffn_b1, ('dp', 'fsdp'), axis=0, tiled=True)]
    unnamed x270 -> x166, local copies, waits for them, and re-layouts: 68.8 us -> 33.2 us
  transfers between devices with their start and end apart: 21 -> 4, of which waited for: 18 -> 0; matrix products, arithmetic and copies ran while one was open for 13% -> 34% of each run, Pallas kernels for 0% -> 53%
where the time goes in v1:
time: 644 us; the launch traced here: 635 us
  Pallas kernels  339 us (53%)
  matrix products  182 us (28%)
  local copies, waits for them, and re-layouts  64.3 us (10%)
  other arithmetic  30.1 us (5%)
  between operations  17.2 us (3%)
    dot_general x30, matrix products, dot(): return lax.dot_general(a, b, dims, preferred_element_type=jnp.float32)  182 us
    pallas_call x1, Pallas kernels, reduce_rows(): pl.pallas_call(functools.partial(reduce_kernel, count, depth), in_specs=[...  122 us
    pallas_call x1, Pallas kernels, gather(): pl.pallas_call(functools.partial(gather_kernel, count, depth), in_specs=[...  118 us
    pallas_call x2, Pallas kernels, flash_bwd(): pl.pallas_call(functools.partial(bwd_kernel, causal, block, width), grid_...  56.9 us
    pallas_call x2, Pallas kernels, flash_fwd(): pl.pallas_call(functools.partial(fwd_kernel, causal, block, width), grid_...  42.8 us
    unnamed x166, local copies, waits for them, and re-layouts  33.2 us
  transfers between devices with their start and end apart: 4, of which 0 were waited for; matrix products, arithmetic and copies ran while one was open for 34% of the time, Pallas kernels for 53%

profile of v1, /device:TPU:0, one launch (start us, length us, event | category | flops | bytes accessed | tf_op | source)
XLA Modules:
  0.0 634.6 jit_solution(5406263966894133790)
XLA Ops:
  8.7 9.4 %concatenate.7 = bf16[544]{0:T(1024)(128)(2,1)S(1)} concatenate(bf16[32]{0:T(256)(128)(2,1)} %param.38, bf16[32]{0:T(256)(128)(2,1)} %param.39, bf16[32]{0:T(256)(128)(2,1)} %param.41, bf16[32]{0:T(256)(128)(2,1)} %param.44, bf16[32]{0:T(256)(128)(2,1)} %param.46, bf16[32]{0:T(256)(128)(2,1)} %param.47, bf16[32]{0:T(256)(128)(2,1)} %param.48, bf16[32]{0:T(256)(128)(2,1)} %param.50, ...), dimensions={0} | concatenate | bytes 2176 | tf_op jit(solution)/shard_map/concatenate | solution.py:322
  18.8 117.8 %gather_rows.1 = (bf16[4,4,2,16,128]{4,3,2,1,0:T(8,128)(2,1)}, bf16[4,4,2,32,1024]{4,3,2,1,0:T(8,128)(2,1)}, bf16[4,4,2,32,1024]{4,3,2,1,0:T(8,128)(2,1)}, bf16[...) custom-call(bf16[16,128]{1,0:T(8,128)(2,1)} %pad_bitcast_fusion.refs, ...), custom_call_target="tpu_custom_call" | custom-call | tf_op jit(solution)/shard_map/gather_rows/pallas_call | solution.py:202
  144.0 3.9 copy.75
  149.6 4.1 convolution_convert_fusion.12.k_ref
  156.5 4.1 add_convert_fusion.3.v_ref
  160.6 29.2 %attend_causal.1 = (bf16[1024,1024]{1,0:T(8,128)(2,1)S(1)}, f32[8,2,1024]{2,1,0:T(2,128)S(1)}) custom-call(s32[1]{0:T(128)S(6)} %copy.103.lim_ref, bf16[1024,1024]{1,0:T(8,128)(2,1)S(1)} %add_convert_fusion.4.q_ref, bf16[1024,1024]{1,0:T(8,128)(2,1)} %convolution_convert_fusion.12.k_ref, bf16[1024,1024]{1,0:T(8,128)(2,1)} %add_convert_fusion.3.v_ref), custom_call_target="tpu_custom_call" | custom-call | flops 2147483648 | bytes 8388608 | tf_op jit(solution)/shard_map/attend_causal/pallas_call | solution.py:62
  200.4 13.6 %attend_text.1 = (bf16[1024,1024]{1,0:T(8,128)(2,1)S(1)}, f32[8,2,1024]{2,1,0:T(2,128)S(1)}) custom-call(s32[1]{0:T(128)S(6)} %copy.103.lim_ref, bf16[1024,1024]{1,0:T(8,128)(2,1)S(1)} %add_convert_fusion.1.q_ref, bf16[256,1024]{1,0:T(8,128)(2,1)S(1)} %convolution_convert_fusion.13.k_ref, bf16[256,1024]{1,0:T(8,128)(2,1)S(1)} %fusion.37.v_ref), custom_call_target="tpu_custom_call" | custom-call | flops 1073741824 | bytes 8388608 | tf_op jit(solution)/shard_map/attend_text/pallas_call | solution.py:62
  219.2 16.9 %fusion.49 = f32[1024,4096]{1,0:T(8,128)} fusion(bf16[1024,4096]{1,0:T(8,128)(2,1)} %all-gather.3.cloned.1.call-done, f32[1024,1024]{0,1:T(8,128)} %copy-done.17, f32[1024]{0:T(1024)S(1)} %add.215, f32[1024]{0:T(1024)S(1)} %mul.258, f32[1024]{0:T(1024)S(1)} %add_rsqrt_fusion, f32[1024]{0:T(1024)S(1)} %broadcast_multiply_fusion.6), kind=kOutput, calls=%fused_computation.135 | convolution fusion | flops 8595177472 | bytes 29376512 | tf_op jit(solution)/shard_map/dot_general | solution.py:16
  236.0 25.2 %convert_reduce_fusion = (f32[4096]{0:T(1024)}, bf16[1024,4096]{1,0:T(8,128)(2,1)}) fusion(f32[1024,4096]{1,0:T(8,128)} %fusion.49, f32[4096]{0:T(1024)S(1)} %fusion.43, bf16[4096,1024]{1,0:T(8,128)(2,1)} %all-gather.5.cloned.1.call-done, bf16[1,1024,1024]{1,2,0:T(8,128)(2,1)S(1)} %copy-done.28, f32[1024]{0:T(1024)S(1)} %fusion.44), kind=kOutput, calls=%fused_computation.14 | convolution fusion | flops 8697933824 | bytes 35688448 | tf_op jit(solution)/shard_map/dot_general | solution.py:16
  261.2 15.4 %convolution_convert_fusion.1 = bf16[1024,4096]{1,0:T(8,128)(2,1)} fusion(bf16[1024,4096]{1,0:T(8,128)(2,1)} %get-tuple-element.188, f32[1024,1024]{0,1:T(8,128)} %copy-done.17, f32[1024]{0:T(1024)S(1)} %add.215, f32[1024]{0:T(1024)S(1)} %mul.258, f32[1024]{0:T(1024)S(1)} %add_rsqrt_fusion, f32[1024]{0:T(1024)S(1)} %broadcast_multiply_fusion.6), kind=kOutput, calls=%fused_computation.17 | convolution fusion | flops 8599371776 | bytes 20987904 | tf_op jit(solution)/shard_map/dot_general | solution.py:16
  276.7 17.4 %fusion.33 = bf16[1,1024,1024]{1,2,0:T(8,128)(2,1)} fusion(f32[1024,1024]{0,1:T(8,128)} %copy-done.17, f32[1024]{0:T(1024)S(1)} %fusion.44, f32[1024]{0:T(1024)S(1)} %add.222, bf16[4096,1024]{1,0:T(8,128)(2,1)} %all-gather.5.cloned.1.call-done, f32[1024,4096]{1,0:T(8,128)} %fusion.49, f32[4096]{0:T(1024)S(1)} %fusion.43), kind=kOutput, calls=%fused_computation.71 | convolution fusion | flops 8636071936 | bytes 31481856 | tf_op jit(solution)/shard_map/dot_general | solution.py:16
  294.1 4.0 copy.83
  298.1 19.7 %convolution_convert_fusion = bf16[4096,1024]{1,0:T(8,128)(2,1)} fusion(bf16[1,1024,1024]{1,2,0:T(8,128)(2,1)S(1)} %copy-done.28, f32[1024]{0:T(1024)S(1)} %fusion.44, f32[1024,4096]{1,0:T(8,128)} %fusion.49, f32[4096]{0:T(1024)S(1)} %fusion.43), kind=kOutput, calls=%fused_computation.16 | convolution fusion | flops 8639217664 | bytes 27283456 | tf_op jit(solution)/shard_map/dot_general | solution.py:16
  317.8 15.4 %fusion.61 = (f32[1024]{0:T(1024)S(1)}, f32[1024,1024]{1,0:T(8,128)}) fusion(bf16[1024,4096]{1,0:T(8,128)(2,1)} %get-tuple-element.188, bf16[1024,4096]{1,0:T(8,128)(2,1)} %all-gather.3.cloned.1.call-done), kind=kOutput, calls=%fused_computation.140 | convolution fusion | flops 8590982144 | bytes 20975616 | tf_op jit(solution)/shard_map/dot_general | solution.py:16
  333.2 5.4 copy.76
  338.6 4.6 multiply_reduce_fusion
  351.1 22.3 %attend_text_back.1 = (bf16[1024,1024]{1,0:T(8,128)(2,1)S(1)}, bf16[256,1024]{1,0:T(8,128)(2,1)S(1)}, bf16[256,1024]{1,0:T(8,128)(2,1)S(1)}) custom-call(s32[1]{0:T(128)S(6)} %copy.103.lim_ref, bf16[1024,1024]{1,0:T(8,128)(2,1)} %copy-done.8, bf16[256,1024]{1,0:T(8,128)(2,1)S(1)} %copy-done.3, bf16[256,1024]{1,0:T(8,128)(2,1)S(1)} %copy-done.5, ...), custom_call_target="tpu_custom_call" | custom-call | flops 2684354560 | bytes 16777216 | tf_op jit(solution)/shard_map/attend_text_back/pallas_call | solution.py:120
  373.4 4.4 fusion.60
  377.8 5.4 copy.77
  383.3 4.7 multiply_reduce_fusion.1
  396.9 34.6 %attend_causal_back.1 = (bf16[1024,1024]{1,0:T(8,128)(2,1)S(1)}, bf16[1024,1024]{1,0:T(8,128)(2,1)S(1)}, bf16[1024,1024]{1,0:T(8,128)(2,1)}) custom-call(s32[1]{0:T(128)S(6)} %copy.103.lim_ref, bf16[1024,1024]{1,0:T(8,128)(2,1)} %copy-done.13, bf16[1024,1024]{1,0:T(8,128)(2,1)} %convolution_convert_fusion.12.k_ref, ...), custom_call_target="tpu_custom_call" | custom-call | flops 5368709120 | bytes 16777216 | tf_op jit(solution)/shard_map/attend_causal_back/pallas_call | solution.py:120
  444.6 5.6 copy.84
  479.4 4.0 convolution_convert_fusion.3
  490.9 121.8 %reduce_rows.1 = (f32[32,1024]{1,0:T(8,128)}, f32[32,1024]{1,0:T(8,128)}, f32[32,1024]{1,0:T(8,128)}, f32[32,1024]{1,0:T(8,128)}, f32[32,1024]{1,0:T(8,128)}, /*...) custom-call(bf16[2,2,4,2,32,1024]{5,4,3,2,1,0:T(8,128)(2,1)} %bitcast.155, ...), custom_call_target="tpu_custom_call" | custom-call | tf_op jit(solution)/shard_map/reduce_rows/pallas_call | solution.py:278
  (257 shorter events, 108.6 us)
Async XLA Ops:
  7.2 211.9 %all-gather.3.cloned.1.call-start = ((), (), s32[]{:S(2)}) async-start(), calls=%async_computation.2 | async-start | bytes 8650752 | tf_op jit(solution)/shard_map/all_gather | solution.py:342
  7.9 228.1 %all-gather.5.cloned.1.call-start = ((), (), s32[]{:S(2)}) async-start(), calls=%async_computation.3 | async-start | bytes 8650752 | tf_op jit(solution)/shard_map/all_gather | solution.py:343
  8.7 610.1 %reduce-scatter.3.cloned.1.call-start = ((), (), s32[]{:S(2)}) async-start(), calls=%async_computation.4 | async-start | bytes 8650752 | tf_op jit(solution)/shard_map/reduce_scatter | solution.py:369
  142.0 47.8 %copy-start.21 = (bf16[1,1024,1024]{1,2,0:T(8,128)(2,1)}, bf16[1,1024,1024]{1,2,0:T(8,128)(2,1)S(1)}, u32[]{:S(2)}) copy-start(bf16[1,1024,1024]{1,2,0:T(8,128)(2,1)S(1)} %copy.72) | copy-start | bytes 6291460
  142.1 14.4 %copy-start.60 = (f32[1024]{0:T(1024)}, f32[1024]{0:T(1024)S(1)}, u32[]{:S(2)}) copy-start(f32[1024]{0:T(1024)S(1)} %add.187) | copy-start | bytes 12292
  142.1 14.3 %copy-start.54 = (f32[1024]{0:T(1024)}, f32[1024]{0:T(1024)S(1)}, u32[]{:S(2)}) copy-start(f32[1024]{0:T(1024)S(1)} %mul.246) | copy-start | bytes 12292
  142.4 55.2 %copy-start.62 = (f32[1024]{0:T(1024)}, f32[1024]{0:T(1024)S(1)}, u32[]{:S(2)}) copy-start(f32[1024]{0:T(1024)S(1)} %add.201) | copy-start | bytes 12292
  142.5 55.1 %copy-start.48 = (f32[1024]{0:T(1024)}, f32[1024]{0:T(1024)S(1)}, u32[]{:S(2)}) copy-start(f32[1024]{0:T(1024)S(1)} %mul.252) | copy-start | bytes 12292
  160.6 29.2 %copy-start.70 = (bf16[4,4,2,32,1024]{4,3,2,1,0:T(8,128)(2,1)S(1)}, bf16[4,4,2,32,1024]{4,3,2,1,0:T(8,128)(2,1)}, u32[]{:S(2)}) copy-start(bf16[4,4,2,32,1024]{4,3,2,1,0:T(8,128)(2,1)} %get-tuple-element.61) | copy-start | bytes 6291460
  192.4 21.6 %copy-start.14 = (f32[1024,1024]{0,1:T(8,128)}, f32[1024,1024]{0,1:T(8,128)S(1)}, u32[]{:S(2)}) copy-start(f32[1024,1024]{0,1:T(8,128)S(1)} %get-tuple-element.184) | copy-start | bytes 12582916
  200.4 16.2 %copy-start.8 = (bf16[1024,1024]{1,0:T(8,128)(2,1)}, bf16[1024,1024]{1,0:T(8,128)(2,1)S(1)}, u32[]{:S(2)}) copy-start(bf16[1024,1024]{1,0:T(8,128)(2,1)S(1)} %add_convert_fusion.1.q_ref) | copy-start | bytes 6291460
  200.4 13.6 %copy-start.74 = (bf16[4,4,2,32,1024]{4,3,2,1,0:T(8,128)(2,1)S(1)}, bf16[4,4,2,32,1024]{4,3,2,1,0:T(8,128)(2,1)}, u32[]{:S(2)}) copy-start(bf16[4,4,2,32,1024]{4,3,2,1,0:T(8,128)(2,1)} %get-tuple-element.66) | copy-start | bytes 6291460
  219.1 16.9 %copy-start.28 = (bf16[1,1024,1024]{1,2,0:T(8,128)(2,1)S(1)}, bf16[1,1024,1024]{1,2,0:T(8,128)(2,1)}, u32[]{:S(2)}) copy-start(bf16[1,1024,1024]{1,2,0:T(8,128)(2,1)} %copy.75) | copy-start | bytes 6291460
  276.6 344.0 %reduce-scatter.5.cloned.1.call-start = ((), (), s32[]{:S(2)}) async-start(), calls=%async_computation.5 | async-start | bytes 8650752 | tf_op jit(solution)/shard_map/reduce_scatter | solution.py:370
  351.1 22.3 %copy-start.73 = (bf16[4,4,2,32,1024]{4,3,2,1,0:T(8,128)(2,1)S(1)}, bf16[4,4,2,32,1024]{4,3,2,1,0:T(8,128)(2,1)}, u32[]{:S(2)}) copy-start(bf16[4,4,2,32,1024]{4,3,2,1,0:T(8,128)(2,1)} %get-tuple-element.62) | copy-start | bytes 6291460
  393.2 48.1 %copy-start.26 = (f32[1024,1024]{0,1:T(8,128)}, f32[1024,1024]{0,1:T(8,128)S(1)}, u32[]{:S(2)}) copy-start(f32[1024,1024]{0,1:T(8,128)S(1)} %get-tuple-element.166) | copy-start | bytes 12582916
  396.9 34.7 %copy-start.69 = (bf16[4,4,2,32,1024]{4,3,2,1,0:T(8,128)(2,1)S(1)}, bf16[4,4,2,32,1024]{4,3,2,1,0:T(8,128)(2,1)}, u32[]{:S(2)}) copy-start(bf16[4,4,2,32,1024]{4,3,2,1,0:T(8,128)(2,1)} %get-tuple-element.57) | copy-start | bytes 6291460
  460.0 8.1 %copy-start.7 = (bf16[1024,1024]{1,0:T(8,128)(2,1)S(1)}, bf16[1024,1024]{1,0:T(8,128)(2,1)}, u32[]{:S(2)}) copy-start(bf16[1024,1024]{1,0:T(8,128)(2,1)} %copy-done.6) | copy-start | bytes 6291460
  460.0 8.1 %copy-start.25 = (f32[1024,1024]{0,1:T(8,128)S(1)}, f32[1024,1024]{0,1:T(8,128)}, u32[]{:S(2)}) copy-start(f32[1024,1024]{0,1:T(8,128)} %copy-done.24) | copy-start | bytes 12582916
  490.9 125.0 %copy-start.33 = (bf16[4,4,2,32,1024]{4,3,2,1,0:T(8,128)(2,1)S(1)}, bf16[4,4,2,32,1024]{4,3,2,1,0:T(8,128)(2,1)}, u32[]{:S(2)}) copy-start(bf16[4,4,2,32,1024]{4,3,2,1,0:T(8,128)(2,1)} %get-tuple-element.63) | copy-start | bytes 6291460
  616.7 8.3 %copy-start.41 = (f32[32,1024]{1,0:T(8,128)S(1)}, f32[32,1024]{1,0:T(8,128)}, u32[]{:S(2)}) copy-start(f32[32,1024]{1,0:T(8,128)} %get-tuple-element.239) | copy-start | bytes 393220
  616.7 9.0 %copy-start.40 = (f32[32,1024]{1,0:T(8,128)S(1)}, f32[32,1024]{1,0:T(8,128)}, u32[]{:S(2)}) copy-start(f32[32,1024]{1,0:T(8,128)} %get-tuple-element.241) | copy-start | bytes 393220
  616.7 9.6 %copy-start.39 = (f32[32,1024]{1,0:T(8,128)S(1)}, f32[32,1024]{1,0:T(8,128)}, u32[]{:S(2)}) copy-start(f32[32,1024]{1,0:T(8,128)} %get-tuple-element.242) | copy-start | bytes 393220
  616.7 10.3 %copy-start.38 = (f32[32,1024]{1,0:T(8,128)S(1)}, f32[32,1024]{1,0:T(8,128)}, u32[]{:S(2)}) copy-start(f32[32,1024]{1,0:T(8,128)} %get-tuple-element.244) | copy-start | bytes 393220
  (56 other events, 220.5 us)
Sparse Core Ops, SparseCore 0:
  11.0 116.3 all-gather.2
  130.4 75.9 all-gather.4
  276.7 154.8 reduce-scatter.2
  433.8 158.2 reduce-scatter.4

commit v2 on v1

v2 whole, which is shorter than its diff:
```python
import functools

import jax
import jax.numpy as jnp
from jax import lax
from jax.experimental import pallas as pl
from jax.experimental.pallas import tpu as pltpu
from jax.sharding import PartitionSpec as P

MIB=1<<20

NEGATIVE=-1e30
NN=(((1,),(0,)),((),()))
NT=(((1,),(1,)),((),()))
TN=(((0,),(0,)),((),()))
def dot(a,b,dims=NN):
    return lax.dot_general(a,b,dims,preferred_element_type=jnp.float32)

def head_masks(width):
    lane=lax.broadcasted_iota(jnp.int32,(1,128),1)
    return [((lane//width)==h) for h in range(128//width)]

def run_beside(plan,depth):
    begin,ticks,finish=plan
    step=pl.program_id(0); steps=pl.num_programs(0)
    @pl.when(step==0)
    def _():
        greet(depth)
        begin()
    for n in range(7):
        @pl.when(step==n+1)
        def _():
            if n<len(ticks): ticks[n]()
    def after():
        @pl.when(step==steps-1)
        def _():
            for tick in ticks[7:]: tick()
            finish()
    return after

def fwd_kernel(causal, block, width, moved, depth, lim_ref, q_ref, k_ref, v_ref, *refs):
    ctx_ref,lse_ref=refs[moved:moved+2]
    if moved:
        after=run_beside(gather_plan(refs[:moved],refs[moved+2:2*moved+2],refs[2*moved+2:],depth),depth)
    rows=q_ref.shape[0]; keys=k_ref.shape[0]
    masks=head_masks(width)
    k=k_ref[...]
    v=v_ref[...]
    vm=[jnp.where(m,v,jnp.zeros_like(v)) for m in masks]
    for i in range(rows//block):
        kend=(i+1)*block if causal else keys
        q=q_ref[pl.ds(i*block,block),:]*jnp.bfloat16(width**-0.5)
        ctx=None
        for h,m in enumerate(masks):
            s=dot(jnp.where(m,q,jnp.zeros_like(q)),k[:kend],NT)
            if causal:
                tail=s[:,kend-block:]
                r=lax.broadcasted_iota(jnp.int32,tail.shape,0)
                c=lax.broadcasted_iota(jnp.int32,tail.shape,1)
                tail=jnp.where(c<=r,tail,NEGATIVE)
                s=tail if kend==block else jnp.concatenate([s[:,:kend-block],tail],1)
            else:
                c=lax.broadcasted_iota(jnp.int32,s.shape,1)
                s=jnp.where(c<lim_ref[0],s,NEGATIVE)
            top=jnp.max(s,axis=1,keepdims=True)
            p=jnp.exp(s-top)
            total=jnp.sum(p,axis=1,keepdims=True)
            part=dot(p.astype(jnp.bfloat16),vm[h][:kend])*(1.0/total)
            ctx=part if ctx is None else ctx+part
            lse=jnp.broadcast_to(top+jnp.log(total),(block,128))
            lse_ref[0,pl.ds(h,1),pl.ds(i*block,block)]=jnp.transpose(lse)[:1]
        ctx_ref[pl.ds(i*block,block),:]=ctx.astype(jnp.bfloat16)
    if moved: after()

def flash_fwd(q,k,v,limit,causal,block=256,width=64,moves=(),depth=0,collective_id=None):
    rows,d=q.shape; keys=k.shape[0]
    pairs=d//128
    per=128//width
    count=len(moves)
    any_=pl.BlockSpec(memory_space=pl.ANY)
    spec=lambda n: pl.BlockSpec((n,128),lambda i,lim:(0,i))
    outs=pl.pallas_call(
        functools.partial(fwd_kernel,causal,block,width,count,depth),
        grid_spec=pltpu.PrefetchScalarGridSpec(
            num_scalar_prefetch=1, grid=(pairs,),
            in_specs=[spec(rows),spec(keys),spec(keys)]+[any_]*count,
            out_specs=[spec(rows),pl.BlockSpec((1,per,rows),lambda i,lim:(i,0,0))]+[any_]*count,
            scratch_shapes=gather_sems(count,depth) if count else []),
        out_shape=[jax.ShapeDtypeStruct((rows,d),jnp.bfloat16),jax.ShapeDtypeStruct((pairs,per,rows),jnp.float32)]+gather_shapes(moves,depth),
        compiler_params=pltpu.CompilerParams(vmem_limit_bytes=48*MIB,collective_id=collective_id,has_side_effects=count>0),
        cost_estimate=pl.CostEstimate(flops=4*rows*keys*d//(2 if causal else 1),bytes_accessed=4*rows*d*2,transcendentals=rows*keys*16//(2 if causal else 1)),
        name="attend_causal" if causal else "attend_text",
    )(limit,q,k,v,*moves)
    return outs[0],outs[1],gather_result(outs[2:],moves)

def bwd_kernel(causal, block, width, moved, depth, lim_ref, q_ref,k_ref,v_ref,g_ref,ctx_ref,lse_ref,*refs):
    dq_ref,dk_ref,dv_ref=refs[moved:moved+3]
    dk_acc,dv_acc=refs[2*moved+3:2*moved+5]
    if moved:
        after=run_beside(reduce_plan(refs[:moved],refs[moved+3:2*moved+3],refs[2*moved+5:],depth),depth)
    rows=q_ref.shape[0]; keys=k_ref.shape[0]
    masks=head_masks(width)
    scale=jnp.bfloat16(width**-0.5)
    k=k_ref[...]; v=v_ref[...]
    km=[jnp.where(m,k*scale,jnp.zeros_like(k)) for m in masks]
    dk_acc[...]=jnp.zeros_like(dk_acc); dv_acc[...]=jnp.zeros_like(dv_acc)
    for i in range(rows//block):
        kend=(i+1)*block if causal else keys
        sl=pl.ds(i*block,block)
        q=q_ref[sl,:]*scale
        g=g_ref[sl,:]
        prod=g.astype(jnp.float32)*ctx_ref[sl,:].astype(jnp.float32)
        dq=None
        for h,m in enumerate(masks):
            qm=jnp.where(m,q,jnp.zeros_like(q))
            gm=jnp.where(m,g,jnp.zeros_like(g))
            delta=jnp.sum(jnp.where(m,prod,0.0),axis=1,keepdims=True)
            delta=jnp.transpose(jnp.broadcast_to(delta,(block,128)))[:1]
            lse=lse_ref[0,pl.ds(h,1),sl]
            s=dot(k[:kend],qm,NT)
            if causal:
                tail=s[kend-block:]
                r=lax.broadcasted_iota(jnp.int32,tail.shape,0)
                c=lax.broadcasted_iota(jnp.int32,tail.shape,1)
                tail=jnp.where(r<=c,tail,NEGATIVE)
                s=tail if kend==block else jnp.concatenate([s[:kend-block],tail],0)
            else:
                r=lax.broadcasted_iota(jnp.int32,s.shape,0)
                s=jnp.where(r<lim_ref[0],s,NEGATIVE)
            p=jnp.exp(s-lse)
            dp=dot(v[:kend],gm,NT)
            ds=(p*(dp-delta)).astype(jnp.bfloat16)
            dk_acc[:kend,:]+=dot(ds,qm)
            dv_acc[:kend,:]+=dot(p.astype(jnp.bfloat16),gm)
            part=dot(ds,km[h][:kend],TN)
            dq=part if dq is None else dq+part
        dq_ref[sl,:]=dq.astype(jnp.bfloat16)
    dk_ref[...]=dk_acc[...].astype(jnp.bfloat16)
    dv_ref[...]=dv_acc[...].astype(jnp.bfloat16)
    if moved: after()

def flash_bwd(q,k,v,g,ctx,lse,limit,causal,block=256,width=64,moves=(),depth=0,collective_id=None):
    rows,d=q.shape; keys=k.shape[0]
    pairs=d//128; per=128//width
    count=len(moves)
    parts=reduce_parts(moves,depth)
    kinds=[p.shape[4:]+(p.dtype,) for p in parts]
    any_=pl.BlockSpec(memory_space=pl.ANY)
    spec=lambda n: pl.BlockSpec((n,128),lambda i,lim:(0,i))
    outs=pl.pallas_call(
        functools.partial(bwd_kernel,causal,block,width,count,depth),
        grid_spec=pltpu.PrefetchScalarGridSpec(
            num_scalar_prefetch=1, grid=(pairs,),
            in_specs=[spec(rows),spec(keys),spec(keys),spec(rows),spec(rows),pl.BlockSpec((1,per,rows),lambda i,lim:(i,0,0))]+[any_]*count,
            out_specs=[spec(rows),spec(keys),spec(keys)]+[pl.BlockSpec(k[:2],lambda i,lim:(0,0)) for k in kinds],
            scratch_shapes=[pltpu.VMEM((keys,128),jnp.float32)]*2+(reduce_scratch(kinds,depth) if count else [])),
        out_shape=[jax.ShapeDtypeStruct((rows,d),jnp.bfloat16),jax.ShapeDtypeStruct((keys,d),jnp.bfloat16),jax.ShapeDtypeStruct((keys,d),jnp.bfloat16)]
          +[jax.ShapeDtypeStruct(k[:2],jnp.float32) for k in kinds],
        compiler_params=pltpu.CompilerParams(vmem_limit_bytes=56*MIB,collective_id=collective_id,has_side_effects=count>0),
        cost_estimate=pl.CostEstimate(flops=10*rows*keys*d//(2 if causal else 1),bytes_accessed=8*rows*d*2,transcendentals=rows*keys*16//(2 if causal else 1)),
        name="attend_causal_back" if causal else "attend_text_back",
    )(limit,q,k,v,g,ctx,lse,*parts)
    return outs[0],outs[1],outs[2],outs[3:]

MESH=pl.DeviceIdType.MESH
DMA=pltpu.SemaphoreType.DMA

def place():
    dp=lax.axis_index("dp"); fs=lax.axis_index("fsdp")
    return dp,fs,fs//2,fs%2

def turned(index,bit):
    return index+bit-2*bit*((index//bit)%2)

def greet(depth):
    dp,fs,z,c=place()
    partners=[(dp,lax.rem(z+k,depth)*2+c) for k in range(1,depth)]+[(turned(dp,1),fs),(turned(dp,2),fs),(dp,z*2+1-c)]
    barrier=pltpu.get_barrier_semaphore()
    for device in partners:
        pl.semaphore_signal(barrier,inc=1,device_id=device,device_id_type=MESH)
    pl.semaphore_wait(barrier,len(partners))

def gather_sems(count,depth):
    return [DMA((count,)),DMA((count,depth-1)),DMA((count,depth-1)),DMA((count,3)),DMA((count,3)),DMA((count,4)),DMA((count,4))]

def gather_plan(ins,outs,sems,depth):
    count=len(ins)
    local,z_send,z_recv,a_send,a_recv,c_send,c_recv=sems
    dp,fs,z,c=place()
    def line(w,k):
        return pltpu.make_async_remote_copy(ins[w],outs[w].at[dp,z,c],z_send.at[w,k-1],z_recv.at[w,k-1],(dp,lax.rem(z+k,depth)*2+c),MESH)
    def across(w,n,src_dp,bit):
        ref=outs[w].at[src_dp,:,c]
        return pltpu.make_async_remote_copy(ref,ref,a_send.at[w,n],a_recv.at[w,n],(turned(dp,bit),fs),MESH)
    def core(w,n,src_dp):
        ref=outs[w].at[src_dp,:,c]
        return pltpu.make_async_remote_copy(ref,ref,c_send.at[w,n],c_recv.at[w,n],(dp,z*2+1-c),MESH)
    def own(w):
        return pltpu.make_async_copy(ins[w],outs[w].at[dp,z,c],local.at[w])
    def bits(w):
        return 1+w%2,2-w%2
    def step0(w):
        f,g=bits(w)
        own(w).wait()
        for k in range(1,depth): line(w,k).wait_recv()
        across(w,0,dp,f).start()
        across(w,1,dp,g).start()
        core(w,0,dp).start()
    def step1(w):
        f,g=bits(w)
        across(w,0,dp,f).wait_recv()
        across(w,2,turned(dp,f),g).start()
        core(w,1,turned(dp,f)).start()
    def step2(w):
        f,g=bits(w)
        across(w,1,dp,g).wait_recv()
        core(w,2,turned(dp,g)).start()
    def step3(w):
        f,g=bits(w)
        across(w,2,turned(dp,f),g).wait_recv()
        core(w,3,turned(turned(dp,f),g)).start()
    def begin():
        for w in range(count):
            own(w).start()
            for k in range(1,depth): line(w,k).start()
    def tick(t):
        for n,step in enumerate((step0,step1,step2,step3)):
            if 0<=t-n<count: step(t-n)
    def finish():
        for w in range(count):
            f,g=bits(w)
            for k in range(1,depth): line(w,k).wait_send()
            across(w,0,dp,f).wait_send(); across(w,1,dp,g).wait_send(); across(w,2,dp,g).wait_send()
            for n in range(4): core(w,n,dp).wait()
    return begin,[functools.partial(tick,t) for t in range(count+3)],finish

def reduce_scratch(kinds,depth):
    count=len(kinds)
    vmem=lambda *lead: [pltpu.VMEM(lead+(r,n),d) for r,n,d in kinds]
    return (vmem(2,2,depth)+vmem(2,2,depth)+vmem(2,depth)+vmem(depth)+vmem(depth-1)
      +[DMA((count,)),DMA((count,)),DMA((count,)),DMA((count,2)),DMA((count,2)),DMA((count,depth-1)),DMA((count,depth-1))])

def reduce_plan(ins,outs,scratch,depth):
    count=len(ins)
    held,r0,r1,r2,r3=(scratch[n*count:(n+1)*count] for n in range(5))
    local,c_send,c_recv,a_send,a_recv,z_send,z_recv=scratch[5*count:]
    dp,fs,z,c=place()
    hi,lo=dp//2,dp%2
    def own(w):
        return pltpu.make_async_copy(ins[w].at[:,:,:,c],held[w],local.at[w])
    def core(w):
        return pltpu.make_async_remote_copy(ins[w].at[:,:,:,1-c],r0[w],c_send.at[w],c_recv.at[w],(dp,z*2+1-c),MESH)
    def first(w):
        if w%2: return pltpu.make_async_remote_copy(held[w].at[1-hi],r1[w],a_send.at[w,0],a_recv.at[w,0],(turned(dp,2),fs),MESH)
        return pltpu.make_async_remote_copy(held[w].at[:,1-lo],r1[w],a_send.at[w,0],a_recv.at[w,0],(turned(dp,1),fs),MESH)
    def second(w):
        if w%2: return pltpu.make_async_remote_copy(held[w].at[hi,1-lo],r2[w],a_send.at[w,1],a_recv.at[w,1],(turned(dp,1),fs),MESH)
        return pltpu.make_async_remote_copy(held[w].at[1-hi,lo],r2[w],a_send.at[w,1],a_recv.at[w,1],(turned(dp,2),fs),MESH)
    def line(w,k):
        return pltpu.make_async_remote_copy(held[w].at[hi,lo,lax.rem(z+k,depth)],r3[w].at[k-1],z_send.at[w,k-1],z_recv.at[w,k-1],(dp,lax.rem(z+k,depth)*2+c),MESH)
    def step0(w):
        own(w).wait(); core(w).wait_recv()
        def add(n,_):
            i,k=n//depth,n%depth
            held[w][i//2,i%2,k]=held[w][i//2,i%2,k]+r0[w][i//2,i%2,k]
            return 0
        lax.fori_loop(0,4*depth,add,0)
        first(w).start()
    def step1(w):
        first(w).wait_recv()
        def add(n,_):
            i,k=n//depth,n%depth
            if w%2: held[w][hi,i,k]=held[w][hi,i,k]+r1[w][i,k]
            else: held[w][i,lo,k]=held[w][i,lo,k]+r1[w][i,k]
            return 0
        lax.fori_loop(0,2*depth,add,0)
        second(w).start()
    def step2(w):
        second(w).wait_recv()
        def add(k,_):
            held[w][hi,lo,k]=held[w][hi,lo,k]+r2[w][k]
            return 0
        lax.fori_loop(0,depth,add,0)
        for k in range(1,depth): line(w,k).start()
    def step3(w):
        total=held[w][hi,lo,z].astype(jnp.float32)
        for k in range(1,depth):
            line(w,k).wait_recv()
            total=total+r3[w][k-1].astype(jnp.float32)
        outs[w][...]=total
    def begin():
        for w in range(count):
            core(w).start(); own(w).start()
    def tick(t):
        for n,step in enumerate((step0,step1,step2,step3)):
            if 0<=t-n<count: step(t-n)
    def finish():
        for w in range(count):
            core(w).wait_send(); first(w).wait_send(); second(w).wait_send()
            for k in range(1,depth): line(w,k).wait_send()
    return begin,[functools.partial(tick,t) for t in range(count+3)],finish

def gather_shapes(shards,depth):
    return [jax.ShapeDtypeStruct((4,depth,2)+s.shape,s.dtype) for s in shards]

def gather_result(outs,shards):
    return [o.reshape((-1,)+s.shape[1:]) for o,s in zip(outs,shards)]

def reduce_parts(partials,depth):
    return [p.reshape((2,2,depth,2,p.shape[0]//(8*depth),p.shape[1])) for p in partials]

def first_kernel(count,lines,depth,*refs):
    ins,vectors,wide=refs[:count],refs[count:count+lines],refs[count+lines]
    refs=refs[count+lines+1:]
    outs,table,long=refs[:count],refs[count],refs[count+1]
    packed,every=refs[count+2:count+4]
    each=vectors[0].shape[1]
    greet(depth)
    packed[...]=jnp.zeros_like(packed)
    for n in range(lines): packed[n:n+1,:each]=vectors[n][...].astype(jnp.float32)
    packed[lines:lines+1,:]=wide[...].astype(jnp.float32)
    begin,ticks,finish=gather_plan([packed]+list(ins),[every]+list(outs),refs[count+4:],depth)
    begin()
    for tick in ticks: tick()
    finish()
    lane=lax.broadcasted_iota(jnp.int32,(16,128),1)
    group=128//each
    def device(n): return every[n//(2*depth),(n//2)%depth,n%2]
    for m in range(8*depth//group):
        tile=device(m*group)
        for r in range(1,group):
            tile=jnp.where(lane>=r*each,pltpu.roll(device(m*group+r),r*each,1),tile)
        table[:,m*128:(m+1)*128]=tile
    for n in range(8*depth):
        long[:,n*128:(n+1)*128]=device(n)[lines:lines+1]

def gather_first(shards,vectors,wide,depth,collective_id):
    count=len(shards); lines=len(vectors)
    any_=pl.BlockSpec(memory_space=pl.ANY); vm=pl.BlockSpec(memory_space=pltpu.VMEM)
    total=vectors[0].shape[0]*8*depth
    outs=pl.pallas_call(
        functools.partial(first_kernel,count,lines,depth),
        in_specs=[any_]*count+[vm]*(lines+1),
        out_specs=[any_]*count+[vm]*2,
        out_shape=gather_shapes(shards,depth)+[jax.ShapeDtypeStruct((16,total),jnp.float32),jax.ShapeDtypeStruct((1,128*8*depth),jnp.float32)],
        scratch_shapes=[pltpu.VMEM((16,128),jnp.float32),pltpu.VMEM((4,depth,2,16,128),jnp.float32)]+gather_sems(count+1,depth),
        compiler_params=pltpu.CompilerParams(collective_id=collective_id,has_side_effects=True),
        name="gather_first",
    )(*shards,*[v[None] for v in vectors],wide[None])
    return gather_result(outs[:count],shards)+list(outs[count:])

def last_kernel(count,depth,*refs):
    ins,outs,scratch=refs[:count],refs[count:2*count],refs[2*count:]
    greet(depth)
    begin,ticks,finish=reduce_plan(ins,outs,scratch,depth)
    begin()
    for tick in ticks: tick()
    finish()

def reduce_rows(partials,depth,collective_id):
    count=len(partials)
    parts=reduce_parts(partials,depth)
    kinds=[p.shape[4:]+(p.dtype,) for p in parts]
    return pl.pallas_call(
        functools.partial(last_kernel,count,depth),
        in_specs=[pl.BlockSpec(memory_space=pl.ANY)]*count,
        out_specs=[pl.BlockSpec(memory_space=pltpu.VMEM)]*count,
        out_shape=[jax.ShapeDtypeStruct(k[:2],jnp.float32) for k in kinds],
        scratch_shapes=reduce_scratch(kinds,depth),
        compiler_params=pltpu.CompilerParams(collective_id=collective_id,has_side_effects=True,vmem_limit_bytes=60*MIB),
        name="reduce_rows",
    )(*parts)

EPSILON=1e-05
def normal(tensor):
    centre=tensor-jnp.mean(tensor,axis=-1,keepdims=True)
    spread=jnp.mean(centre*centre,axis=-1,keepdims=True)
    inverse=lax.rsqrt(spread+EPSILON)
    return centre*inverse,inverse

def pull_norm(hat,inverse,gain,grad):
    scaled=grad*gain
    return inverse*(scaled-jnp.mean(scaled,axis=-1,keepdims=True)-hat*jnp.mean(scaled*hat,axis=-1,keepdims=True))

def ffn_kernel(strip, length_ref, after_ref, cot_ref, w1_ref, w2_ref, b1_ref, vec_ref,
               mixed_ref, grad_ref, dw1_ref, dw2_ref, db1_ref, dvec_ref, n3, n3t, gf, branch, gn):
    j=pl.program_id(0)
    rows=after_ref.shape[0]
    gain,shift,b2=vec_ref[0:1,:],vec_ref[1:2,:],vec_ref[2:3,:]
    def live(r):
        return (r*strip+lax.broadcasted_iota(jnp.int32,(strip,1),0)<length_ref[0]).astype(jnp.float32)
    @pl.when(j==0)
    def _():
        def one(r,total):
            sl=pl.ds(r*strip,strip)
            hat,_=normal(after_ref[sl,:])
            n3[sl,:]=(hat*gain+shift).astype(jnp.bfloat16)
            top=(cot_ref[sl,:].astype(jnp.float32)*live(r)).astype(jnp.bfloat16)
            gf[sl,:]=top
            return total+jnp.sum(top.astype(jnp.float32),axis=0,keepdims=True)
        dvec_ref[2:3,:]=lax.fori_loop(0,rows//strip,one,jnp.zeros((1,after_ref.shape[1]),jnp.float32))
        n3t[...]=jnp.transpose(n3[...])
        branch[...]=jnp.zeros_like(branch); gn[...]=jnp.zeros_like(gn)
    w1=w1_ref[...]; w2=w2_ref[...]
    pre=dot(n3[...],w1)+b1_ref[...]
    back=dot(gf[...],w2,NT).astype(jnp.bfloat16).astype(jnp.float32)
    root=0.7978845608028654
    square=pre*pre
    t=jnp.tanh(root*pre*(1.0+0.044715*square))
    half=0.5*(1.0+t)
    hidden=(pre*half).astype(jnp.bfloat16)
    slope=half+0.5*pre*(1.0-t*t)*(root*(1.0+3*0.044715*square))
    g_pre=(back*slope).astype(jnp.bfloat16)
    db1_ref[...]=jnp.sum(g_pre.astype(jnp.float32),axis=0,keepdims=True)
    branch[...]+=dot(hidden,w2)
    dw2_ref[...]=dot(hidden,gf[...],TN).astype(jnp.bfloat16)
    dw1_ref[...]=dot(n3t[...],g_pre).astype(jnp.bfloat16)
    gn[...]+=dot(g_pre,w1,NT)
    @pl.when(j==pl.num_programs(0)-1)
    def _():
        def one(r,totals):
            sl=pl.ds(r*strip,strip)
            valid=live(r)
            after=after_ref[sl,:]
            mixed_ref[sl,:]=((after+(branch[sl,:]+b2))*valid).astype(jnp.bfloat16)
            hat,inverse=normal(after)
            grad=gn[sl,:]
            grad_ref[sl,:]=cot_ref[sl,:].astype(jnp.float32)*valid+pull_norm(hat,inverse,gain,grad)
            return totals[0]+jnp.sum(grad*hat,axis=0,keepdims=True),totals[1]+jnp.sum(grad,axis=0,keepdims=True)
        zero=jnp.zeros((1,after_ref.shape[1]),jnp.float32)
        dg,ds=lax.fori_loop(0,rows//strip,one,(zero,zero))
        dvec_ref[0:1,:]=dg
        dvec_ref[1:2,:]=ds

def feed_forward(after,cot,length,w1,w2,b1,vec,block=512,strip=128):
    rows,d=after.shape; ff=w1.shape[1]
    once=lambda shape: pl.BlockSpec(shape,lambda j,n:(0,0),pipeline_mode=pl.Buffered(1))
    keep=lambda shape: pl.BlockSpec(shape,lambda j,n:(0,0))
    wide=pl.BlockSpec((d,block),lambda j,n:(0,j)); tall=pl.BlockSpec((block,d),lambda j,n:(j,0)); line=pl.BlockSpec((1,block),lambda j,n:(0,j))
    bf=jnp.bfloat16; f32=jnp.float32
    return pl.pallas_call(
        functools.partial(ffn_kernel,strip),
        grid_spec=pltpu.PrefetchScalarGridSpec(
            num_scalar_prefetch=1,grid=(ff//block,),
            in_specs=[once((rows,d)),once((rows,d)),wide,tall,line,once(vec.shape)],
            out_specs=[keep((rows,d)),keep((rows,d)),wide,tall,line,keep((8,d))],
            scratch_shapes=[pltpu.VMEM((rows,d),bf),pltpu.VMEM((d,rows),bf),pltpu.VMEM((rows,d),bf),pltpu.VMEM((rows,d),f32),pltpu.VMEM((rows,d),f32)]),
        out_shape=[jax.ShapeDtypeStruct((rows,d),bf),jax.ShapeDtypeStruct((rows,d),f32),jax.ShapeDtypeStruct((d,ff),bf),jax.ShapeDtypeStruct((ff,d),bf),jax.ShapeDtypeStruct((1,ff),f32),jax.ShapeDtypeStruct((8,d),f32)],
        compiler_params=pltpu.CompilerParams(vmem_limit_bytes=60*MIB),
        cost_estimate=pl.CostEstimate(flops=12*rows*d*ff,bytes_accessed=4*d*ff*2+rows*d*12,transcendentals=rows*ff),
        name="feed_forward",
    )(length,after,cot,w1,w2,b1,vec)

AXES=("dp","fsdp")

def layer_norm(tensor, gain, shift):
    return normal(tensor)[0]*gain+shift

def layer_norm_back(tensor, gain, grad):
    hat,inverse=normal(tensor)
    return pull_norm(hat,inverse,gain,grad),jnp.sum(grad*hat,axis=0),jnp.sum(grad,axis=0)

def low(tensor):
    return tensor.astype(jnp.bfloat16)

def columns(tensor):
    return jnp.sum(tensor.astype(jnp.float32),axis=0)

def gather_all(shards):
    return [lax.all_gather(s,AXES,axis=0,tiled=True) for s in shards]

def reduce_all(partials):
    return [lax.psum_scatter(p,AXES,scatter_dimension=0,tiled=True).astype(jnp.float32) for p in partials]

def gather_vectors(vectors,wide):
    rows=jnp.stack([jnp.pad(v,(0,128-v.shape[0])) for v in list(vectors)+[wide]])
    rows=jnp.pad(rows,((0,15-len(vectors)),(0,0)))
    whole=lax.all_gather(rows,AXES).astype(jnp.float32)
    return whole[:,:,:vectors[0].shape[0]].transpose(1,0,2).reshape(16,-1),whole[:,len(vectors),:wide.shape[0]].reshape(1,-1)

def pack_grads(vectors,wide,devices):
    each=1024//devices
    flat=jnp.stack(vectors).reshape(len(vectors),devices,each).transpose(1,0,2).reshape(devices,-1)
    flat=jnp.concatenate([flat,wide.reshape(devices,4*each)],1)
    return jnp.pad(flat,((0,0),(0,1024-flat.shape[1]))).reshape(devices*8,128)

def shards(devices, depth, unit_states, dec_states, enc_states, unit_len, text_len, task_flag, cotangent,
    ln1_gain, ln1_shift, self_wq, self_bq, self_wk, self_wv, self_bv, self_wo, self_bo,
    ln2_gain, ln2_shift, cross_wq, cross_bq, cross_wk, cross_wv, cross_bv, cross_wo, cross_bo,
    ln3_gain, ln3_shift, ffn_w1, ffn_b1, ffn_w2, ffn_b2):
    w1=lax.all_gather(ffn_w1,AXES,axis=0,tiled=True)
    w2=lax.all_gather(ffn_w2,AXES,axis=0,tiled=True)
    small=[ln1_gain,ln1_shift,self_bq,self_bv,self_bo,ln2_gain,ln2_shift,cross_bq,cross_bv,cross_bo,ln3_gain,ln3_shift,ffn_b2]
    late=[self_wo,cross_wq,cross_wk,cross_wv,cross_wo]
    if depth:
        wq,wk,wv,vectors,b1=gather_first([self_wq,self_wk,self_wv],small,ffn_b1,depth,1)
    else:
        wq,wk,wv,*late=gather_all([self_wq,self_wk,self_wv]+late)
        vectors,b1=gather_vectors(small,ffn_b1)
    g1,s1,bq,bv,bo,g2,s2,cbq,cbv,cbo,g3,s3,b2=[vectors[i] for i in range(13)]
    units=unit_states[0].astype(jnp.float32)
    memory=jnp.where(task_flag[0]==1,dec_states[0],enc_states[0])
    n1=low(layer_norm(units,g1,s1))
    q=low(dot(n1,wq)+bq); k=low(dot(n1,wk)); v=low(dot(n1,wv)+bv)
    if depth: ctx,lse,late=flash_fwd(q,k,v,text_len,True,moves=late,depth=depth,collective_id=2)
    else: ctx,lse,_=flash_fwd(q,k,v,text_len,True)
    wo,cwq,cwk,cwv,cwo=late
    after_self=units+(dot(ctx,wo)+bo)
    n2=low(layer_norm(after_self,g2,s2))
    cq=low(dot(n2,cwq)+cbq); ck=low(dot(memory,cwk)); cv=low(dot(memory,cwv)+cbv)
    cctx,clse,_=flash_fwd(cq,ck,cv,text_len,False)
    after_cross=after_self+(dot(cctx,cwo)+cbo)
    mixed,g_cross,dw1,dw2,db1,dvec=feed_forward(after_cross,cotangent[0],unit_len,w1,w2,b1,jnp.concatenate([vectors[10:13],jnp.zeros((5,1024),jnp.float32)]))
    dw1,dw2=reduce_all([dw1,dw2])
    gc=low(g_cross)
    dcwo=low(dot(cctx,gc,TN))
    gcq,gck,gcv,_=flash_bwd(cq,ck,cv,low(dot(gc,cwo,NT)),cctx,clse,text_len,False)
    dcwq=low(dot(n2,gcq,TN)); dcwk=low(dot(memory,gck,TN)); dcwv=low(dot(memory,gcv,TN))
    g_memory=dot(gck,cwk,NT)+dot(gcv,cwv,NT)
    pulled,dg2,ds2=layer_norm_back(after_self,g2,dot(gcq,cwq,NT))
    g_self=g_cross+pulled
    gs=low(g_self)
    dwo=low(dot(ctx,gs,TN))
    early=[dcwo,dcwq,dcwk,dcwv,dwo]
    if depth: gq,gk,gv,early=flash_bwd(q,k,v,low(dot(gs,wo,NT)),ctx,lse,text_len,True,moves=early,depth=depth,collective_id=3)
    else: gq,gk,gv,_=flash_bwd(q,k,v,low(dot(gs,wo,NT)),ctx,lse,text_len,True)
    dwq=low(dot(n1,gq,TN)); dwk=low(dot(n1,gk,TN)); dwv=low(dot(n1,gv,TN))
    pulled,dg1,ds1=layer_norm_back(units,g1,dot(gq,wq,NT)+dot(gk,wk,NT)+dot(gv,wv,NT))
    g_units=g_self+pulled
    is_dec=(task_flag[0]==1).astype(jnp.float32)
    grads=pack_grads([dg1,ds1,columns(gq),columns(gv),columns(gs),dg2,ds2,columns(gcq),columns(gcv),columns(gc),dvec[0],dvec[1],dvec[2]],db1[0],devices)
    if depth: dwq,dwk,dwv,grads=reduce_rows([dwq,dwk,dwv,grads],depth,4)
    else: dwq,dwk,dwv,grads,*early=reduce_all([dwq,dwk,dwv,grads]+early)
    dcwo,dcwq,dcwk,dcwv,dwo=early
    each=1024//devices
    grads=grads.reshape(1024)
    ng=[grads[i*each:(i+1)*each] for i in range(13)]
    db1=grads[13*each:17*each]
    return (mixed[None],g_units[None],(g_memory*is_dec)[None],(g_memory*(1.0-is_dec))[None],
        ng[0],ng[1],dwq,ng[2],dwk,dwv,ng[3],dwo,ng[4],ng[5],ng[6],dcwq,ng[7],dcwk,dcwv,ng[8],dcwo,ng[9],ng[10],ng[11],dw1,db1,dw2,ng[12])

def solution(mesh):
    devices=mesh.shape["dp"]*mesh.shape["fsdp"]
    depth=mesh.shape["fsdp"]//2 if mesh.shape["dp"]==4 and (1024//devices)%16==0 else 0
    cube,flat,row=P(AXES,None,None),P(AXES),P(AXES,None)
    return jax.shard_map(
        functools.partial(shards,devices,depth),
        mesh=mesh,
        in_specs=(cube,)*3+(flat,)*3+(cube,flat,flat,row,flat,row,row,flat,row,flat,flat,flat,row,flat,row,row,flat,row,flat,flat,flat,row,flat,row,flat),
        out_specs=(cube,)*4+(flat,flat,row,flat,row,row,flat,row,flat,flat,flat,row,flat,row,row,flat,row,flat,flat,flat,row,flat,row,flat),
        check_vma=False,
    )
```

time: 644 us -> 617 us (0.958)
  matrix products: 182 us -> 87.2 us
  Pallas kernels: 339 us -> 419 us
  waiting for transfers between devices: 1.42 us -> 43.8 us
  local copies, waits for them, and re-layouts: 64.3 us -> 22 us
  other arithmetic: 30.1 us -> 18.8 us
    dot_general x30 -> x24, matrix products: 182 us -> 87.2 us  [dot(): return lax.dot_general(a, b, dims, preferred_element_type=jnp.float32)]
    pallas_call x6 -> x7, Pallas kernels: 339 us -> 419 us  [the longest x2 123 us: flash_bwd(): pl.pallas_call(functools.partial(bwd_kernel, causal, block, width, count,...]
    reduce_scatter x2, waiting for transfers between devices: 0.01 us -> 32.8 us  [reduce_all(): lax.psum_scatter(p, AXES, scatter_dimension=0, tiled=True)]
    unnamed x166 -> x139, local copies, waits for them, and re-layouts: 33.2 us -> 11.5 us
    dot_general x2 -> x0, local copies, waits for them, and re-layouts: 10.8 us -> none  [dot(): return lax.dot_general(a, b, dims, preferred_element_type=jnp.float32)]
    all_gather x1, waiting for transfers between devices: 0.01 us -> 9.08 us  [shards(): w2 = lax.all_gather(ffn_w2, AXES, axis=0, tiled=True)]
    concatenate x1, local copies, waits for them, and re-layouts: 9.43 us -> 0.62 us  [shards(): jnp.concatenate([vectors[10:13], jnp.zeros((5, 1024), jnp.float32)])]
    reduce_sum x6 -> x3, other arithmetic: 11.2 us -> 3.17 us  [the longest x1 1.93 us: normal(): centre = tensor - jnp.mean(tensor, axis=-1, keepdims=True)]
  transfers between devices with their start and end apart: 4 -> 4, of which waited for: 0 -> 2; matrix products, arithmetic and copies ran while one was open for 34% -> 19% of each run, Pallas kernels for 53% -> 57%
where the time goes in v2:
time: 617 us; the launch traced here: 608 us
  Pallas kernels  419 us (68%)
  matrix products  87.2 us (14%)
  waiting for transfers between devices  43.8 us (7%)
  local copies, waits for them, and re-layouts  22 us (4%)
  other arithmetic  18.8 us (3%)
  between operations  16.8 us (3%)
    pallas_call x2, Pallas kernels, flash_bwd(): pl.pallas_call(functools.partial(bwd_kernel, causal, block, width, count,...  123 us
    pallas_call x2, Pallas kernels, flash_fwd(): pl.pallas_call(functools.partial(fwd_kernel, causal, block, width, count,...  93.8 us
    dot_general x24, matrix products, dot(): return lax.dot_general(a, b, dims, preferred_element_type=jnp.float32)  87.2 us
    pallas_call x1, Pallas kernels, feed_forward(): pl.pallas_call(functools.partial(ffn_kernel, strip), grid_spec=pltpu.Pref...  73.5 us
    pallas_call x1, Pallas kernels, reduce_rows(): pl.pallas_call(functools.partial(last_kernel, count, depth), in_specs=[pl...  72.4 us
    pallas_call x1, Pallas kernels, gather_first(): pl.pallas_call(functools.partial(first_kernel, count, lines, depth), in_s...  56.5 us
    reduce_scatter x2, waiting for transfers between devices, reduce_all(): lax.psum_scatter(p, AXES, scatter_dimension=0, tiled=True)  32.8 us
  transfers between devices with their start and end apart: 4, of which 2 were waited for; matrix products, arithmetic and copies ran while one was open for 19% of the time, Pallas kernels for 57%

profile of v2, /device:TPU:0, one launch (start us, length us, event | category | flops | bytes accessed | tf_op | source)
XLA Modules:
  0.0 607.8 jit_solution(9374314767591776083)
XLA Ops:
  10.0 56.5 %gather_first.1 = (bf16[4,4,2,32,1024]{4,3,2,1,0:T(8,128)(2,1)}, bf16[4,4,2,32,1024]{4,3,2,1,0:T(8,128)(2,1)}, bf16[4,4,2,32,1024]{4,3,2,1,0:T(8,128)(2,1)}, f32[16,1024]{1,0:T(8,128)}, f32[1,4096]{1,0:T(1,128)}) custom-call(bf16[32,1024]{1,0:T(8,128)(2,1)} %refs_0_.2, bf16[32,1024]{1,0:T(8,128)(2,1)} %refs_1_.2, bf16[32,1024]{1,0:T(8,128)(2,1)} %refs_2_.2, ...), custom_call_target="tpu_custom_call" | custom-call | tf_op jit(solution)/shard_map/gather_first/pallas_call | solution.py:341
  71.5 3.7 convolution_convert_fusion.10.k_ref
  75.3 3.8 add_convert_fusion.2.v_ref
  79.1 3.8 add_convert_fusion.3.q_ref
  82.9 80.5 %attend_causal.1 = (bf16[1024,1024]{1,0:T(8,128)(2,1)S(1)}, f32[8,2,1024]{2,1,0:T(2,128)S(1)}, bf16[4,4,2,32,1024]{4,3,2,1,0:T(8,128)(2,1)S(1)}, bf16[4,4,2,32,1...) custom-call(s32[1]{0:T(128)S(6)} %copy.74.lim_ref, ...), custom_call_target="tpu_custom_call" | custom-call | flops 2147483648 | bytes 8388608 | tf_op jit(solution)/shard_map/attend_causal/pallas_call | solution.py:82
  173.5 13.4 %attend_text.1 = (bf16[1024,1024]{1,0:T(8,128)(2,1)S(1)}, f32[8,2,1024]{2,1,0:T(2,128)S(1)}) custom-call(s32[1]{0:T(128)S(6)} %copy.74.lim_ref, bf16[1024,1024]{1,0:T(8,128)(2,1)S(1)} %add_convert_fusion.q_ref, bf16[256,1024]{1,0:T(8,128)(2,1)S(1)} %convolution_convert_fusion.11.k_ref, bf16[256,1024]{1,0:T(8,128)(2,1)S(1)} %fusion.22.v_ref), custom_call_target="tpu_custom_call" | custom-call | flops 1073741824 | bytes 8388608 | tf_op jit(solution)/shard_map/attend_text/pallas_call | solution.py:82
  188.9 4.4 add_add_fusion.1.after_ref
  193.2 9.1 %all-gather.5.cloned.1.call-done.w2_ref = bf16[4096,1024]{1,0:T(8,128)(2,1)} async-done(((bf16[128,1024]{1,0:T(8,128)(2,1)}), bf16[4096,1024]{1,0:T(8,128)(2,1)}) %all-gather.5.cloned.1.call-update) | async-done | bytes 8388624 | tf_op jit(solution)/shard_map/all_gather | solution.py:492
  202.3 73.5 %feed_forward.1 = (bf16[1024,1024]{1,0:T(8,128)(2,1)}, f32[1024,1024]{1,0:T(8,128)}, bf16[1024,4096]{1,0:T(8,128)(2,1)}, bf16[4096,1024]{1,0:T(8,128)(2,1)}, f32[1,4096]{1,0:T(1,128)}, /*index=5*/f32[8,1024]{1,0:T(8,128)}) custom-call(s32[1]{0:T(128)S(6)} %copy.73.length_ref, f32[1024,1024]{1,0:T(8,128)} %add_add_fusion.1.after_ref, ...), custom_call_target="tpu_custom_call" | custom-call | flops 51539607552 | bytes 46137344 | tf_op jit(solution)/shard_map/feed_forward/pallas_call | solution.py:441
  276.4 6.6 %convolution_convert_fusion.9.g_ref = bf16[1024,1024]{1,0:T(8,128)(2,1)} fusion(bf16[1024,1024]{1,0:T(8,128)(2,1)} %bitcast.210, f32[1024,1024]{1,0:T(8,128)} %get-tuple-element.76), kind=kOutput, calls=%fused_computation.52 | convolution fusion | flops 2149580800 | bytes 8388608 | tf_op jit(solution)/shard_map/dot_general | solution.py:17
  283.0 22.0 %attend_text_back.1 = (bf16[1024,1024]{1,0:T(8,128)(2,1)}, bf16[256,1024]{1,0:T(8,128)(2,1)}, bf16[256,1024]{1,0:T(8,128)(2,1)}) custom-call(s32[1]{0:T(128)S(6)} %copy.74.lim_ref, bf16[1024,1024]{1,0:T(8,128)(2,1)} %copy-done.13, bf16[256,1024]{1,0:T(8,128)(2,1)} %copy-done.9, bf16[256,1024]{1,0:T(8,128)(2,1)} %copy-done.10, ...), custom_call_target="tpu_custom_call" | custom-call | flops 2684354560 | bytes 16777216 | tf_op jit(solution)/shard_map/attend_text_back/pallas_call | solution.py:150
  305.1 5.7 multiply_reduce_fusion
  315.0 3.8 convolution_convert_fusion.7
  321.1 3.8 convolution_convert_fusion.3
  328.6 4.1 convolution_convert_fusion.6
  332.6 100.8 %attend_causal_back.1 = (bf16[1024,1024]{1,0:T(8,128)(2,1)}, bf16[1024,1024]{1,0:T(8,128)(2,1)}, bf16[1024,1024]{1,0:T(8,128)(2,1)}, f32[32,1024]{1,0:T(8,128)},...) custom-call(s32[1]{0:T(128)S(6)} %copy.74.lim_ref, ...), custom_call_target="tpu_custom_call" | custom-call | flops 5368709120 | bytes 16777216 | tf_op jit(solution)/shard_map/attend_causal_back/pallas_call | solution.py:150
  433.5 4.1 fusion.42
  440.5 6.0 fusion.15
  459.9 5.8 convolution_convert_fusion.2
  465.8 4.2 convolution_convert_fusion.1
  470.0 4.2 convolution_convert_fusion
  474.2 72.4 %reduce_rows.1 = (f32[32,1024]{1,0:T(8,128)}, f32[32,1024]{1,0:T(8,128)}, f32[32,1024]{1,0:T(8,128)}, f32[8,128]{1,0:T(8,128)}) custom-call(bf16[2,2,4,2,32,1024]{5,4,3,2,1,0:T(8,128)(2,1)} %bitcast.150, bf16[2,2,4,2,32,1024]{5,4,3,2,1,0:T(8,128)(2,1)} %bitcast.151, bf16[2,2,4,2,32,1024]{5,4,3,2,1,0:T(8,128)(2,1)} %bitcast.152, ...), custom_call_target="tpu_custom_call" | custom-call | tf_op jit(solution)/shard_map/reduce_rows/pallas_call | solution.py:364
  552.1 4.3 multiply_bitcast_fusion
  561.2 32.8 %reduce-scatter.5.cloned.1.call-done = bf16[128,1024]{1,0:T(8,128)(2,1)} async-done(((bf16[4096,1024]{1,0:T(8,128)(2,1)}), bf16[128,1024]{1,0:T(8,128)(2,1)}) %reduce-scatter.5.cloned.1.call-update) | async-done | bytes 262160 | tf_op jit(solution)/shard_map/reduce_scatter | solution.py:473
  (198 shorter events, 61.9 us)
Async XLA Ops:
  7.2 63.5 %copy-start.15 = (bf16[1,1024,1024]{2,1,0:T(8,128)(2,1)S(1)}, bf16[1,1024,1024]{2,1,0:T(8,128)(2,1)}, u32[]{:S(2)}) copy-start(bf16[1,1024,1024]{2,1,0:T(8,128)(2,1)} %param.31) | copy-start | bytes 6291460
  7.2 186.0 %all-gather.3.cloned.1.call-start = ((), (), s32[]{:S(2)}) async-start(), calls=%async_computation.2 | async-start | bytes 8650752 | tf_op jit(solution)/shard_map/all_gather | solution.py:491
  8.0 194.3 %all-gather.5.cloned.1.call-start = ((), (), s32[]{:S(2)}) async-start(), calls=%async_computation.3 | async-start | bytes 8650752 | tf_op jit(solution)/shard_map/all_gather | solution.py:492
  8.7 550.7 %reduce-scatter.3.cloned.1.call-start = ((), (), s32[]{:S(2)}) async-start(), calls=%async_computation.4 | async-start | bytes 8650752 | tf_op jit(solution)/shard_map/reduce_scatter | solution.py:473
  70.7 369.3 %copy-start.45 = (f32[1024]{0:T(1024)}, f32[1024]{0:T(1024)S(1)}, u32[]{:S(2)}) copy-start(f32[1024]{0:T(1024)S(1)} %broadcast_multiply_fusion.5) | copy-start | bytes 12292
  71.4 368.6 %copy-start.49 = (f32[1024]{0:T(1024)}, f32[1024]{0:T(1024)S(1)}, u32[]{:S(2)}) copy-start(f32[1024]{0:T(1024)S(1)} %add_rsqrt_fusion.1) | copy-start | bytes 12292
  71.5 368.6 %copy-start.47 = (f32[1,1024]{1,0:T(1,128)}, f32[1,1024]{1,0:T(1,128)S(1)}, u32[]{:S(2)}) copy-start(f32[1,1024]{1,0:T(1,128)S(1)} %get-tuple-element.120) | copy-start | bytes 12292
  82.9 80.5 %copy-start.16 = (bf16[1,1024,1024]{2,1,0:T(8,128)(2,1)S(1)}, bf16[1,1024,1024]{2,1,0:T(8,128)(2,1)}, u32[]{:S(2)}) copy-start(bf16[1,1024,1024]{2,1,0:T(8,128)(2,1)} %param.31) | copy-start | bytes 6291460
  163.4 157.6 %copy-start = (bf16[1024,1024]{1,0:T(8,128)(2,1)}, bf16[1024,1024]{1,0:T(8,128)(2,1)S(1)}, u32[]{:S(2)}) copy-start(bf16[1024,1024]{1,0:T(8,128)(2,1)S(1)} %get-tuple-element.67.ctx_ref) | copy-start | bytes 6291460
  165.9 21.6 %copy-start.20 = (f32[1024,1024]{1,0:T(8,128)}, f32[1024,1024]{1,0:T(8,128)S(1)}, u32[]{:S(2)}) copy-start(f32[1024,1024]{1,0:T(8,128)S(1)} %get-tuple-element.135) | copy-start | bytes 12582916
  173.5 15.4 %copy-start.64 = (bf16[4,4,2,32,1024]{4,3,2,1,0:T(8,128)(2,1)S(1)}, bf16[4,4,2,32,1024]{4,3,2,1,0:T(8,128)(2,1)}, u32[]{:S(2)}) copy-start(bf16[4,4,2,32,1024]{4,3,2,1,0:T(8,128)(2,1)} %get-tuple-element.73) | copy-start | bytes 6291460
  275.8 318.1 %reduce-scatter.5.cloned.1.call-start = ((), (), s32[]{:S(2)}) async-start(), calls=%async_computation.5 | async-start | bytes 8650752 | tf_op jit(solution)/shard_map/reduce_scatter | solution.py:473
  283.0 22.0 %copy-start.21 = (f32[1024,1024]{1,0:T(8,128)S(1)}, f32[1024,1024]{1,0:T(8,128)}, u32[]{:S(2)}) copy-start(f32[1024,1024]{1,0:T(8,128)} %copy-done.20) | copy-start | bytes 12582916
  332.6 100.8 %copy-start.61 = (bf16[4,4,2,32,1024]{4,3,2,1,0:T(8,128)(2,1)S(1)}, bf16[4,4,2,32,1024]{4,3,2,1,0:T(8,128)(2,1)}, u32[]{:S(2)}) copy-start(bf16[4,4,2,32,1024]{4,3,2,1,0:T(8,128)(2,1)} %get-tuple-element.65) | copy-start | bytes 6291460
  474.2 73.6 %copy-start.55 = (f32[1024]{0:T(1024)S(1)}, f32[1024]{0:T(1024)}, u32[]{:S(2)}) copy-start(f32[1024]{0:T(1024)} %get-tuple-element.101) | copy-start | bytes 12292
  474.2 73.6 %copy-start.54 = (f32[1024]{0:T(1024)S(1)}, f32[1024]{0:T(1024)}, u32[]{:S(2)}) copy-start(f32[1024]{0:T(1024)} %get-tuple-element.102) | copy-start | bytes 12292
  556.5 39.3 %copy-start.43 = (f32[32,1024]{1,0:T(8,128)S(1)}, f32[32,1024]{1,0:T(8,128)}, u32[]{:S(2)}) copy-start(f32[32,1024]{1,0:T(8,128)} %get-tuple-element.174) | copy-start | bytes 393220
  556.5 40.0 %copy-start.42 = (f32[32,1024]{1,0:T(8,128)S(1)}, f32[32,1024]{1,0:T(8,128)}, u32[]{:S(2)}) copy-start(f32[32,1024]{1,0:T(8,128)} %get-tuple-element.176) | copy-start | bytes 393220
  556.5 40.6 %copy-start.41 = (f32[32,1024]{1,0:T(8,128)S(1)}, f32[32,1024]{1,0:T(8,128)}, u32[]{:S(2)}) copy-start(f32[32,1024]{1,0:T(8,128)} %get-tuple-element.177) | copy-start | bytes 393220
  556.5 41.3 %copy-start.40 = (f32[32,1024]{1,0:T(8,128)S(1)}, f32[32,1024]{1,0:T(8,128)}, u32[]{:S(2)}) copy-start(f32[32,1024]{1,0:T(8,128)} %get-tuple-element.179) | copy-start | bytes 393220
  556.5 41.9 %copy-start.39 = (f32[32,1024]{1,0:T(8,128)S(1)}, f32[32,1024]{1,0:T(8,128)}, u32[]{:S(2)}) copy-start(f32[32,1024]{1,0:T(8,128)} %get-tuple-element.183) | copy-start | bytes 393220
  556.5 42.6 %copy-start.38 = (f32[32,1024]{1,0:T(8,128)S(1)}, f32[32,1024]{1,0:T(8,128)}, u32[]{:S(2)}) copy-start(f32[32,1024]{1,0:T(8,128)} %get-tuple-element.185) | copy-start | bytes 393220
  556.5 43.2 %copy-start.37 = (f32[32,1024]{1,0:T(8,128)S(1)}, f32[32,1024]{1,0:T(8,128)}, u32[]{:S(2)}) copy-start(f32[32,1024]{1,0:T(8,128)} %get-tuple-element.186) | copy-start | bytes 393220
  556.5 43.9 %copy-start.36 = (f32[32,1024]{1,0:T(8,128)S(1)}, f32[32,1024]{1,0:T(8,128)}, u32[]{:S(2)}) copy-start(f32[32,1024]{1,0:T(8,128)} %get-tuple-element.188) | copy-start | bytes 393220
  (45 other events, 202.2 us)
Sparse Core Ops, SparseCore 0:
  11.0 103.6 all-gather.2
  117.7 84.5 all-gather.4
  276.0 158.7 reduce-scatter.2
  436.9 157.0 reduce-scatter.4

commit v3 on v2

--- a/solution.py
+++ b/solution.py
@@ -93,11 +93,7 @@
     )(limit,q,k,v,*moves)
     return outs[0],outs[1],gather_result(outs[2:],moves)
 
-def bwd_kernel(causal, block, width, moved, depth, lim_ref, q_ref,k_ref,v_ref,g_ref,ctx_ref,lse_ref,*refs):
-    dq_ref,dk_ref,dv_ref=refs[moved:moved+3]
-    dk_acc,dv_acc=refs[2*moved+3:2*moved+5]
-    if moved:
-        after=run_beside(reduce_plan(refs[:moved],refs[moved+3:2*moved+3],refs[2*moved+5:],depth),depth)
+def back_of_pair(causal, block, width, lim_ref, q_ref, k_ref, v_ref, g_ref, ctx_ref, lse_ref, dq_ref, dk_acc, dv_acc):
     rows=q_ref.shape[0]; keys=k_ref.shape[0]
     masks=head_masks(width)
     scale=jnp.bfloat16(width**-0.5)
@@ -135,32 +131,137 @@
             part=dot(ds,km[h][:kend],TN)
             dq=part if dq is None else dq+part
         dq_ref[sl,:]=dq.astype(jnp.bfloat16)
+
+def bwd_kernel(causal, block, width, lim_ref, *refs):
+    dq_ref,dk_ref,dv_ref,dk_acc,dv_acc=refs[6:]
+    back_of_pair(causal,block,width,lim_ref,*refs[:6],dq_ref,dk_acc,dv_acc)
     dk_ref[...]=dk_acc[...].astype(jnp.bfloat16)
     dv_ref[...]=dv_acc[...].astype(jnp.bfloat16)
-    if moved: after()
-
-def flash_bwd(q,k,v,g,ctx,lse,limit,causal,block=256,width=64,moves=(),depth=0,collective_id=None):
+
+def flash_bwd(q,k,v,g,ctx,lse,limit,causal,block=256,width=64):
     rows,d=q.shape; keys=k.shape[0]
     pairs=d//128; per=128//width
-    count=len(moves)
-    parts=reduce_parts(moves,depth)
-    kinds=[p.shape[4:]+(p.dtype,) for p in parts]
+    spec=lambda n: pl.BlockSpec((n,128),lambda i,lim:(0,i))
+    return pl.pallas_call(
+        functools.partial(bwd_kernel,causal,block,width),
+        grid_spec=pltpu.PrefetchScalarGridSpec(
+            num_scalar_prefetch=1,grid=(pairs,),
+            in_specs=[spec(rows),spec(keys),spec(keys),spec(rows),spec(rows),pl.BlockSpec((1,per,rows),lambda i,lim:(i,0,0))],
+            out_specs=[spec(rows),spec(keys),spec(keys)],
+            scratch_shapes=[pltpu.VMEM((keys,128),jnp.float32)]*2),
+        out_shape=[jax.ShapeDtypeStruct((n,d),jnp.bfloat16) for n in (rows,keys,keys)],
+        compiler_params=pltpu.CompilerParams(vmem_limit_bytes=60*MIB),
+        name="attend_causal_back" if causal else "attend_text_back",
+    )(limit,q,k,v,g,ctx,lse)
+
+def sub_layer_kernel(causal, block, width, pairs, depth, lim_ref, flag_ref, *refs):
+    pair_refs=refs[:6]; refs=refs[6:]
+    normed_ref,source_ref,whole_ref,out_ref,gain_ref=refs[:5]; refs=refs[5:]
+    late_count=5 if causal else 6
+    late_in=refs[:late_count]; refs=refs[late_count:]
+    if causal: grad_out,sums_ref=refs[:2]; refs=refs[2:]
+    else: grad_out,low_out,ctx_out,dec_ref,enc_ref,sums_ref=refs[:6]; refs=refs[6:]
+    results=refs[:4]; refs=refs[4:]
+    late=refs[:late_count]; late_sem=refs[late_count]; refs=refs[late_count+1:]
+    normed_t,source_t,whole_t,dq_all,dk_all,dv_all,dk_acc,dv_acc=refs[:8]; refs=refs[8:]
+    low_all,ctx_all=(None,None) if causal else refs[:2]
+    streams=refs if causal else refs[2:]
+    half=len(streams)//2
+    step=pl.program_id(0)
+    rows=pair_refs[0].shape[0]
+    def keep_pair(first):
+        def store(i,total):
+            for n in range(2):
+                results[first+n][:,pl.ds(pl.multiple_of(i*128,128),128)]=total[:,n*128:(n+1)*128]
+        return store
+    tick1,rest1=stream_plan(pairs,lambda i: 0,keep_pair(0),streams[:half],depth)
+    tick2,rest2=stream_plan(pairs,lambda i: 1,keep_pair(2),streams[half:],depth)
+    def late_copy(n): return pltpu.make_async_copy(late_in[n],late[n],late_sem.at[n])
+    @pl.when(step==0)
+    def _():
+        greet(depth)
+        for n in range(late_count): late_copy(n).start()
+        normed_t[...]=jnp.transpose(normed_ref[...])
+        whole_t[...]=jnp.transpose(whole_ref[...])
+        if not causal: source_t[...]=jnp.transpose(source_ref[...])
+    tick1(step); tick2(step)
+    here=pl.ds(pl.multiple_of(step*128,128),128)
+    back_of_pair(causal,block,width,lim_ref,*pair_refs,dq_all.at[:,here],dk_acc,dv_acc)
+    dq=dq_all[:,here]; dk=dk_acc[...].astype(jnp.bfloat16); dv=dv_acc[...].astype(jnp.bfloat16); do=out_ref[...]
+    dk_all[:,here]=dk; dv_all[:,here]=dv
+    source=normed_t[...] if causal else source_t[...]
+    write_made(streams[0],step,0,dot(normed_t[...],dq).astype(jnp.bfloat16))
+    write_made(streams[0],step,128,dot(source,dk).astype(jnp.bfloat16))
+    write_made(streams[half],step,0,dot(source,dv).astype(jnp.bfloat16))
+    write_made(streams[half],step,128,dot(whole_t[...],do).astype(jnp.bfloat16))
+    for n,value in enumerate((dq,dv,do)):
+        sums_ref[n:n+1,here]=jnp.sum(value.astype(jnp.float32),axis=0,keepdims=True)
+    @pl.when(step==pairs-1)
+    def _():
+        for n in range(late_count): late_copy(n).wait()
+        gain=gain_ref[0:1,:]
+        sums_ref[3:8,:]=jnp.zeros((5,sums_ref.shape[1]),jnp.float32)
+        strip=256
+        for r in range(rows//strip):
+            rest1[r](); rest2[r]()
+            sl=pl.ds(r*strip,strip)
+            if causal:
+                wq,wk,wv,residual,total=late
+                grad=dot(dq_all[sl,:],wq[...],NT)+dot(dk_all[sl,:],wk[...],NT)+dot(dv_all[sl,:],wv[...],NT)
+            else:
+                wq,wk,wv,wo,residual,total=late
+                grad=dot(dq_all[sl,:],wq[...],NT)
+            hat,inverse=normal(residual[sl,:].astype(jnp.float32))
+            sums_ref[3:4,:]+=jnp.sum(grad*hat,axis=0,keepdims=True)
+            sums_ref[4:5,:]+=jnp.sum(grad,axis=0,keepdims=True)
+            whole=total[sl,:]+pull_norm(hat,inverse,gain,grad)
+            total[sl,:]=whole
+            if not causal:
+                low_all[sl,:]=whole.astype(jnp.bfloat16)
+                ctx_all[sl,:]=dot(low_all[sl,:],wo[...],NT).astype(jnp.bfloat16)
+        copies=[pltpu.make_async_copy(late[-1],grad_out,late_sem.at[0])]
+        if not causal:
+            copies+=[pltpu.make_async_copy(low_all,low_out,late_sem.at[1]),pltpu.make_async_copy(ctx_all,ctx_out,late_sem.at[2])]
+        for copy in copies: copy.start()
+        for n in range(rows//strip,len(rest1)): rest1[n](); rest2[n]()
+        if not causal:
+            memory_grad=dot(dk_all[...],late[1][...],NT)+dot(dv_all[...],late[2][...],NT)
+            flag=jnp.where(flag_ref[0]==1,1.0,0.0)
+            dec_ref[...]=memory_grad*flag
+            enc_ref[...]=memory_grad*(1.0-flag)
+        for copy in copies: copy.wait()
+
+def sub_layer_back(q,k,v,g,ctx,lse,limit,flag,causal,normed,source,out_grad,gain,late,depth,collective_id,block=256,width=64):
+    rows,d=q.shape; keys=k.shape[0]
+    pairs=d//128; per=128//width
+    each=d//(8*depth)
+    bf=jnp.bfloat16; f32=jnp.float32
+    spec=lambda n: pl.BlockSpec((n,128),lambda i,a,b:(0,i))
+    once=lambda shape: pl.BlockSpec(shape,lambda i,a,b:(0,0),pipeline_mode=pl.Buffered(1))
+    keep=lambda shape: pl.BlockSpec(shape,lambda i,a,b:(0,0))
     any_=pl.BlockSpec(memory_space=pl.ANY)
-    spec=lambda n: pl.BlockSpec((n,128),lambda i,lim:(0,i))
-    outs=pl.pallas_call(
-        functools.partial(bwd_kernel,causal,block,width,count,depth),
-        grid_spec=pltpu.PrefetchScalarGridSpec(
-            num_scalar_prefetch=1, grid=(pairs,),
-            in_specs=[spec(rows),spec(keys),spec(keys),spec(rows),spec(rows),pl.BlockSpec((1,per,rows),lambda i,lim:(i,0,0))]+[any_]*count,
-            out_specs=[spec(rows),spec(keys),spec(keys)]+[pl.BlockSpec(k[:2],lambda i,lim:(0,0)) for k in kinds],
-            scratch_shapes=[pltpu.VMEM((keys,128),jnp.float32)]*2+(reduce_scratch(kinds,depth) if count else [])),
-        out_shape=[jax.ShapeDtypeStruct((rows,d),jnp.bfloat16),jax.ShapeDtypeStruct((keys,d),jnp.bfloat16),jax.ShapeDtypeStruct((keys,d),jnp.bfloat16)]
-          +[jax.ShapeDtypeStruct(k[:2],jnp.float32) for k in kinds],
-        compiler_params=pltpu.CompilerParams(vmem_limit_bytes=56*MIB,collective_id=collective_id,has_side_effects=count>0),
-        cost_estimate=pl.CostEstimate(flops=10*rows*keys*d//(2 if causal else 1),bytes_accessed=8*rows*d*2,transcendentals=rows*keys*16//(2 if causal else 1)),
-        name="attend_causal_back" if causal else "attend_text_back",
-    )(limit,q,k,v,g,ctx,lse,*parts)
-    return outs[0],outs[1],outs[2],outs[3:]
+    shape=lambda n,t: jax.ShapeDtypeStruct((n,d),t)
+    in_specs=[spec(rows),spec(keys),spec(keys),spec(rows),spec(rows),pl.BlockSpec((1,per,rows),lambda i,a,b:(i,0,0))]
+    in_specs+=[once((rows,d)),once(source.shape),once((rows,d)),spec(rows),once(gain.shape)]+[any_]*len(late)
+    out_specs=[any_]; out_shape=[shape(rows,f32)]
+    scratch=[pltpu.VMEM(a.shape,a.dtype) for a in late]+[DMA((len(late),))]
+    scratch+=[pltpu.VMEM((d,rows),bf),pltpu.VMEM((8,128) if causal else (d,keys),bf),pltpu.VMEM((d,rows),bf)]
+    scratch+=[pltpu.VMEM((n,d),bf) for n in (rows,keys,keys)]+[pltpu.VMEM((keys,128),f32)]*2
+    if not causal:
+        out_specs+=[any_,any_,keep((keys,d)),keep((keys,d))]
+        out_shape+=[shape(rows,bf),shape(rows,bf),shape(keys,f32),shape(keys,f32)]
+        scratch+=[pltpu.VMEM((rows,d),bf)]*2
+    out_specs+=[keep((8,d))]+[keep((each,d))]*4
+    out_shape+=[shape(8,f32)]+[shape(each,f32)]*4
+    scratch+=stream_scratch(each,256,depth)*2
+    return pl.pallas_call(
+        functools.partial(sub_layer_kernel,causal,block,width,pairs,depth),
+        grid_spec=pltpu.PrefetchScalarGridSpec(num_scalar_prefetch=2,grid=(pairs,),in_specs=in_specs,out_specs=out_specs,scratch_shapes=scratch),
+        out_shape=out_shape,
+        compiler_params=pltpu.CompilerParams(vmem_limit_bytes=62*MIB,collective_id=collective_id,has_side_effects=True),
+        cost_estimate=pl.CostEstimate(flops=20*rows*keys*d,bytes_accessed=20*rows*d*2,transcendentals=rows*keys*16),
+        name="self_back" if causal else "cross_back",
+    )(limit,flag,q,k,v,g,ctx,lse,normed,source,ctx,out_grad,gain,*late)
 
 MESH=pl.DeviceIdType.MESH
 DMA=pltpu.SemaphoreType.DMA
@@ -371,6 +472,91 @@
         name="reduce_rows",
     )(*parts)
 
+SLOTS=4
+
+def stream_scratch(rows,cols,depth):
+    vmem=lambda *lead: pltpu.VMEM(lead+(rows,cols),jnp.bfloat16)
+    return [vmem(2,2,2,depth,2),vmem(SLOTS,2,2,depth),vmem(SLOTS,2,2,depth),vmem(SLOTS,2,depth),vmem(SLOTS,depth),vmem(SLOTS,depth-1),
+      DMA((SLOTS,)),DMA((SLOTS,)),DMA((SLOTS,2)),DMA((SLOTS,2)),DMA((SLOTS,depth-1)),DMA((SLOTS,depth-1))]
+
+def stream_plan(count,parity,store,scratch,depth):
+    made,r0,held,r1,r2,r3,c_send,c_recv,a_send,a_recv,z_send,z_recv=scratch
+    dp,fs,z,c=place()
+    hi,lo=dp//2,dp%2
+    def slot(i): return lax.rem(i,SLOTS)
+    def core(i):
+        s=slot(i)
+        return pltpu.make_async_remote_copy(made.at[lax.rem(i,2),:,:,:,1-c],r0.at[s],c_send.at[s],c_recv.at[s],(dp,z*2+1-c),MESH)
+    def first(i,odd):
+        s=slot(i)
+        src=held.at[s,1-hi] if odd else held.at[s,:,1-lo]
+        return pltpu.make_async_remote_copy(src,r1.at[s],a_send.at[s,0],a_recv.at[s,0],(turned(dp,2 if odd else 1),fs),MESH)
+    def second(i,odd):
+        s=slot(i)
+        src=held.at[s,hi,1-lo] if odd else held.at[s,1-hi,lo]
+        return pltpu.make_async_remote_copy(src,r2.at[s],a_send.at[s,1],a_recv.at[s,1],(turned(dp,1 if odd else 2),fs),MESH)
+    def line(i,k):
+        s=slot(i)
+        return pltpu.make_async_remote_copy(held.at[s,hi,lo,lax.rem(z+k,depth)],r3.at[s,k-1],z_send.at[s,k-1],z_recv.at[s,k-1],(dp,lax.rem(z+k,depth)*2+c),MESH)
+    def by_parity(i,run):
+        p=parity(i)
+        if isinstance(p,int): run(p)
+        else:
+            for odd in (0,1):
+                @pl.when(p==odd)
+                def _(): run(odd)
+    def step0(i):
+        s=slot(i); m=lax.rem(i,2)
+        core(i).wait()
+        def add(n,_):
+            a,k=n//depth,n%depth
+            held[s,a//2,a%2,k]=made[m,a//2,a%2,k,c]+r0[s,a//2,a%2,k]
+            return 0
+        lax.fori_loop(0,4*depth,add,0)
+        by_parity(i,lambda odd: first(i,odd).start())
+    def step1(i):
+        s=slot(i)
+        first(i,0).wait_recv()
+        def run(odd):
+            def add(n,_):
+                a,k=n//depth,n%depth
+                if odd: held[s,hi,a,k]=held[s,hi,a,k]+r1[s,a,k]
+                else: held[s,a,lo,k]=held[s,a,lo,k]+r1[s,a,k]
+                return 0
+            lax.fori_loop(0,2*depth,add,0)
+            second(i,odd).start()
+        by_parity(i,run)
+    def step2(i):
+        s=slot(i)
+        second(i,0).wait_recv()
+        def add(k,_):
+            held[s,hi,lo,k]=held[s,hi,lo,k]+r2[s,k]
+            return 0
+        lax.fori_loop(0,depth,add,0)
+        for k in range(1,depth): line(i,k).start()
+    def step3(i):
+        s=slot(i)
+        total=held[s,hi,lo,z].astype(jnp.float32)
+        for k in range(1,depth):
+            line(i,k).wait_recv()
+            total=total+r3[s,k-1].astype(jnp.float32)
+        store(i,total)
+        first(i,0).wait_send(); second(i,0).wait_send()
+        for k in range(1,depth): line(i,k).wait_send()
+    stages=((5,step3),(4,step2),(3,step1),(2,step0),(1,lambda i: core(i).start()))
+    def tick(j):
+        for lag,step in stages:
+            if isinstance(j,int):
+                if 0<=j-lag<count: step(jnp.int32(j-lag))
+            else:
+                @pl.when(j>=lag)
+                def _(): step(j-lag)
+    return tick,[functools.partial(tick,count+n) for n in range(5)]
+
+def write_made(made,i,col,value):
+    shape=made.shape[1:6]+value.shape[1:]
+    made[lax.rem(i,2),:,:,:,:,:,col:col+value.shape[1]]=value.reshape(shape)
+
 EPSILON=1e-05
 def normal(tensor):
     centre=tensor-jnp.mean(tensor,axis=-1,keepdims=True)
@@ -382,15 +568,24 @@
     scaled=grad*gain
     return inverse*(scaled-jnp.mean(scaled,axis=-1,keepdims=True)-hat*jnp.mean(scaled*hat,axis=-1,keepdims=True))
 
-def ffn_kernel(strip, length_ref, after_ref, cot_ref, w1_ref, w2_ref, b1_ref, vec_ref,
-               mixed_ref, grad_ref, dw1_ref, dw2_ref, db1_ref, dvec_ref, n3, n3t, gf, branch, gn):
+def ffn_kernel(strip, steps, depth, length_ref, after_ref, cot_ref, w1_ref, w2_ref, b1_ref, vec_ref, wo_ref,
+               mixed_ref, grad_ref, low_ref, ctx_ref, dw1_ref, dw2_ref, db1_ref, dvec_ref, n3, n3t, gf, branch, gn, wo, sem, *refs):
     j=pl.program_id(0)
-    rows=after_ref.shape[0]
+    rows,d=after_ref.shape
     gain,shift,b2=vec_ref[0:1,:],vec_ref[1:2,:],vec_ref[2:3,:]
     def live(r):
         return (r*strip+lax.broadcasted_iota(jnp.int32,(strip,1),0)<length_ref[0]).astype(jnp.float32)
+    if depth:
+        half=len(refs)//2
+        wide=w1_ref.shape[1]
+        def store1(i,total): dw1_ref[:,pl.ds(pl.multiple_of(i*wide,128),wide)]=total
+        def store2(i,total): dw2_ref[i]=total
+        tick1,rest1=stream_plan(steps,lambda i: 0,store1,refs[:half],depth)
+        tick2,rest2=stream_plan(steps,lambda i: 1,store2,refs[half:],depth)
     @pl.when(j==0)
     def _():
+        if depth: greet(depth)
+        pltpu.make_async_copy(wo_ref,wo,sem.at[2]).start()
         def one(r,total):
             sl=pl.ds(r*strip,strip)
             hat,_=normal(after_ref[sl,:])
@@ -398,58 +593,90 @@
             top=(cot_ref[sl,:].astype(jnp.float32)*live(r)).astype(jnp.bfloat16)
             gf[sl,:]=top
             return total+jnp.sum(top.astype(jnp.float32),axis=0,keepdims=True)
-        dvec_ref[2:3,:]=lax.fori_loop(0,rows//strip,one,jnp.zeros((1,after_ref.shape[1]),jnp.float32))
+        dvec_ref[...]=jnp.zeros_like(dvec_ref)
+        dvec_ref[2:3,:]=lax.fori_loop(0,rows//strip,one,jnp.zeros((1,d),jnp.float32))
         n3t[...]=jnp.transpose(n3[...])
         branch[...]=jnp.zeros_like(branch); gn[...]=jnp.zeros_like(gn)
-    w1=w1_ref[...]; w2=w2_ref[...]
+    if depth:
+        tick1(j); tick2(j)
+    w1=w1_ref[...]; w2=w2_ref[...].reshape(w1.shape[1],d)
     pre=dot(n3[...],w1)+b1_ref[...]
     back=dot(gf[...],w2,NT).astype(jnp.bfloat16).astype(jnp.float32)
     root=0.7978845608028654
     square=pre*pre
     t=jnp.tanh(root*pre*(1.0+0.044715*square))
-    half=0.5*(1.0+t)
-    hidden=(pre*half).astype(jnp.bfloat16)
-    slope=half+0.5*pre*(1.0-t*t)*(root*(1.0+3*0.044715*square))
+    half_t=0.5*(1.0+t)
+    hidden=(pre*half_t).astype(jnp.bfloat16)
+    slope=half_t+0.5*pre*(1.0-t*t)*(root*(1.0+3*0.044715*square))
     g_pre=(back*slope).astype(jnp.bfloat16)
     db1_ref[...]=jnp.sum(g_pre.astype(jnp.float32),axis=0,keepdims=True)
     branch[...]+=dot(hidden,w2)
-    dw2_ref[...]=dot(hidden,gf[...],TN).astype(jnp.bfloat16)
-    dw1_ref[...]=dot(n3t[...],g_pre).astype(jnp.bfloat16)
+    dw2=dot(hidden,gf[...],TN).astype(jnp.bfloat16)
+    dw1=dot(n3t[...],g_pre).astype(jnp.bfloat16)
+    if depth:
+        write_made(refs[0],j,0,dw1)
+        write_made(refs[half],j,0,dw2)
+    else:
+        dw1_ref[...]=dw1
+        dw2_ref[...]=dw2.reshape(dw2_ref.shape)
     gn[...]+=dot(g_pre,w1,NT)
-    @pl.when(j==pl.num_programs(0)-1)
+    @pl.when(j==steps-1)
     def _():
-        def one(r,totals):
+        def one(r):
             sl=pl.ds(r*strip,strip)
             valid=live(r)
             after=after_ref[sl,:]
-            mixed_ref[sl,:]=((after+(branch[sl,:]+b2))*valid).astype(jnp.bfloat16)
+            n3[sl,:]=((after+(branch[sl,:]+b2))*valid).astype(jnp.bfloat16)
             hat,inverse=normal(after)
             grad=gn[sl,:]
-            grad_ref[sl,:]=cot_ref[sl,:].astype(jnp.float32)*valid+pull_norm(hat,inverse,gain,grad)
-            return totals[0]+jnp.sum(grad*hat,axis=0,keepdims=True),totals[1]+jnp.sum(grad,axis=0,keepdims=True)
-        zero=jnp.zeros((1,after_ref.shape[1]),jnp.float32)
-        dg,ds=lax.fori_loop(0,rows//strip,one,(zero,zero))
-        dvec_ref[0:1,:]=dg
-        dvec_ref[1:2,:]=ds
-
-def feed_forward(after,cot,length,w1,w2,b1,vec,block=512,strip=128):
+            dvec_ref[0:1,:]+=jnp.sum(grad*hat,axis=0,keepdims=True)
+            dvec_ref[1:2,:]+=jnp.sum(grad,axis=0,keepdims=True)
+            grad=cot_ref[sl,:].astype(jnp.float32)*valid+pull_norm(hat,inverse,gain,grad)
+            gn[sl,:]=grad
+            gf[sl,:]=grad.astype(jnp.bfloat16)
+            n3t[sl,:]=dot(gf[sl,:],wo[...],NT).astype(jnp.bfloat16)
+        late=list(zip(rest1,rest2)) if depth else []
+        pltpu.make_async_copy(wo_ref,wo,sem.at[2]).wait()
+        for r in range(rows//strip):
+            if r%2==0 and r//2<len(late):
+                late[r//2][0](); late[r//2][1]()
+            one(r)
+        copies=[pltpu.make_async_copy(a,b,sem.at[n]) for n,(a,b) in enumerate(((n3,mixed_ref),(gn,grad_ref),(gf,low_ref),(n3t,ctx_ref)))]
+        for copy in copies: copy.start()
+        for a,b in late[rows//strip//2:]:
+            a(); b()
+        for copy in copies: copy.wait()
+
+def feed_forward(after,cot,length,w1,w2,b1,vec,wo,block=512,strip=128,depth=0,collective_id=None):
     rows,d=after.shape; ff=w1.shape[1]
+    steps=ff//block
     once=lambda shape: pl.BlockSpec(shape,lambda j,n:(0,0),pipeline_mode=pl.Buffered(1))
-    keep=lambda shape: pl.BlockSpec(shape,lambda j,n:(0,0))
-    wide=pl.BlockSpec((d,block),lambda j,n:(0,j)); tall=pl.BlockSpec((block,d),lambda j,n:(j,0)); line=pl.BlockSpec((1,block),lambda j,n:(0,j))
+    keep=lambda shape: pl.BlockSpec(shape,lambda j,n:(0,)*len(shape))
+    any_=pl.BlockSpec(memory_space=pl.ANY)
+    wide=pl.BlockSpec((d,block),lambda j,n:(0,j)); line=pl.BlockSpec((1,block),lambda j,n:(0,j))
+    tall=pl.BlockSpec((w2.shape[0],block//w2.shape[0],d),lambda j,n:(0,j,0))
     bf=jnp.bfloat16; f32=jnp.float32
+    scratch=[pltpu.VMEM((rows,d),bf),pltpu.VMEM((d,rows),bf),pltpu.VMEM((rows,d),bf),pltpu.VMEM((rows,d),f32),pltpu.VMEM((rows,d),f32),pltpu.VMEM((d,d),bf),DMA((4,))]
+    if depth:
+        each=d//(8*depth); part=block//(8*depth)
+        grad_specs=[keep((each,ff)),keep((steps,part,d))]
+        grad_shapes=[jax.ShapeDtypeStruct((each,ff),f32),jax.ShapeDtypeStruct((steps,part,d),f32)]
+        scratch+=stream_scratch(each,block,depth)+stream_scratch(part,d,depth)
+    else:
+        grad_specs=[wide,tall]
+        grad_shapes=[jax.ShapeDtypeStruct(w1.shape,bf),jax.ShapeDtypeStruct(w2.shape,bf)]
     return pl.pallas_call(
-        functools.partial(ffn_kernel,strip),
+        functools.partial(ffn_kernel,strip,steps,depth),
         grid_spec=pltpu.PrefetchScalarGridSpec(
-            num_scalar_prefetch=1,grid=(ff//block,),
-            in_specs=[once((rows,d)),once((rows,d)),wide,tall,line,once(vec.shape)],
-            out_specs=[keep((rows,d)),keep((rows,d)),wide,tall,line,keep((8,d))],
-            scratch_shapes=[pltpu.VMEM((rows,d),bf),pltpu.VMEM((d,rows),bf),pltpu.VMEM((rows,d),bf),pltpu.VMEM((rows,d),f32),pltpu.VMEM((rows,d),f32)]),
-        out_shape=[jax.ShapeDtypeStruct((rows,d),bf),jax.ShapeDtypeStruct((rows,d),f32),jax.ShapeDtypeStruct((d,ff),bf),jax.ShapeDtypeStruct((ff,d),bf),jax.ShapeDtypeStruct((1,ff),f32),jax.ShapeDtypeStruct((8,d),f32)],
-        compiler_params=pltpu.CompilerParams(vmem_limit_bytes=60*MIB),
+            num_scalar_prefetch=1,grid=(steps,),
+            in_specs=[once((rows,d)),once((rows,d)),wide,tall,line,once(vec.shape),any_],
+            out_specs=[any_]*4+grad_specs+[line,keep((8,d))],
+            scratch_shapes=scratch),
+        out_shape=[jax.ShapeDtypeStruct((rows,d),bf),jax.ShapeDtypeStruct((rows,d),f32)]+[jax.ShapeDtypeStruct((rows,d),bf)]*2+grad_shapes+[jax.ShapeDtypeStruct((1,ff),f32),jax.ShapeDtypeStruct((8,d),f32)],
+        compiler_params=pltpu.CompilerParams(vmem_limit_bytes=62*MIB,collective_id=collective_id,has_side_effects=depth>0),
         cost_estimate=pl.CostEstimate(flops=12*rows*d*ff,bytes_accessed=4*d*ff*2+rows*d*12,transcendentals=rows*ff),
         name="feed_forward",
-    )(length,after,cot,w1,w2,b1,vec)
+    )(length,after,cot,w1,w2,b1,vec,wo)
 
 AXES=("dp","fsdp")
 
@@ -488,6 +715,11 @@
     ln1_gain, ln1_shift, self_wq, self_bq, self_wk, self_wv, self_bv, self_wo, self_bo,
     ln2_gain, ln2_shift, cross_wq, cross_bq, cross_wk, cross_wv, cross_bv, cross_wo, cross_bo,
     ln3_gain, ln3_shift, ffn_w1, ffn_b1, ffn_w2, ffn_b2):
+    steps=8
+    each=1024//devices
+    if depth:
+        part=4*each//steps
+        ffn_w1=ffn_w1.reshape(each,devices,steps,part).transpose(0,2,1,3).reshape(each,4096)
     w1=lax.all_gather(ffn_w1,AXES,axis=0,tiled=True)
     w2=lax.all_gather(ffn_w2,AXES,axis=0,tiled=True)
     small=[ln1_gain,ln1_shift,self_bq,self_bv,self_bo,ln2_gain,ln2_shift,cross_bq,cross_bv,cross_bo,ln3_gain,ln3_shift,ffn_b2]
@@ -510,33 +742,43 @@
     cq=low(dot(n2,cwq)+cbq); ck=low(dot(memory,cwk)); cv=low(dot(memory,cwv)+cbv)
     cctx,clse,_=flash_fwd(cq,ck,cv,text_len,False)
     after_cross=after_self+(dot(cctx,cwo)+cbo)
-    mixed,g_cross,dw1,dw2,db1,dvec=feed_forward(after_cross,cotangent[0],unit_len,w1,w2,b1,jnp.concatenate([vectors[10:13],jnp.zeros((5,1024),jnp.float32)]))
-    dw1,dw2=reduce_all([dw1,dw2])
-    gc=low(g_cross)
-    dcwo=low(dot(cctx,gc,TN))
-    gcq,gck,gcv,_=flash_bwd(cq,ck,cv,low(dot(gc,cwo,NT)),cctx,clse,text_len,False)
-    dcwq=low(dot(n2,gcq,TN)); dcwk=low(dot(memory,gck,TN)); dcwv=low(dot(memory,gcv,TN))
-    g_memory=dot(gck,cwk,NT)+dot(gcv,cwv,NT)
-    pulled,dg2,ds2=layer_norm_back(after_self,g2,dot(gcq,cwq,NT))
-    g_self=g_cross+pulled
-    gs=low(g_self)
-    dwo=low(dot(ctx,gs,TN))
-    early=[dcwo,dcwq,dcwk,dcwv,dwo]
-    if depth: gq,gk,gv,early=flash_bwd(q,k,v,low(dot(gs,wo,NT)),ctx,lse,text_len,True,moves=early,depth=depth,collective_id=3)
-    else: gq,gk,gv,_=flash_bwd(q,k,v,low(dot(gs,wo,NT)),ctx,lse,text_len,True)
-    dwq=low(dot(n1,gq,TN)); dwk=low(dot(n1,gk,TN)); dwv=low(dot(n1,gv,TN))
-    pulled,dg1,ds1=layer_norm_back(units,g1,dot(gq,wq,NT)+dot(gk,wk,NT)+dot(gv,wv,NT))
-    g_units=g_self+pulled
-    is_dec=(task_flag[0]==1).astype(jnp.float32)
-    grads=pack_grads([dg1,ds1,columns(gq),columns(gv),columns(gs),dg2,ds2,columns(gcq),columns(gcv),columns(gc),dvec[0],dvec[1],dvec[2]],db1[0],devices)
-    if depth: dwq,dwk,dwv,grads=reduce_rows([dwq,dwk,dwv,grads],depth,4)
-    else: dwq,dwk,dwv,grads,*early=reduce_all([dwq,dwk,dwv,grads]+early)
-    dcwo,dcwq,dcwk,dcwv,dwo=early
-    each=1024//devices
+    last=jnp.concatenate([vectors[10:13],jnp.zeros((5,1024),jnp.float32)])
+    if depth:
+        b1=b1.reshape(devices,steps,part).transpose(1,0,2).reshape(1,4096)
+        mixed,g_cross,gc,g_cctx,dw1,dw2,db1,dvec=feed_forward(after_cross,cotangent[0],unit_len,w1,w2.reshape(devices,4*each,1024),b1,last,cwo,depth=depth,collective_id=3)
+        dw1=dw1.reshape(each,steps,devices,part).transpose(0,2,1,3).reshape(each,4096)
+        dw2=dw2.reshape(4*each,1024)
+        db1=db1.reshape(steps,devices,part).transpose(1,0,2)
+    else:
+        mixed,g_cross,gc,g_cctx,dw1,dw2,db1,dvec=feed_forward(after_cross,cotangent[0],unit_len,w1,w2[None],b1,last,cwo)
+        dw1,dw2=reduce_all([dw1,dw2[0]])
+    gain1,gain2=vectors[0:1],vectors[5:6]
+    if depth:
+        g_self,gs,g_ctx,g_dec,g_enc,csums,dcwq,dcwk,dcwv,dcwo=sub_layer_back(
+            cq,ck,cv,g_cctx,cctx,clse,text_len,task_flag,False,n2,memory,gc,gain2,[cwq,cwk,cwv,wo,after_self,g_cross],depth,4)
+        g_units,sums,dwq,dwk,dwv,dwo=sub_layer_back(
+            q,k,v,g_ctx,ctx,lse,text_len,task_flag,True,n1,memory,gs,gain1,[wq,wk,wv,unit_states[0],g_self],depth,5)
+        small_grads=[sums[3],sums[4],sums[0],sums[1],sums[2],csums[3],csums[4],csums[0],csums[1],csums[2],dvec[0],dvec[1],dvec[2]]
+    else:
+        gcq,gck,gcv=flash_bwd(cq,ck,cv,g_cctx,cctx,clse,text_len,False)
+        dcwq,dcwk,dcwv,dcwo=reduce_all([low(dot(n2,gcq,TN)),low(dot(memory,gck,TN)),low(dot(memory,gcv,TN)),low(dot(cctx,gc,TN))])
+        g_memory=dot(gck,cwk,NT)+dot(gcv,cwv,NT)
+        pulled,dg2,ds2=layer_norm_back(after_self,g2,dot(gcq,cwq,NT))
+        g_self=g_cross+pulled
+        gs=low(g_self)
+        gq,gk,gv=flash_bwd(q,k,v,low(dot(gs,wo,NT)),ctx,lse,text_len,True)
+        dwq,dwk,dwv,dwo=reduce_all([low(dot(n1,gq,TN)),low(dot(n1,gk,TN)),low(dot(n1,gv,TN)),low(dot(ctx,gs,TN))])
+        pulled,dg1,ds1=layer_norm_back(units,g1,dot(gq,wq,NT)+dot(gk,wk,NT)+dot(gv,wv,NT))
+        g_units=g_self+pulled
+        is_dec=(task_flag[0]==1).astype(jnp.float32)
+        g_dec,g_enc=g_memory*is_dec,g_memory*(1.0-is_dec)
+        small_grads=[dg1,ds1,columns(gq),columns(gv),columns(gs),dg2,ds2,columns(gcq),columns(gcv),columns(gc),dvec[0],dvec[1],dvec[2]]
+    grads=pack_grads(small_grads,db1,devices)
+    grads,=reduce_rows([grads],depth,6) if depth else reduce_all([grads])
     grads=grads.reshape(1024)
     ng=[grads[i*each:(i+1)*each] for i in range(13)]
     db1=grads[13*each:17*each]
-    return (mixed[None],g_units[None],(g_memory*is_dec)[None],(g_memory*(1.0-is_dec))[None],
+    return (mixed[None],g_units[None],g_dec[None],g_enc[None],
         ng[0],ng[1],dwq,ng[2],dwk,dwv,ng[3],dwo,ng[4],ng[5],ng[6],dcwq,ng[7],dcwk,dcwv,ng[8],dcwo,ng[9],ng[10],ng[11],dw1,db1,dw2,ng[12])
 
 def solution(mesh):

time: 617 us -> 526 us (0.85)
  matrix products: 87.2 us -> 21.8 us
  waiting for transfers between devices: 43.8 us -> 2.7 us
  Pallas kernels: 419 us -> 436 us
  local copies, waits for them, and re-layouts: 22 us -> 37.3 us
  other arithmetic: 18.8 us -> 6.79 us
    pallas_call x3, Pallas kernels: 196 us -> 269 us  [the longest x2 150 us: sub_layer_back(): pl.pallas_call(functools.partial(sub_layer_kernel, causal, block, width,...]
    dot_general x24 -> x8, matrix products: 87.2 us -> 21.8 us  [dot(): return lax.dot_general(a, b, dims, preferred_element_type=jnp.float32)]
    pallas_call x1, Pallas kernels: 72.4 us -> 13.2 us  [reduce_rows(): pl.pallas_call(functools.partial(last_kernel, count, depth), in_specs=[pl...]
    reduce_scatter x2 -> x0, waiting for transfers between devices: 32.8 us -> none  [reduce_all(): lax.psum_scatter(p, AXES, scatter_dimension=0, tiled=True)]
    unnamed x139 -> x108, local copies, waits for them, and re-layouts: 11.5 us -> 24.4 us
    reduce_sum x5 -> x0, other arithmetic: 8.28 us -> none  [columns(): return jnp.sum(tensor.astype(jnp.float32), axis=0)]
    all_gather x1, waiting for transfers between devices: 9.08 us -> 1.98 us  [shards(): w2 = lax.all_gather(ffn_w2, AXES, axis=0, tiled=True)]
  transfers between devices with their start and end apart: 4 -> 2, of which waited for: 2 -> 1; matrix products, arithmetic and copies ran while one was open for 19% -> 6% of each run, Pallas kernels for 57% -> 29%
where the time goes in v3:
time: 526 us; the launch traced here: 521 us
  Pallas kernels  436 us (83%)
  local copies, waits for them, and re-layouts  37.3 us (7%)
  matrix products  21.8 us (4%)
  between operations  16.9 us (3%)
  other arithmetic  6.79 us (1%)
    pallas_call x2, Pallas kernels, sub_layer_back(): pl.pallas_call(functools.partial(sub_layer_kernel, causal, block, width,...  150 us
    pallas_call x1, Pallas kernels, feed_forward(): pl.pallas_call(functools.partial(ffn_kernel, strip, steps, depth), grid_s...  119 us
    pallas_call x2, Pallas kernels, flash_fwd(): pl.pallas_call(functools.partial(fwd_kernel, causal, block, width, count,...  95.5 us
    pallas_call x1, Pallas kernels, gather_first(): pl.pallas_call(functools.partial(first_kernel, count, lines, depth), in_s...  57.6 us
    unnamed x108, local copies, waits for them, and re-layouts  24.4 us
    dot_general x8, matrix products, dot(): return lax.dot_general(a, b, dims, preferred_element_type=jnp.float32)  21.8 us
    pallas_call x1, Pallas kernels, reduce_rows(): pl.pallas_call(functools.partial(last_kernel, count, depth), in_specs=[pl...  13.2 us
  transfers between devices with their start and end apart: 2, of which 1 were waited for; matrix products, arithmetic and copies ran while one was open for 6% of the time, Pallas kernels for 29%

profile of v3, /device:TPU:0, one launch (start us, length us, event | category | flops | bytes accessed | tf_op | source)
XLA Modules:
  0.0 521.2 jit_solution(14941656500385477896)
XLA Ops:
  7.3 2.4 copy.66
  9.7 1.4 copy.67
  14.2 57.6 %gather_first.1 = (bf16[4,4,2,32,1024]{4,3,2,1,0:T(8,128)(2,1)}, bf16[4,4,2,32,1024]{4,3,2,1,0:T(8,128)(2,1)}, bf16[4,4,2,32,1024]{4,3,2,1,0:T(8,128)(2,1)}, f32[16,1024]{1,0:T(8,128)}, f32[1,4096]{1,0:T(1,128)}) custom-call(bf16[32,1024]{1,0:T(8,128)(2,1)} %refs_0_.2, bf16[32,1024]{1,0:T(8,128)(2,1)} %refs_1_.2, bf16[32,1024]{1,0:T(8,128)(2,1)} %refs_2_.2, ...), custom_call_target="tpu_custom_call" | custom-call | tf_op jit(solution)/shard_map/gather_first/pallas_call | solution.py:442
  72.3 1.4 reduce.6
  77.9 3.7 convolution_convert_fusion.k_ref.refs_1_
  81.7 3.7 add_convert_fusion.2.v_ref.refs_2_
  85.5 3.7 add_convert_fusion.3.q_ref.refs_0_
  89.2 82.1 %attend_causal.1 = (bf16[1024,1024]{1,0:T(8,128)(2,1)S(1)}, f32[8,2,1024]{2,1,0:T(2,128)S(1)}, bf16[4,4,2,32,1024]{4,3,2,1,0:T(8,128)(2,1)S(1)}, bf16[4,4,2,32,1...) custom-call(s32[1]{0:T(128)S(6)} %copy.94.lim_ref, ...), custom_call_target="tpu_custom_call" | custom-call | flops 2147483648 | bytes 8388608 | tf_op jit(solution)/shard_map/attend_causal/pallas_call | solution.py:82
  171.4 2.5 fusion.14
  175.9 1.9 copy-done.20
  181.6 2.3 add_convert_fusion.q_ref.refs_0_
  183.9 13.4 %attend_text.1 = (bf16[1024,1024]{1,0:T(8,128)(2,1)S(1)}, f32[8,2,1024]{2,1,0:T(2,128)S(1)}) custom-call(s32[1]{0:T(128)S(6)} %copy.94.lim_ref, bf16[1024,1024]{1,0:T(8,128)(2,1)S(1)} %add_convert_fusion.q_ref.refs_0_, bf16[256,1024]{1,0:T(8,128)(2,1)S(1)} %convolution_convert_fusion.1.k_ref.refs_1_, bf16[256,1024]{1,0:T(8,128)(2,1)S(1)} %fusion.7.v_ref.refs_2_), custom_call_target="tpu_custom_call" | custom-call | flops 1073741824 | bytes 8388608 | tf_op jit(solution)/shard_map/attend_text/pallas_call | solution.py:82
  197.4 2.2 fusion.5.refs_6_
  199.6 4.4 add_add_fusion.after_ref
  203.9 2.0 all-gather.5.cloned.1.call-done
  205.9 119.2 %feed_forward.1 = (bf16[1024,1024]{1,0:T(8,128)(2,1)}, f32[1024,1024]{1,0:T(8,128)}, bf16[1024,1024]{1,0:T(8,128)(2,1)}, bf16[1024,1024]{1,0:T(8,128)(2,1)}, f32...) custom-call(s32[1]{0:T(128)S(6)} %copy.93.length_ref, ...), custom_call_target="tpu_custom_call" | custom-call | flops 51539607552 | bytes 46137344 | tf_op jit(solution)/shard_map/feed_forward/pallas_call | solution.py:668
  325.1 67.1 %cross_back.1 = (f32[1024,1024]{1,0:T(8,128)}, bf16[1024,1024]{1,0:T(8,128)(2,1)}, bf16[1024,1024]{1,0:T(8,128)(2,1)}, f32[256,1024]{1,0:T(8,128)}, f32[256,1024...) custom-call(s32[1]{0:T(128)S(6)} %copy.94.lim_ref, ...), custom_call_target="tpu_custom_call" | custom-call | flops 5368709120 | bytes 41943040 | tf_op jit(solution)/shard_map/cross_back/pallas_call | solution.py:257
  392.3 83.1 %self_back.1 = (f32[1024,1024]{1,0:T(8,128)}, f32[8,1024]{1,0:T(8,128)}, f32[32,1024]{1,0:T(8,128)}, f32[32,1024]{1,0:T(8,128)}, f32[32,1024]{1,0:T(8,128)}, /*index=5*/f32[32,1024]{1,0:T(8,128)}) custom-call(s32[1]{0:T(128)S(6)} %copy.94.lim_ref, s32[1]{0:T(128)S(6)} %copy.95.flag_ref, bf16[1024,1024]{1,0:T(8,128)(2,1)} %add_convert_fusion.3.q_ref.refs_0_, ...), custom_call_target="tpu_custom_call" | custom-call | flops 21474836480 | bytes 41943040 | tf_op jit(solution)/shard_map/self_back/pallas_call | solution.py:257
  479.2 13.2 %reduce_rows.1 = f32[8,128]{1,0:T(8,128)} custom-call(f32[2,2,4,2,8,128]{5,4,3,2,1,0:T(8,128)} %bitcast.105), custom_call_target="tpu_custom_call" | custom-call | tf_op jit(solution)/shard_map/reduce_rows/pallas_call | solution.py:465
  492.5 1.8 fusion.13
  496.1 1.6 copy.74
  497.7 3.0 copy.75
  500.7 3.2 copy.96
  503.9 2.1 copy.97
  (143 shorter events, 25.2 us)
Async XLA Ops:
  7.2 69.6 %copy-start.14 = (bf16[1,1024,1024]{2,1,0:T(8,128)(2,1)S(1)}, bf16[1,1024,1024]{2,1,0:T(8,128)(2,1)}, u32[]{:S(2)}) copy-start(bf16[1,1024,1024]{2,1,0:T(8,128)(2,1)} %param.31) | copy-start | bytes 6291460
  7.2 196.7 %all-gather.3.cloned.1.call-start = ((), (), s32[]{:S(2)}) async-start(), calls=%async_computation | async-start | bytes 8650752 | tf_op jit(solution)/shard_map/all_gather | solution.py:723
  12.1 193.8 %all-gather.5.cloned.1.call-start = ((), (), s32[]{:S(2)}) async-start(), calls=%async_computation.1 | async-start | bytes 8650752 | tf_op jit(solution)/shard_map/all_gather | solution.py:724
  71.8 6.1 %copy-start.36 = (f32[16,1024]{1,0:T(8,128)S(1)}, f32[16,1024]{1,0:T(8,128)}, u32[]{:S(2)}) copy-start(f32[16,1024]{1,0:T(8,128)} %get-tuple-element.66) | copy-start | bytes 196612
  77.9 101.6 %copy-start.37 = (f32[1,1024]{1,0:T(1,128)}, f32[1,1024]{1,0:T(1,128)S(1)}, u32[]{:S(2)}) copy-start(f32[1,1024]{1,0:T(1,128)S(1)} %get-tuple-element.136.refs_10_) | copy-start | bytes 12292
  77.9 119.4 %copy-start.40 = (f32[1,1024]{1,0:T(1,128)}, f32[1,1024]{1,0:T(1,128)S(1)}, u32[]{:S(2)}) copy-start(f32[1,1024]{1,0:T(1,128)S(1)} %get-tuple-element.141.refs_10_) | copy-start | bytes 12292
  173.9 25.7 %copy-start.13 = (f32[1024,1024]{1,0:T(8,128)}, f32[1024,1024]{1,0:T(8,128)S(1)}, u32[]{:S(2)}) copy-start(f32[1024,1024]{1,0:T(8,128)S(1)} %get-tuple-element.156.refs_15_) | copy-start | bytes 12582916
  173.9 4.9 copy-start.21
  175.9 4.3 copy-start.18
  178.5 5.4 %copy-start.3 = (bf16[256,1024]{1,0:T(8,128)(2,1)}, bf16[256,1024]{1,0:T(8,128)(2,1)S(1)}, u32[]{:S(2)}) copy-start(bf16[256,1024]{1,0:T(8,128)(2,1)S(1)} %convolution_convert_fusion.1.k_ref.refs_1_) | copy-start | bytes 1572868
  179.5 4.4 copy-start.4
  183.9 15.6 %copy-start.2 = (bf16[1024,1024]{1,0:T(8,128)(2,1)}, bf16[1024,1024]{1,0:T(8,128)(2,1)S(1)}, u32[]{:S(2)}) copy-start(bf16[1024,1024]{1,0:T(8,128)(2,1)S(1)} %add_convert_fusion.q_ref.refs_0_) | copy-start | bytes 6291460
  183.9 13.4 %copy-start.15 = (bf16[1,1024,1024]{2,1,0:T(8,128)(2,1)S(1)}, bf16[1,1024,1024]{2,1,0:T(8,128)(2,1)}, u32[]{:S(2)}) copy-start(bf16[1,1024,1024]{2,1,0:T(8,128)(2,1)} %param.31) | copy-start | bytes 6291460
  183.9 15.6 %copy-start.45 = (bf16[4,4,2,32,1024]{4,3,2,1,0:T(8,128)(2,1)S(1)}, bf16[4,4,2,32,1024]{4,3,2,1,0:T(8,128)(2,1)}, u32[]{:S(2)}) copy-start(bf16[4,4,2,32,1024]{4,3,2,1,0:T(8,128)(2,1)} %get-tuple-element.76) | copy-start | bytes 6291460
  392.2 84.6 %copy-start.38 = (f32[8,1024]{1,0:T(8,128)S(1)}, f32[8,1024]{1,0:T(8,128)}, u32[]{:S(2)}) copy-start(f32[8,1024]{1,0:T(8,128)} %get-tuple-element.91) | copy-start | bytes 98308
  392.2 84.7 %copy-start.41 = (f32[8,1024]{1,0:T(8,128)S(1)}, f32[8,1024]{1,0:T(8,128)}, u32[]{:S(2)}) copy-start(f32[8,1024]{1,0:T(8,128)} %get-tuple-element.92) | copy-start | bytes 98308
  392.3 85.2 %copy-start.39 = (f32[1,4096]{1,0:T(1,128)S(1)}, f32[1,4096]{1,0:T(1,128)}, u32[]{:S(2)}) copy-start(f32[1,4096]{1,0:T(1,128)} %get-tuple-element.93) | copy-start | bytes 49156
  392.3 103.2 %copy-start.24 = (f32[32,4096]{1,0:T(8,128)S(1)}, f32[32,4096]{1,0:T(8,128)}, u32[]{:S(2)}) copy-start(f32[32,4096]{1,0:T(8,128)} %get-tuple-element.102) | copy-start | bytes 1572868
  506.1 4.0 copy-start.32
  506.1 4.6 copy-start.31
  506.1 5.3 %copy-start.30 = (f32[32,1024]{1,0:T(8,128)S(1)}, f32[32,1024]{1,0:T(8,128)}, u32[]{:S(2)}) copy-start(f32[32,1024]{1,0:T(8,128)} %get-tuple-element.202) | copy-start | bytes 393220
  506.1 5.9 %copy-start.29 = (f32[32,1024]{1,0:T(8,128)S(1)}, f32[32,1024]{1,0:T(8,128)}, u32[]{:S(2)}) copy-start(f32[32,1024]{1,0:T(8,128)} %get-tuple-element.203) | copy-start | bytes 393220
  506.1 6.6 %copy-start.28 = (f32[32,1024]{1,0:T(8,128)S(1)}, f32[32,1024]{1,0:T(8,128)}, u32[]{:S(2)}) copy-start(f32[32,1024]{1,0:T(8,128)} %get-tuple-element.205) | copy-start | bytes 393220
  506.1 7.2 %copy-start.27 = (f32[8,16,1024]{2,1,0:T(8,128)S(1)}, f32[8,16,1024]{2,1,0:T(8,128)}, u32[]{:S(2)}) copy-start(f32[8,16,1024]{2,1,0:T(8,128)} %get-tuple-element.103) | copy-start | bytes 1572868
  (24 other events, 69.6 us)
Sparse Core Ops, SparseCore 0:
  12.3 103.2 all-gather.2
  118.6 87.2 all-gather.4

commit v4 on v3

--- a/solution.py
+++ b/solution.py
@@ -93,7 +93,7 @@
     )(limit,q,k,v,*moves)
     return outs[0],outs[1],gather_result(outs[2:],moves)
 
-def back_of_pair(causal, block, width, lim_ref, q_ref, k_ref, v_ref, g_ref, ctx_ref, lse_ref, dq_ref, dk_acc, dv_acc):
+def back_of_pair(causal, block, width, lim_ref, q_ref, k_ref, v_ref, g_ref, ctx_ref, lse_ref, dq_ref, dk_acc, dv_acc, middle=None):
     rows=q_ref.shape[0]; keys=k_ref.shape[0]
     masks=head_masks(width)
     scale=jnp.bfloat16(width**-0.5)
@@ -131,6 +131,7 @@
             part=dot(ds,km[h][:kend],TN)
             dq=part if dq is None else dq+part
         dq_ref[sl,:]=dq.astype(jnp.bfloat16)
+        if middle and i==rows//block//2: middle()
 
 def bwd_kernel(causal, block, width, lim_ref, *refs):
     dq_ref,dk_ref,dv_ref,dk_acc,dv_acc=refs[6:]
@@ -159,14 +160,22 @@
     normed_ref,source_ref,whole_ref,out_ref,gain_ref=refs[:5]; refs=refs[5:]
     late_count=5 if causal else 6
     late_in=refs[:late_count]; refs=refs[late_count:]
+    carried=4 if causal else 2
+    before,starts=refs[:2],refs[2:2+carried]; refs=refs[2+carried:]
     if causal: grad_out,sums_ref=refs[:2]; refs=refs[2:]
     else: grad_out,low_out,ctx_out,dec_ref,enc_ref,sums_ref=refs[:6]; refs=refs[6:]
     results=refs[:4]; refs=refs[4:]
+    left=(None,None)
+    if not causal: left=refs[:2]; refs=refs[2:]
+    ends=refs[:carried]; refs=refs[carried:]
     late=refs[:late_count]; late_sem=refs[late_count]; refs=refs[late_count+1:]
-    normed_t,source_t,whole_t,dq_all,dk_all,dv_all,dk_acc,dv_acc=refs[:8]; refs=refs[8:]
+    normed_t,source_t,whole_t,dq_all,dk_all,dv_all,dk_acc,dv_acc,out_part=refs[:9]; refs=refs[9:]
     low_all,ctx_all=(None,None) if causal else refs[:2]
     streams=refs if causal else refs[2:]
-    half=len(streams)//2
+    half=STREAM
+    earlier=streams[2*half:]; streams=streams[:2*half]
+    count=pairs if causal else pairs-CROSS_LATE
+    before_late=CROSS_LATE if causal else FFN_LATE
     step=pl.program_id(0)
     rows=pair_refs[0].shape[0]
     def keep_pair(first):
@@ -174,28 +183,64 @@
             for n in range(2):
                 results[first+n][:,pl.ds(pl.multiple_of(i*128,128),128)]=total[:,n*128:(n+1)*128]
         return store
-    tick1,rest1=stream_plan(pairs,lambda i: 0,keep_pair(0),streams[:half],depth)
-    tick2,rest2=stream_plan(pairs,lambda i: 1,keep_pair(2),streams[half:],depth)
+    tick1,middle1=stream_plan(count,0,keep_pair(0),streams[:half],depth)
+    tick2,middle2=stream_plan(count,1,keep_pair(2),streams[half:],depth)
+    def store_earlier(w,total):
+        if causal:
+            at=pairs-before_late+w//2
+            for n in range(2): ends[w%2*2+n][:,at*128:(at+1)*128]=total[:,n*128:(n+1)*128]
+        elif w%2==0:
+            wide=total.shape[1]
+            at=ends[0].shape[1]//wide-before_late+w//2
+            ends[0][:,at*wide:(at+1)*wide]=total
+        else:
+            ends[1][ends[1].shape[0]-before_late+w//2]=total
+    begin,ticks,finish=(lambda: None),[],(lambda: None)
+    if before_late: begin,ticks,finish=reduce_plan([before[w%2].at[w//2] for w in range(2*before_late)],store_earlier,earlier,depth)
+    def leave(n):
+        m=(pairs-CROSS_LATE+n)%2
+        return [pltpu.make_async_copy(streams[half*h].at[m],left[h].at[n],late_sem.at[late_count+2*n+h]) for h in (0,1)]
     def late_copy(n): return pltpu.make_async_copy(late_in[n],late[n],late_sem.at[n])
     @pl.when(step==0)
     def _():
         greet(depth)
+        begin()
         for n in range(late_count): late_copy(n).start()
+        for a,b in zip(starts,ends): b[...]=a[...]
         normed_t[...]=jnp.transpose(normed_ref[...])
         whole_t[...]=jnp.transpose(whole_ref[...])
         if not causal: source_t[...]=jnp.transpose(source_ref[...])
     tick1(step); tick2(step)
+    for n in range(len(ticks)):
+        @pl.when(step==n+1)
+        def _(): ticks[n]()
     here=pl.ds(pl.multiple_of(step*128,128),128)
-    back_of_pair(causal,block,width,lim_ref,*pair_refs,dq_all.at[:,here],dk_acc,dv_acc)
-    dq=dq_all[:,here]; dk=dk_acc[...].astype(jnp.bfloat16); dv=dv_acc[...].astype(jnp.bfloat16); do=out_ref[...]
+    back_of_pair(causal,block,width,lim_ref,*pair_refs,dq_all.at[:,here],dk_acc,dv_acc,lambda: (middle1(step),middle2(step)))
+    dq=dq_all[:,here]; dk=dk_acc[...].astype(jnp.bfloat16); dv=dv_acc[...].astype(jnp.bfloat16)
     dk_all[:,here]=dk; dv_all[:,here]=dv
-    source=normed_t[...] if causal else source_t[...]
-    write_made(streams[0],step,0,dot(normed_t[...],dq).astype(jnp.bfloat16))
-    write_made(streams[0],step,128,dot(source,dk).astype(jnp.bfloat16))
-    write_made(streams[half],step,0,dot(source,dv).astype(jnp.bfloat16))
-    write_made(streams[half],step,128,dot(whole_t[...],do).astype(jnp.bfloat16))
-    for n,value in enumerate((dq,dv,do)):
-        sums_ref[n:n+1,here]=jnp.sum(value.astype(jnp.float32),axis=0,keepdims=True)
+    def add_sum(n,value): sums_ref[n:n+1,here]=jnp.sum(value.astype(jnp.float32),axis=0,keepdims=True)
+    add_sum(0,dq); add_sum(1,dv)
+    @pl.when(step%2==0)
+    def _():
+        out_part[...]=dot(whole_t[...],out_ref[...]).astype(jnp.bfloat16)
+        add_sum(2,out_ref[:,:128])
+        write_made(streams[half],step,128,out_part[:,:128])
+    @pl.when(step%2==1)
+    def _():
+        add_sum(2,out_ref[:,128:])
+        write_made(streams[half],step,128,out_part[:,128:])
+    if causal:
+        write_made(streams[0],step,0,dot(normed_t[...],jnp.concatenate([dq,dk],1)).astype(jnp.bfloat16))
+        write_made(streams[half],step,0,dot(normed_t[...],dv).astype(jnp.bfloat16))
+    else:
+        both=dot(source_t[...],jnp.concatenate([dk,dv],1)).astype(jnp.bfloat16)
+        write_made(streams[0],step,0,dot(normed_t[...],dq).astype(jnp.bfloat16))
+        write_made(streams[0],step,128,both[:,:128])
+        write_made(streams[half],step,0,both[:,128:])
+        for n in range(CROSS_LATE):
+            @pl.when(step==pairs-CROSS_LATE+n)
+            def _():
+                for copy in leave(n): copy.start()
     @pl.when(step==pairs-1)
     def _():
         for n in range(late_count): late_copy(n).wait()
@@ -203,7 +248,7 @@
         sums_ref[3:8,:]=jnp.zeros((5,sums_ref.shape[1]),jnp.float32)
         strip=256
         for r in range(rows//strip):
-            rest1[r](); rest2[r]()
+            tick1(pairs+r); tick2(pairs+r)
             sl=pl.ds(r*strip,strip)
             if causal:
                 wq,wk,wv,residual,total=late
@@ -216,6 +261,7 @@
             sums_ref[4:5,:]+=jnp.sum(grad,axis=0,keepdims=True)
             whole=total[sl,:]+pull_norm(hat,inverse,gain,grad)
             total[sl,:]=whole
+            middle1(pairs+r); middle2(pairs+r)
             if not causal:
                 low_all[sl,:]=whole.astype(jnp.bfloat16)
                 ctx_all[sl,:]=dot(low_all[sl,:],wo[...],NT).astype(jnp.bfloat16)
@@ -223,15 +269,17 @@
         if not causal:
             copies+=[pltpu.make_async_copy(low_all,low_out,late_sem.at[1]),pltpu.make_async_copy(ctx_all,ctx_out,late_sem.at[2])]
         for copy in copies: copy.start()
-        for n in range(rows//strip,len(rest1)): rest1[n](); rest2[n]()
+        for t in range(pairs+rows//strip,count+LAST_LAG): tick1(t); tick2(t); middle1(t); middle2(t)
+        finish()
         if not causal:
             memory_grad=dot(dk_all[...],late[1][...],NT)+dot(dv_all[...],late[2][...],NT)
             flag=jnp.where(flag_ref[0]==1,1.0,0.0)
             dec_ref[...]=memory_grad*flag
             enc_ref[...]=memory_grad*(1.0-flag)
+            for n in range(CROSS_LATE): copies+=leave(n)
         for copy in copies: copy.wait()
 
-def sub_layer_back(q,k,v,g,ctx,lse,limit,flag,causal,normed,source,out_grad,gain,late,depth,collective_id,block=256,width=64):
+def sub_layer_back(q,k,v,g,ctx,lse,limit,flag,causal,normed,source,out_grad,gain,late,before,starts,depth,collective_id,block=256,width=64):
     rows,d=q.shape; keys=k.shape[0]
     pairs=d//128; per=128//width
     each=d//(8*depth)
@@ -242,18 +290,26 @@
     any_=pl.BlockSpec(memory_space=pl.ANY)
     shape=lambda n,t: jax.ShapeDtypeStruct((n,d),t)
     in_specs=[spec(rows),spec(keys),spec(keys),spec(rows),spec(rows),pl.BlockSpec((1,per,rows),lambda i,a,b:(i,0,0))]
-    in_specs+=[once((rows,d)),once(source.shape),once((rows,d)),spec(rows),once(gain.shape)]+[any_]*len(late)
+    in_specs+=[once((rows,d)),once(source.shape),once((rows,d)),pl.BlockSpec((rows,256),lambda i,a,b:(0,i//2)),once(gain.shape)]+[any_]*(len(late)+2)
+    in_specs+=[pl.BlockSpec(a.shape,lambda i,a,b,n=a.ndim:(0,)*n,pipeline_mode=pl.Buffered(1)) for a in starts]
     out_specs=[any_]; out_shape=[shape(rows,f32)]
-    scratch=[pltpu.VMEM(a.shape,a.dtype) for a in late]+[DMA((len(late),))]
+    scratch=[pltpu.VMEM(a.shape,a.dtype) for a in late]+[DMA((len(late)+2*CROSS_LATE,))]
     scratch+=[pltpu.VMEM((d,rows),bf),pltpu.VMEM((8,128) if causal else (d,keys),bf),pltpu.VMEM((d,rows),bf)]
-    scratch+=[pltpu.VMEM((n,d),bf) for n in (rows,keys,keys)]+[pltpu.VMEM((keys,128),f32)]*2
+    scratch+=[pltpu.VMEM((n,d),bf) for n in (rows,keys,keys)]+[pltpu.VMEM((keys,128),f32)]*2+[pltpu.VMEM((d,256),bf)]
     if not causal:
         out_specs+=[any_,any_,keep((keys,d)),keep((keys,d))]
         out_shape+=[shape(rows,bf),shape(rows,bf),shape(keys,f32),shape(keys,f32)]
         scratch+=[pltpu.VMEM((rows,d),bf)]*2
     out_specs+=[keep((8,d))]+[keep((each,d))]*4
     out_shape+=[shape(8,f32)]+[shape(each,f32)]*4
+    if not causal:
+        out_specs+=[any_]*2
+        out_shape+=[jax.ShapeDtypeStruct((max(CROSS_LATE,1),2,2,depth,2,each,256),bf)]*2
+    out_specs+=[pl.BlockSpec(a.shape,lambda i,a,b,n=a.ndim:(0,)*n) for a in starts]
+    out_shape+=[jax.ShapeDtypeStruct(a.shape,a.dtype) for a in starts]
     scratch+=stream_scratch(each,256,depth)*2
+    before_late=CROSS_LATE if causal else FFN_LATE
+    if before_late: scratch+=reduce_scratch([before[w%2].shape[5:]+(bf,) for w in range(2*before_late)],depth)
     return pl.pallas_call(
         functools.partial(sub_layer_kernel,causal,block,width,pairs,depth),
         grid_spec=pltpu.PrefetchScalarGridSpec(num_scalar_prefetch=2,grid=(pairs,),in_specs=in_specs,out_specs=out_specs,scratch_shapes=scratch),
@@ -261,7 +317,7 @@
         compiler_params=pltpu.CompilerParams(vmem_limit_bytes=62*MIB,collective_id=collective_id,has_side_effects=True),
         cost_estimate=pl.CostEstimate(flops=20*rows*keys*d,bytes_accessed=20*rows*d*2,transcendentals=rows*keys*16),
         name="self_back" if causal else "cross_back",
-    )(limit,flag,q,k,v,g,ctx,lse,normed,source,ctx,out_grad,gain,*late)
+    )(limit,flag,q,k,v,g,ctx,lse,normed,source,ctx,out_grad,gain,*late,*before,*starts)
 
 MESH=pl.DeviceIdType.MESH
 DMA=pltpu.SemaphoreType.DMA
@@ -281,10 +337,20 @@
         pl.semaphore_signal(barrier,inc=1,device_id=device,device_id_type=MESH)
     pl.semaphore_wait(barrier,len(partners))
 
+PIECES=2
+AHEAD=2
+
 def gather_sems(count,depth):
+    count=PIECES*count
     return [DMA((count,)),DMA((count,depth-1)),DMA((count,depth-1)),DMA((count,3)),DMA((count,3)),DMA((count,4)),DMA((count,4))]
 
 def gather_plan(ins,outs,sems,depth):
+    parts=[]
+    for a,b in zip(ins,outs):
+        wide=a.shape[1]//PIECES
+        if wide%128: parts+=[(a,b)]
+        else: parts+=[(a.at[:,n*wide:(n+1)*wide],b.at[:,:,:,:,n*wide:(n+1)*wide]) for n in range(PIECES)]
+    ins,outs=[p[0] for p in parts],[p[1] for p in parts]
     count=len(ins)
     local,z_send,z_recv,a_send,a_recv,c_send,c_recv=sems
     dp,fs,z,c=place()
@@ -320,20 +386,25 @@
         f,g=bits(w)
         across(w,2,turned(dp,f),g).wait_recv()
         core(w,3,turned(turned(dp,f),g)).start()
+    def along(t):
+        for w in (2*t,2*t+1):
+            if w<count:
+                own(w).start()
+                for k in range(1,depth): line(w,k).start()
     def begin():
-        for w in range(count):
-            own(w).start()
-            for k in range(1,depth): line(w,k).start()
+        for t in range(AHEAD): along(t)
     def tick(t):
+        along(t+AHEAD)
         for n,step in enumerate((step0,step1,step2,step3)):
-            if 0<=t-n<count: step(t-n)
+            for w in (2*(t-n),2*(t-n)+1):
+                if 0<=w<count: step(w)
     def finish():
         for w in range(count):
             f,g=bits(w)
             for k in range(1,depth): line(w,k).wait_send()
             across(w,0,dp,f).wait_send(); across(w,1,dp,g).wait_send(); across(w,2,dp,g).wait_send()
             for n in range(4): core(w,n,dp).wait()
-    return begin,[functools.partial(tick,t) for t in range(count+3)],finish
+    return begin,[functools.partial(tick,t) for t in range((count+1)//2+3)],finish
 
 def reduce_scratch(kinds,depth):
     count=len(kinds)
@@ -341,7 +412,7 @@
     return (vmem(2,2,depth)+vmem(2,2,depth)+vmem(2,depth)+vmem(depth)+vmem(depth-1)
       +[DMA((count,)),DMA((count,)),DMA((count,)),DMA((count,2)),DMA((count,2)),DMA((count,depth-1)),DMA((count,depth-1))])
 
-def reduce_plan(ins,outs,scratch,depth):
+def reduce_plan(ins,store,scratch,depth):
     count=len(ins)
     held,r0,r1,r2,r3=(scratch[n*count:(n+1)*count] for n in range(5))
     local,c_send,c_recv,a_send,a_recv,z_send,z_recv=scratch[5*count:]
@@ -361,34 +432,24 @@
         return pltpu.make_async_remote_copy(held[w].at[hi,lo,lax.rem(z+k,depth)],r3[w].at[k-1],z_send.at[w,k-1],z_recv.at[w,k-1],(dp,lax.rem(z+k,depth)*2+c),MESH)
     def step0(w):
         own(w).wait(); core(w).wait_recv()
-        def add(n,_):
-            i,k=n//depth,n%depth
-            held[w][i//2,i%2,k]=held[w][i//2,i%2,k]+r0[w][i//2,i%2,k]
-            return 0
-        lax.fori_loop(0,4*depth,add,0)
+        for i in range(4): held[w][i//2,i%2]=held[w][i//2,i%2]+r0[w][i//2,i%2]
         first(w).start()
     def step1(w):
         first(w).wait_recv()
-        def add(n,_):
-            i,k=n//depth,n%depth
-            if w%2: held[w][hi,i,k]=held[w][hi,i,k]+r1[w][i,k]
-            else: held[w][i,lo,k]=held[w][i,lo,k]+r1[w][i,k]
-            return 0
-        lax.fori_loop(0,2*depth,add,0)
+        for i in range(2):
+            if w%2: held[w][hi,i]=held[w][hi,i]+r1[w][i]
+            else: held[w][i,lo]=held[w][i,lo]+r1[w][i]
         second(w).start()
     def step2(w):
         second(w).wait_recv()
-        def add(k,_):
-            held[w][hi,lo,k]=held[w][hi,lo,k]+r2[w][k]
-            return 0
-        lax.fori_loop(0,depth,add,0)
+        held[w][hi,lo]=held[w][hi,lo]+r2[w][...]
         for k in range(1,depth): line(w,k).start()
     def step3(w):
         total=held[w][hi,lo,z].astype(jnp.float32)
         for k in range(1,depth):
             line(w,k).wait_recv()
             total=total+r3[w][k-1].astype(jnp.float32)
-        outs[w][...]=total
+        store(w,total)
     def begin():
         for w in range(count):
             core(w).start(); own(w).start()
@@ -410,11 +471,25 @@
 def reduce_parts(partials,depth):
     return [p.reshape((2,2,depth,2,p.shape[0]//(8*depth),p.shape[1])) for p in partials]
 
-def first_kernel(count,lines,depth,*refs):
+def shuffle(read,write,outer,inner,part):
+    each=128//part
+    for t in range(outer*inner//each):
+        whole=None
+        for u in range(each):
+            b,a=divmod(t*each+u,outer)
+            tile,at=divmod(a*inner+b,each)
+            piece=read(tile)
+            if u!=at: piece=pltpu.roll(piece,(u-at)*part%128,1)
+            lane=lax.broadcasted_iota(jnp.int32,piece.shape,1)
+            whole=piece if whole is None else jnp.where(lane>=u*part,piece,whole)
+        write(t,whole)
+
+def first_kernel(count,lines,depth,blocks,*refs):
     ins,vectors,wide=refs[:count],refs[count:count+lines],refs[count+lines]
     refs=refs[count+lines+1:]
     outs,table,long=refs[:count],refs[count],refs[count+1]
     packed,every=refs[count+2:count+4]
+    part=128//blocks
     each=vectors[0].shape[1]
     greet(depth)
     packed[...]=jnp.zeros_like(packed)
@@ -432,15 +507,15 @@
         for r in range(1,group):
             tile=jnp.where(lane>=r*each,pltpu.roll(device(m*group+r),r*each,1),tile)
         table[:,m*128:(m+1)*128]=tile
-    for n in range(8*depth):
-        long[:,n*128:(n+1)*128]=device(n)[lines:lines+1]
-
-def gather_first(shards,vectors,wide,depth,collective_id):
+    def write_long(t,value): long[:,t*128:(t+1)*128]=value
+    shuffle(lambda n: device(n)[lines:lines+1],write_long,8*depth,blocks,part)
+
+def gather_first(shards,vectors,wide,blocks,depth,collective_id):
     count=len(shards); lines=len(vectors)
     any_=pl.BlockSpec(memory_space=pl.ANY); vm=pl.BlockSpec(memory_space=pltpu.VMEM)
     total=vectors[0].shape[0]*8*depth
     outs=pl.pallas_call(
-        functools.partial(first_kernel,count,lines,depth),
+        functools.partial(first_kernel,count,lines,depth,blocks),
         in_specs=[any_]*count+[vm]*(lines+1),
         out_specs=[any_]*count+[vm]*2,
         out_shape=gather_shapes(shards,depth)+[jax.ShapeDtypeStruct((16,total),jnp.float32),jax.ShapeDtypeStruct((1,128*8*depth),jnp.float32)],
@@ -453,7 +528,8 @@
 def last_kernel(count,depth,*refs):
     ins,outs,scratch=refs[:count],refs[count:2*count],refs[2*count:]
     greet(depth)
-    begin,ticks,finish=reduce_plan(ins,outs,scratch,depth)
+    def store(w,total): outs[w][...]=total
+    begin,ticks,finish=reduce_plan(ins,store,scratch,depth)
     begin()
     for tick in ticks: tick()
     finish()
@@ -473,89 +549,113 @@
     )(*parts)
 
 SLOTS=4
+STREAM=14
+LAST_LAG=5
 
 def stream_scratch(rows,cols,depth):
     vmem=lambda *lead: pltpu.VMEM(lead+(rows,cols),jnp.bfloat16)
-    return [vmem(2,2,2,depth,2),vmem(SLOTS,2,2,depth),vmem(SLOTS,2,2,depth),vmem(SLOTS,2,depth),vmem(SLOTS,depth),vmem(SLOTS,depth-1),
+    return [vmem(2,2,2,depth,2),vmem(SLOTS,2,2,depth),vmem(SLOTS,2,2,depth),vmem(SLOTS,2,depth),vmem(SLOTS,2,depth),vmem(SLOTS,depth),vmem(SLOTS,depth),vmem(SLOTS,depth-1),
       DMA((SLOTS,)),DMA((SLOTS,)),DMA((SLOTS,2)),DMA((SLOTS,2)),DMA((SLOTS,depth-1)),DMA((SLOTS,depth-1))]
 
-def stream_plan(count,parity,store,scratch,depth):
-    made,r0,held,r1,r2,r3,c_send,c_recv,a_send,a_recv,z_send,z_recv=scratch
+def stream_plan(count,odd,store,scratch,depth):
+    made,r0,sum0,r1,sum1,r2,sum2,r3,c_send,c_recv,a_send,a_recv,z_send,z_recv=scratch
     dp,fs,z,c=place()
     hi,lo=dp//2,dp%2
+    here,there=(hi,1-hi) if odd else (lo,1-lo)
+    here2,there2=(lo,1-lo) if odd else (hi,1-hi)
     def slot(i): return lax.rem(i,SLOTS)
     def core(i):
         s=slot(i)
         return pltpu.make_async_remote_copy(made.at[lax.rem(i,2),:,:,:,1-c],r0.at[s],c_send.at[s],c_recv.at[s],(dp,z*2+1-c),MESH)
-    def first(i,odd):
+    def first(i):
         s=slot(i)
-        src=held.at[s,1-hi] if odd else held.at[s,:,1-lo]
+        src=sum0.at[s,there] if odd else sum0.at[s,:,there]
         return pltpu.make_async_remote_copy(src,r1.at[s],a_send.at[s,0],a_recv.at[s,0],(turned(dp,2 if odd else 1),fs),MESH)
-    def second(i,odd):
+    def second(i):
         s=slot(i)
-        src=held.at[s,hi,1-lo] if odd else held.at[s,1-hi,lo]
-        return pltpu.make_async_remote_copy(src,r2.at[s],a_send.at[s,1],a_recv.at[s,1],(turned(dp,1 if odd else 2),fs),MESH)
+        return pltpu.make_async_remote_copy(sum1.at[s,there2],r2.at[s],a_send.at[s,1],a_recv.at[s,1],(turned(dp,1 if odd else 2),fs),MESH)
     def line(i,k):
         s=slot(i)
-        return pltpu.make_async_remote_copy(held.at[s,hi,lo,lax.rem(z+k,depth)],r3.at[s,k-1],z_send.at[s,k-1],z_recv.at[s,k-1],(dp,lax.rem(z+k,depth)*2+c),MESH)
-    def by_parity(i,run):
-        p=parity(i)
-        if isinstance(p,int): run(p)
-        else:
-            for odd in (0,1):
-                @pl.when(p==odd)
-                def _(): run(odd)
+        return pltpu.make_async_remote_copy(sum2.at[s,lax.rem(z+k,depth)],r3.at[s,k-1],z_send.at[s,k-1],z_recv.at[s,k-1],(dp,lax.rem(z+k,depth)*2+c),MESH)
     def step0(i):
         s=slot(i); m=lax.rem(i,2)
         core(i).wait()
-        def add(n,_):
-            a,k=n//depth,n%depth
-            held[s,a//2,a%2,k]=made[m,a//2,a%2,k,c]+r0[s,a//2,a%2,k]
-            return 0
-        lax.fori_loop(0,4*depth,add,0)
-        by_parity(i,lambda odd: first(i,odd).start())
+        for a in range(4):
+            sum0[s,a//2,a%2]=made[m,a//2,a%2,:,c]+r0[s,a//2,a%2]
+        first(i).start()
     def step1(i):
         s=slot(i)
-        first(i,0).wait_recv()
-        def run(odd):
-            def add(n,_):
-                a,k=n//depth,n%depth
-                if odd: held[s,hi,a,k]=held[s,hi,a,k]+r1[s,a,k]
-                else: held[s,a,lo,k]=held[s,a,lo,k]+r1[s,a,k]
-                return 0
-            lax.fori_loop(0,2*depth,add,0)
-            second(i,odd).start()
-        by_parity(i,run)
+        first(i).wait()
+        for a in range(2):
+            sum1[s,a]=(sum0[s,here,a] if odd else sum0[s,a,here])+r1[s,a]
+        second(i).start()
     def step2(i):
         s=slot(i)
-        second(i,0).wait_recv()
-        def add(k,_):
-            held[s,hi,lo,k]=held[s,hi,lo,k]+r2[s,k]
-            return 0
-        lax.fori_loop(0,depth,add,0)
+        second(i).wait()
+        sum2[s]=sum1[s,here2]+r2[s]
         for k in range(1,depth): line(i,k).start()
     def step3(i):
         s=slot(i)
-        total=held[s,hi,lo,z].astype(jnp.float32)
+        total=sum2[s,z].astype(jnp.float32)
         for k in range(1,depth):
-            line(i,k).wait_recv()
+            line(i,k).wait()
             total=total+r3[s,k-1].astype(jnp.float32)
         store(i,total)
-        first(i,0).wait_send(); second(i,0).wait_send()
-        for k in range(1,depth): line(i,k).wait_send()
-    stages=((5,step3),(4,step2),(3,step1),(2,step0),(1,lambda i: core(i).start()))
-    def tick(j):
+    def run(j,stages):
         for lag,step in stages:
             if isinstance(j,int):
                 if 0<=j-lag<count: step(jnp.int32(j-lag))
             else:
-                @pl.when(j>=lag)
+                @pl.when((j>=lag)&(j<lag+count))
                 def _(): step(j-lag)
-    return tick,[functools.partial(tick,count+n) for n in range(5)]
+    def tick(j):
+        run(j,((5,step3),(4,step2),(3,step1),(1,lambda i: core(i).start())))
+    def middle(j):
+        run(j,((1,step0),))
+    return tick,middle
 
 def write_made(made,i,col,value):
     shape=made.shape[1:6]+value.shape[1:]
     made[lax.rem(i,2),:,:,:,:,:,col:col+value.shape[1]]=value.reshape(shape)
+
+
+def deliver_kernel(count,devices,blocks,*refs):
+    ins,outs,held,(here,there)=refs[:count],refs[count:2*count],refs[2*count:3*count-1],refs[3*count-1:]
+    come=[pltpu.make_async_copy(ins[n],held[n-1],here.at[n]) for n in range(1,count)]
+    go=[pltpu.make_async_copy(held[n-1],outs[n],there.at[n]) for n in range(1,count)]
+    for copy in come: copy.start()
+    def read(t): return ins[0][:,t*128:(t+1)*128]
+    def write(t,value): outs[0][:,t*128:(t+1)*128]=value
+    shuffle(read,write,blocks,devices,128//blocks)
+    for a,b in zip(come,go):
+        a.wait()
+        b.start()
+    for copy in go: copy.wait()
+
+def deliver(arrays,devices,blocks):
+    count=len(arrays)
+    any_=pl.BlockSpec(memory_space=pl.ANY); vm=pl.BlockSpec(memory_space=pltpu.VMEM)
+    return pl.pallas_call(
+        functools.partial(deliver_kernel,count,devices,blocks),
+        in_specs=[vm]+[any_]*(count-1),
+        out_specs=[vm]+[any_]*(count-1),
+        out_shape=[jax.ShapeDtypeStruct(a.shape,a.dtype) for a in arrays],
+        scratch_shapes=[pltpu.VMEM(a.shape,a.dtype) for a in arrays[1:]]+[DMA((count,)),DMA((count,))],
+        compiler_params=pltpu.CompilerParams(vmem_limit_bytes=62*MIB),
+        name="deliver",
+    )(*arrays)
+
+def order_kernel(blocks,outer,shard,out):
+    def read(t): return shard[:,t*128:(t+1)*128].astype(jnp.float32)
+    def write(t,value): out[:,t*128:(t+1)*128]=value.astype(jnp.bfloat16)
+    shuffle(read,write,outer,blocks,128//blocks)
+
+def order_columns(shard,outer,blocks):
+    return pl.pallas_call(
+        functools.partial(order_kernel,blocks,outer),
+        out_shape=jax.ShapeDtypeStruct(shard.shape,shard.dtype),
+        name="order_columns",
+    )(shard)
 
 EPSILON=1e-05
 def normal(tensor):
@@ -568,8 +668,11 @@
     scaled=grad*gain
     return inverse*(scaled-jnp.mean(scaled,axis=-1,keepdims=True)-hat*jnp.mean(scaled*hat,axis=-1,keepdims=True))
 
+FFN_LATE=0
+CROSS_LATE=0
+
 def ffn_kernel(strip, steps, depth, length_ref, after_ref, cot_ref, w1_ref, w2_ref, b1_ref, vec_ref, wo_ref,
-               mixed_ref, grad_ref, low_ref, ctx_ref, dw1_ref, dw2_ref, db1_ref, dvec_ref, n3, n3t, gf, branch, gn, wo, sem, *refs):
+               mixed_ref, grad_ref, low_ref, ctx_ref, dw1_ref, dw2_ref, db1_ref, dvec_ref, late1_ref, late2_ref, n3, n3t, gf, branch, gn, wo, sem, *refs):
     j=pl.program_id(0)
     rows,d=after_ref.shape
     gain,shift,b2=vec_ref[0:1,:],vec_ref[1:2,:],vec_ref[2:3,:]
@@ -580,8 +683,11 @@
         wide=w1_ref.shape[1]
         def store1(i,total): dw1_ref[:,pl.ds(pl.multiple_of(i*wide,128),wide)]=total
         def store2(i,total): dw2_ref[i]=total
-        tick1,rest1=stream_plan(steps,lambda i: 0,store1,refs[:half],depth)
-        tick2,rest2=stream_plan(steps,lambda i: 1,store2,refs[half:],depth)
+        tick1,middle1=stream_plan(steps-FFN_LATE,0,store1,refs[:half],depth)
+        tick2,middle2=stream_plan(steps-FFN_LATE,1,store2,refs[half:],depth)
+        def leave(n):
+            m=(steps-FFN_LATE+n)%2
+            return [pltpu.make_async_copy(refs[0].at[m],late1_ref.at[n],sem.at[4+2*n]),pltpu.make_async_copy(refs[half].at[m],late2_ref.at[n],sem.at[5+2*n])]
     @pl.when(j==0)
     def _():
         if depth: greet(depth)
@@ -602,6 +708,8 @@
     w1=w1_ref[...]; w2=w2_ref[...].reshape(w1.shape[1],d)
     pre=dot(n3[...],w1)+b1_ref[...]
     back=dot(gf[...],w2,NT).astype(jnp.bfloat16).astype(jnp.float32)
+    if depth:
+        middle1(j); middle2(j)
     root=0.7978845608028654
     square=pre*pre
     t=jnp.tanh(root*pre*(1.0+0.044715*square))
@@ -616,6 +724,10 @@
     if depth:
         write_made(refs[0],j,0,dw1)
         write_made(refs[half],j,0,dw2)
+        for n in range(FFN_LATE):
+            @pl.when(j==steps-FFN_LATE+n)
+            def _():
+                for copy in leave(n): copy.start()
     else:
         dw1_ref[...]=dw1
         dw2_ref[...]=dw2.reshape(dw2_ref.shape)
@@ -635,16 +747,19 @@
             gn[sl,:]=grad
             gf[sl,:]=grad.astype(jnp.bfloat16)
             n3t[sl,:]=dot(gf[sl,:],wo[...],NT).astype(jnp.bfloat16)
-        late=list(zip(rest1,rest2)) if depth else []
         pltpu.make_async_copy(wo_ref,wo,sem.at[2]).wait()
         for r in range(rows//strip):
-            if r%2==0 and r//2<len(late):
-                late[r//2][0](); late[r//2][1]()
+            if depth and r%2==0:
+                tick1(steps+r//2); tick2(steps+r//2)
             one(r)
+            if depth and r%2==0:
+                middle1(steps+r//2); middle2(steps+r//2)
         copies=[pltpu.make_async_copy(a,b,sem.at[n]) for n,(a,b) in enumerate(((n3,mixed_ref),(gn,grad_ref),(gf,low_ref),(n3t,ctx_ref)))]
         for copy in copies: copy.start()
-        for a,b in late[rows//strip//2:]:
-            a(); b()
+        if depth:
+            for t in range(steps+rows//strip//2,steps-FFN_LATE+LAST_LAG):
+                tick1(t); tick2(t); middle1(t); middle2(t)
+            for n in range(FFN_LATE): copies+=leave(n)
         for copy in copies: copy.wait()
 
 def feed_forward(after,cot,length,w1,w2,b1,vec,wo,block=512,strip=128,depth=0,collective_id=None):
@@ -656,23 +771,25 @@
     wide=pl.BlockSpec((d,block),lambda j,n:(0,j)); line=pl.BlockSpec((1,block),lambda j,n:(0,j))
     tall=pl.BlockSpec((w2.shape[0],block//w2.shape[0],d),lambda j,n:(0,j,0))
     bf=jnp.bfloat16; f32=jnp.float32
-    scratch=[pltpu.VMEM((rows,d),bf),pltpu.VMEM((d,rows),bf),pltpu.VMEM((rows,d),bf),pltpu.VMEM((rows,d),f32),pltpu.VMEM((rows,d),f32),pltpu.VMEM((d,d),bf),DMA((4,))]
+    scratch=[pltpu.VMEM((rows,d),bf),pltpu.VMEM((d,rows),bf),pltpu.VMEM((rows,d),bf),pltpu.VMEM((rows,d),f32),pltpu.VMEM((rows,d),f32),pltpu.VMEM((d,d),bf),DMA((4+2*FFN_LATE,))]
     if depth:
         each=d//(8*depth); part=block//(8*depth)
         grad_specs=[keep((each,ff)),keep((steps,part,d))]
         grad_shapes=[jax.ShapeDtypeStruct((each,ff),f32),jax.ShapeDtypeStruct((steps,part,d),f32)]
+        late_shapes=[jax.ShapeDtypeStruct((max(FFN_LATE,1),2,2,depth,2,each,block),bf),jax.ShapeDtypeStruct((max(FFN_LATE,1),2,2,depth,2,part,d),bf)]
         scratch+=stream_scratch(each,block,depth)+stream_scratch(part,d,depth)
     else:
         grad_specs=[wide,tall]
         grad_shapes=[jax.ShapeDtypeStruct(w1.shape,bf),jax.ShapeDtypeStruct(w2.shape,bf)]
+        late_shapes=[jax.ShapeDtypeStruct((8,128),bf)]*2
     return pl.pallas_call(
         functools.partial(ffn_kernel,strip,steps,depth),
         grid_spec=pltpu.PrefetchScalarGridSpec(
             num_scalar_prefetch=1,grid=(steps,),
             in_specs=[once((rows,d)),once((rows,d)),wide,tall,line,once(vec.shape),any_],
-            out_specs=[any_]*4+grad_specs+[line,keep((8,d))],
+            out_specs=[any_]*4+grad_specs+[line,keep((8,d)),any_,any_],
             scratch_shapes=scratch),
-        out_shape=[jax.ShapeDtypeStruct((rows,d),bf),jax.ShapeDtypeStruct((rows,d),f32)]+[jax.ShapeDtypeStruct((rows,d),bf)]*2+grad_shapes+[jax.ShapeDtypeStruct((1,ff),f32),jax.ShapeDtypeStruct((8,d),f32)],
+        out_shape=[jax.ShapeDtypeStruct((rows,d),bf),jax.ShapeDtypeStruct((rows,d),f32)]+[jax.ShapeDtypeStruct((rows,d),bf)]*2+grad_shapes+[jax.ShapeDtypeStruct((1,ff),f32),jax.ShapeDtypeStruct((8,d),f32)]+late_shapes,
         compiler_params=pltpu.CompilerParams(vmem_limit_bytes=62*MIB,collective_id=collective_id,has_side_effects=depth>0),
         cost_estimate=pl.CostEstimate(flops=12*rows*d*ff,bytes_accessed=4*d*ff*2+rows*d*12,transcendentals=rows*ff),
         name="feed_forward",
@@ -717,15 +834,14 @@
     ln3_gain, ln3_shift, ffn_w1, ffn_b1, ffn_w2, ffn_b2):
     steps=8
     each=1024//devices
-    if depth:
-        part=4*each//steps
-        ffn_w1=ffn_w1.reshape(each,devices,steps,part).transpose(0,2,1,3).reshape(each,4096)
+    if depth: ffn_w1=order_columns(ffn_w1,devices,steps)
     w1=lax.all_gather(ffn_w1,AXES,axis=0,tiled=True)
     w2=lax.all_gather(ffn_w2,AXES,axis=0,tiled=True)
     small=[ln1_gain,ln1_shift,self_bq,self_bv,self_bo,ln2_gain,ln2_shift,cross_bq,cross_bv,cross_bo,ln3_gain,ln3_shift,ffn_b2]
     late=[self_wo,cross_wq,cross_wk,cross_wv,cross_wo]
     if depth:
-        wq,wk,wv,vectors,b1=gather_first([self_wq,self_wk,self_wv],small,ffn_b1,depth,1)
+        part=4*each//steps
+        wq,wk,wv,vectors,b1=gather_first([self_wq,self_wk,self_wv],small,ffn_b1,steps,depth,1)
     else:
         wq,wk,wv,*late=gather_all([self_wq,self_wk,self_wv]+late)
         vectors,b1=gather_vectors(small,ffn_b1)
@@ -744,20 +860,18 @@
     after_cross=after_self+(dot(cctx,cwo)+cbo)
     last=jnp.concatenate([vectors[10:13],jnp.zeros((5,1024),jnp.float32)])
     if depth:
-        b1=b1.reshape(devices,steps,part).transpose(1,0,2).reshape(1,4096)
-        mixed,g_cross,gc,g_cctx,dw1,dw2,db1,dvec=feed_forward(after_cross,cotangent[0],unit_len,w1,w2.reshape(devices,4*each,1024),b1,last,cwo,depth=depth,collective_id=3)
-        dw1=dw1.reshape(each,steps,devices,part).transpose(0,2,1,3).reshape(each,4096)
-        dw2=dw2.reshape(4*each,1024)
+        mixed,g_cross,gc,g_cctx,dw1,dw2,db1,dvec,*before=feed_forward(after_cross,cotangent[0],unit_len,w1,w2.reshape(devices,4*each,1024),b1,last,cwo,depth=depth,collective_id=3)
         db1=db1.reshape(steps,devices,part).transpose(1,0,2)
     else:
-        mixed,g_cross,gc,g_cctx,dw1,dw2,db1,dvec=feed_forward(after_cross,cotangent[0],unit_len,w1,w2[None],b1,last,cwo)
+        mixed,g_cross,gc,g_cctx,dw1,dw2,db1,dvec,*_=feed_forward(after_cross,cotangent[0],unit_len,w1,w2[None],b1,last,cwo)
         dw1,dw2=reduce_all([dw1,dw2[0]])
     gain1,gain2=vectors[0:1],vectors[5:6]
     if depth:
-        g_self,gs,g_ctx,g_dec,g_enc,csums,dcwq,dcwk,dcwv,dcwo=sub_layer_back(
-            cq,ck,cv,g_cctx,cctx,clse,text_len,task_flag,False,n2,memory,gc,gain2,[cwq,cwk,cwv,wo,after_self,g_cross],depth,4)
-        g_units,sums,dwq,dwk,dwv,dwo=sub_layer_back(
-            q,k,v,g_ctx,ctx,lse,text_len,task_flag,True,n1,memory,gs,gain1,[wq,wk,wv,unit_states[0],g_self],depth,5)
+        g_self,gs,g_ctx,g_dec,g_enc,csums,*starts,left1,left2,dw1,dw2=sub_layer_back(
+            cq,ck,cv,g_cctx,cctx,clse,text_len,task_flag,False,n2,memory,gc,gain2,[cwq,cwk,cwv,wo,after_self,g_cross],before,[dw1,dw2],depth,4)
+        dw2=dw2.reshape(4*each,1024)
+        g_units,sums,dwq,dwk,dwv,dwo,dcwq,dcwk,dcwv,dcwo=sub_layer_back(
+            q,k,v,g_ctx,ctx,lse,text_len,task_flag,True,n1,memory,gs,gain1,[wq,wk,wv,unit_states[0],g_self],[left1,left2],starts,depth,5)
         small_grads=[sums[3],sums[4],sums[0],sums[1],sums[2],csums[3],csums[4],csums[0],csums[1],csums[2],dvec[0],dvec[1],dvec[2]]
     else:
         gcq,gck,gcv=flash_bwd(cq,ck,cv,g_cctx,cctx,clse,text_len,False)
@@ -778,6 +892,9 @@
     grads=grads.reshape(1024)
     ng=[grads[i*each:(i+1)*each] for i in range(13)]
     db1=grads[13*each:17*each]
+    if depth:
+        dw1,mixed,g_units,g_dec,g_enc,dwq,dwk,dwv,dwo,dcwq,dcwk,dcwv,dcwo,dw2=deliver(
+            [dw1,mixed,g_units,g_dec,g_enc,dwq,dwk,dwv,dwo,dcwq,dcwk,dcwv,dcwo,dw2],devices,steps)
     return (mixed[None],g_units[None],g_dec[None],g_enc[None],
         ng[0],ng[1],dwq,ng[2],dwk,dwv,ng[3],dwo,ng[4],ng[5],ng[6],dcwq,ng[7],dcwk,dcwv,ng[8],dcwo,ng[9],ng[10],ng[11],dw1,db1,dw2,ng[12])
 

time: 526 us -> 495 us (0.941)
  local copies, waits for them, and re-layouts: 37.3 us -> 12.5 us
  Pallas kernels: 436 us -> 425 us
  waiting for transfers between devices: 2.7 us -> 9.84 us
    unnamed x108 -> x67, local copies, waits for them, and re-layouts: 24.4 us -> 5.07 us
    pallas_call x2, Pallas kernels: 150 us -> 138 us  [sub_layer_back(): pl.pallas_call(functools.partial(sub_layer_kernel, causal, block, width,...]
    pallas_call x1 -> x3, Pallas kernels: 57.6 us -> 67.6 us  [the longest x1 55.7 us: gather_first(): pl.pallas_call(functools.partial(first_kernel, count, lines, depth, block...]
    all_gather x1, waiting for transfers between devices: 1.98 us -> 9.13 us  [shards(): w2 = lax.all_gather(ffn_w2, AXES, axis=0, tiled=True)]
    pallas_call x2, Pallas kernels: 95.5 us -> 89.9 us  [flash_fwd(): pl.pallas_call(functools.partial(fwd_kernel, causal, block, width, count,...]
  transfers between devices with their start and end apart: 2 -> 2, of which waited for: 1 -> 1; matrix products, arithmetic and copies ran while one was open for 6% -> 6% of each run, Pallas kernels for 29% -> 30%
where the time goes in v4:
time: 495 us; the launch traced here: 493 us
  Pallas kernels  425 us (86%)
  matrix products  21.7 us (4%)
  between operations  16.8 us (3%)
  local copies, waits for them, and re-layouts  12.5 us (3%)
  waiting for transfers between devices  9.84 us (2%)
  other arithmetic  6.96 us (1%)
    pallas_call x2, Pallas kernels, sub_layer_back(): pl.pallas_call(functools.partial(sub_layer_kernel, causal, block, width,...  138 us
    pallas_call x1, Pallas kernels, feed_forward(): pl.pallas_call(functools.partial(ffn_kernel, strip, steps, depth), grid_s...  116 us
    pallas_call x2, Pallas kernels, flash_fwd(): pl.pallas_call(functools.partial(fwd_kernel, causal, block, width, count,...  89.9 us
    pallas_call x1, Pallas kernels, gather_first(): pl.pallas_call(functools.partial(first_kernel, count, lines, depth, block...  55.7 us
    dot_general x8, matrix products, dot(): return lax.dot_general(a, b, dims, preferred_element_type=jnp.float32)  21.7 us
    pallas_call x1, Pallas kernels, reduce_rows(): pl.pallas_call(functools.partial(last_kernel, count, depth), in_specs=[pl...  12.9 us
  transfers between devices with their start and end apart: 2, of which 1 were waited for; matrix products, arithmetic and copies ran while one was open for 6% of the time, Pallas kernels for 30%

profile of v4, /device:TPU:0, one launch (start us, length us, event | category | flops | bytes accessed | tf_op | source)
XLA Modules:
  0.0 492.6 jit_solution(13393230195059464899)
XLA Ops:
  7.3 2.3 order_columns.1
  11.7 55.7 %gather_first.1 = (bf16[4,4,2,32,1024]{4,3,2,1,0:T(8,128)(2,1)}, bf16[4,4,2,32,1024]{4,3,2,1,0:T(8,128)(2,1)}, bf16[4,4,2,32,1024]{4,3,2,1,0:T(8,128)(2,1)}, f32[16,1024]{1,0:T(8,128)}, f32[1,4096]{1,0:T(1,128)}) custom-call(bf16[32,1024]{1,0:T(8,128)(2,1)} %refs_0_.2, bf16[32,1024]{1,0:T(8,128)(2,1)} %refs_1_.2, bf16[32,1024]{1,0:T(8,128)(2,1)} %refs_2_.2, ...), custom_call_target="tpu_custom_call" | custom-call | tf_op jit(solution)/shard_map/gather_first/pallas_call | solution.py:517
  67.4 0.9 slice.115
  69.6 1.9 convert_reduce_fusion
  72.3 3.7 convolution_convert_fusion.k_ref.refs_1_
  76.1 3.7 add_convert_fusion.2.v_ref.refs_2_
  79.8 3.7 add_convert_fusion.3.q_ref.refs_0_
  83.6 76.6 %attend_causal.1 = (bf16[1024,1024]{1,0:T(8,128)(2,1)S(1)}, f32[8,2,1024]{2,1,0:T(2,128)S(1)}, bf16[4,4,2,32,1024]{4,3,2,1,0:T(8,128)(2,1)S(1)}, bf16[4,4,2,32,1...) custom-call(s32[1]{0:T(128)S(6)} %copy.71.lim_ref, ...), custom_call_target="tpu_custom_call" | custom-call | flops 2147483648 | bytes 8388608 | tf_op jit(solution)/shard_map/attend_causal/pallas_call | solution.py:82
  160.2 2.5 fusion.14
  163.3 0.8 copy-done.21
  164.7 1.6 copy-done.19
  168.5 1.3 copy-done.16
  169.8 2.3 add_convert_fusion.q_ref.refs_0_
  172.2 13.4 %attend_text.1 = (bf16[1024,1024]{1,0:T(8,128)(2,1)S(1)}, f32[8,2,1024]{2,1,0:T(2,128)S(1)}) custom-call(s32[1]{0:T(128)S(6)} %copy.71.lim_ref, bf16[1024,1024]{1,0:T(8,128)(2,1)S(1)} %add_convert_fusion.q_ref.refs_0_, bf16[256,1024]{1,0:T(8,128)(2,1)S(1)} %convolution_convert_fusion.1.k_ref.refs_1_, bf16[256,1024]{1,0:T(8,128)(2,1)S(1)} %fusion.7.v_ref.refs_2_), custom_call_target="tpu_custom_call" | custom-call | flops 1073741824 | bytes 8388608 | tf_op jit(solution)/shard_map/attend_text/pallas_call | solution.py:82
  185.6 2.2 fusion.5.refs_6_
  187.8 4.4 add_add_fusion.after_ref
  192.2 9.1 %all-gather.5.cloned.1.call-done = bf16[4096,1024]{1,0:T(8,128)(2,1)} async-done(((bf16[128,1024]{1,0:T(8,128)(2,1)}), bf16[4096,1024]{1,0:T(8,128)(2,1)}) %all-gather.5.cloned.1.call-update) | async-done | bytes 8388624 | tf_op jit(solution)/shard_map/all_gather | solution.py:839
  201.3 116.3 %feed_forward.1 = (bf16[1024,1024]{1,0:T(8,128)(2,1)}, f32[1024,1024]{1,0:T(8,128)}, bf16[1024,1024]{1,0:T(8,128)(2,1)}, bf16[1024,1024]{1,0:T(8,128)(2,1)}, f32...) custom-call(s32[1]{0:T(128)S(6)} %copy.70.length_ref, ...), custom_call_target="tpu_custom_call" | custom-call | flops 51539607552 | bytes 46137344 | tf_op jit(solution)/shard_map/feed_forward/pallas_call | solution.py:785
  317.6 62.3 %cross_back.1 = (f32[1024,1024]{1,0:T(8,128)}, bf16[1024,1024]{1,0:T(8,128)(2,1)}, bf16[1024,1024]{1,0:T(8,128)(2,1)}, f32[256,1024]{1,0:T(8,128)}, f32[256,1024...) custom-call(s32[1]{0:T(128)S(6)} %copy.71.lim_ref, ...), custom_call_target="tpu_custom_call" | custom-call | flops 5368709120 | bytes 41943040 | tf_op jit(solution)/shard_map/cross_back/pallas_call | solution.py:313
  380.0 75.7 %self_back.1 = (f32[1024,1024]{1,0:T(8,128)}, f32[8,1024]{1,0:T(8,128)}, f32[32,1024]{1,0:T(8,128)}, f32[32,1024]{1,0:T(8,128)}, f32[32,1024]{1,0:T(8,128)}, /*i...) custom-call(s32[1]{0:T(128)S(6)} %copy.71.lim_ref, ...), custom_call_target="tpu_custom_call" | custom-call | flops 21474836480 | bytes 41943040 | tf_op jit(solution)/shard_map/self_back/pallas_call | solution.py:313
  460.1 12.9 %reduce_rows.1 = f32[8,128]{1,0:T(8,128)} custom-call(f32[2,2,4,2,8,128]{5,4,3,2,1,0:T(8,128)} %bitcast.87), custom_call_target="tpu_custom_call" | custom-call | tf_op jit(solution)/shard_map/reduce_rows/pallas_call | solution.py:541
  472.9 1.8 fusion.13
  474.7 1.3 slice.133
  476.0 9.5 %deliver.1 = (f32[32,4096]{1,0:T(8,128)}, bf16[1024,1024]{1,0:T(8,128)(2,1)}, f32[1024,1024]{1,0:T(8,128)}, f32[256,1024]{1,0:T(8,128)}, f32[256,1024]{1,0:T(8,1...) custom-call(f32[32,4096]{1,0:T(8,128)} %get-tuple-element.110.refs_0, ...), custom_call_target="tpu_custom_call" | custom-call | tf_op jit(solution)/shard_map/deliver/pallas_call | solution.py:638
  (96 shorter events, 9.9 us)
Async XLA Ops:
  7.2 64.3 %copy-start.14 = (bf16[1,1024,1024]{2,1,0:T(8,128)(2,1)S(1)}, bf16[1,1024,1024]{2,1,0:T(8,128)(2,1)}, u32[]{:S(2)}) copy-start(bf16[1,1024,1024]{2,1,0:T(8,128)(2,1)} %param.31) | copy-start | bytes 6291460
  7.2 185.0 %all-gather.3.cloned.1.call-start = ((), (), s32[]{:S(2)}) async-start(), calls=%async_computation | async-start | bytes 8650752 | tf_op jit(solution)/shard_map/all_gather | solution.py:838
  9.6 191.7 %all-gather.5.cloned.1.call-start = ((), (), s32[]{:S(2)}) async-start(), calls=%async_computation.1 | async-start | bytes 8650752 | tf_op jit(solution)/shard_map/all_gather | solution.py:839
  67.4 4.9 copy-start.23
  67.4 4.9 %copy-start.30 = (bf16[4,4,2,32,1024]{4,3,2,1,0:T(8,128)(2,1)S(1)}, bf16[4,4,2,32,1024]{4,3,2,1,0:T(8,128)(2,1)}, u32[]{:S(2)}) copy-start(bf16[4,4,2,32,1024]{4,3,2,1,0:T(8,128)(2,1)} %get-tuple-element.92) | copy-start | bytes 6291460
  72.3 95.5 %copy-start.24 = (f32[1,1024]{1,0:T(1,128)}, f32[1,1024]{1,0:T(1,128)S(1)}, u32[]{:S(2)}) copy-start(f32[1,1024]{1,0:T(1,128)S(1)} %get-tuple-element.156.refs_10_) | copy-start | bytes 12292
  72.3 113.3 %copy-start.27 = (f32[1,1024]{1,0:T(1,128)}, f32[1,1024]{1,0:T(1,128)S(1)}, u32[]{:S(2)}) copy-start(f32[1,1024]{1,0:T(1,128)S(1)} %get-tuple-element.161.refs_10_) | copy-start | bytes 12292
  72.3 3.7 copy-start.31
  79.8 3.8 copy-start.6
  79.8 3.8 copy-start.7
  79.8 3.8 copy-start.8
  79.8 3.8 copy-start.9
  79.8 3.7 copy-start.10
  162.7 25.2 %copy-start.13 = (f32[1024,1024]{1,0:T(8,128)}, f32[1024,1024]{1,0:T(8,128)S(1)}, u32[]{:S(2)}) copy-start(f32[1024,1024]{1,0:T(8,128)S(1)} %get-tuple-element.176.refs_15_) | copy-start | bytes 12582916
  162.7 4.3 copy-start.20
  164.7 3.8 copy-start.17
  167.0 5.2 %copy-start.3 = (bf16[256,1024]{1,0:T(8,128)(2,1)}, bf16[256,1024]{1,0:T(8,128)(2,1)S(1)}, u32[]{:S(2)}) copy-start(bf16[256,1024]{1,0:T(8,128)(2,1)S(1)} %convolution_convert_fusion.1.k_ref.refs_1_) | copy-start | bytes 1572868
  167.8 4.4 copy-start.4
  172.2 15.6 %copy-start.2 = (bf16[1024,1024]{1,0:T(8,128)(2,1)}, bf16[1024,1024]{1,0:T(8,128)(2,1)S(1)}, u32[]{:S(2)}) copy-start(bf16[1024,1024]{1,0:T(8,128)(2,1)S(1)} %add_convert_fusion.q_ref.refs_0_) | copy-start | bytes 6291460
  172.2 13.4 %copy-start.15 = (bf16[1,1024,1024]{2,1,0:T(8,128)(2,1)S(1)}, bf16[1,1024,1024]{2,1,0:T(8,128)(2,1)}, u32[]{:S(2)}) copy-start(bf16[1,1024,1024]{2,1,0:T(8,128)(2,1)} %param.31) | copy-start | bytes 6291460
  172.2 15.6 %copy-start.32 = (bf16[4,4,2,32,1024]{4,3,2,1,0:T(8,128)(2,1)S(1)}, bf16[4,4,2,32,1024]{4,3,2,1,0:T(8,128)(2,1)}, u32[]{:S(2)}) copy-start(bf16[4,4,2,32,1024]{4,3,2,1,0:T(8,128)(2,1)} %get-tuple-element.100) | copy-start | bytes 6291460
  380.0 77.3 %copy-start.25 = (f32[8,1024]{1,0:T(8,128)S(1)}, f32[8,1024]{1,0:T(8,128)}, u32[]{:S(2)}) copy-start(f32[8,1024]{1,0:T(8,128)} %get-tuple-element.139) | copy-start | bytes 98308
  380.0 77.3 %copy-start.28 = (f32[8,1024]{1,0:T(8,128)S(1)}, f32[8,1024]{1,0:T(8,128)}, u32[]{:S(2)}) copy-start(f32[8,1024]{1,0:T(8,128)} %get-tuple-element.140) | copy-start | bytes 98308
  380.0 78.4 %copy-start.26 = (f32[1,4096]{1,0:T(1,128)S(1)}, f32[1,4096]{1,0:T(1,128)}, u32[]{:S(2)}) copy-start(f32[1,4096]{1,0:T(1,128)} %get-tuple-element.141) | copy-start | bytes 49156
  (11 other events, 26.7 us)
Sparse Core Ops, SparseCore 0:
  11.6 103.4 all-gather.2
  118.0 83.2 all-gather.4

commit v5 on v4

--- a/solution.py
+++ b/solution.py
@@ -162,18 +162,21 @@
     late_in=refs[:late_count]; refs=refs[late_count:]
     carried=4 if causal else 2
     before,starts=refs[:2],refs[2:2+carried]; refs=refs[2+carried:]
+    if causal: cross_sums,last_sums,wide=refs[:3]; refs=refs[3:]
     if causal: grad_out,sums_ref=refs[:2]; refs=refs[2:]
     else: grad_out,low_out,ctx_out,dec_ref,enc_ref,sums_ref=refs[:6]; refs=refs[6:]
     results=refs[:4]; refs=refs[4:]
     left=(None,None)
     if not causal: left=refs[:2]; refs=refs[2:]
     ends=refs[:carried]; refs=refs[carried:]
+    if causal: small_out=refs[0]; refs=refs[1:]
     late=refs[:late_count]; late_sem=refs[late_count]; refs=refs[late_count+1:]
     normed_t,source_t,whole_t,dq_all,dk_all,dv_all,dk_acc,dv_acc,out_part=refs[:9]; refs=refs[9:]
     low_all,ctx_all=(None,None) if causal else refs[:2]
     streams=refs if causal else refs[2:]
     half=STREAM
     earlier=streams[2*half:]; streams=streams[:2*half]
+    if causal: table,packed=earlier[-14:-12]; vector_scratch=earlier[-12:]; earlier=earlier[:-14]
     count=pairs if causal else pairs-CROSS_LATE
     before_late=CROSS_LATE if causal else FFN_LATE
     step=pl.program_id(0)
@@ -269,8 +272,27 @@
         if not causal:
             copies+=[pltpu.make_async_copy(low_all,low_out,late_sem.at[1]),pltpu.make_async_copy(ctx_all,ctx_out,late_sem.at[2])]
         for copy in copies: copy.start()
+        if causal:
+            for n,(ref,row) in enumerate([(sums_ref,r) for r in (3,4,0,1,2)]+[(cross_sums,r) for r in (3,4,0,1,2)]+[(last_sums,r) for r in (0,1,2)]):
+                table[n:n+1,:]=ref[row:row+1,:]
+            table[13:,:]=jnp.zeros((3,table.shape[1]),jnp.float32)
+            each=results[0].shape[0]
+            for n in range(8*depth):
+                at=n*each//128*128
+                turn=-n*each%128
+                tile=table[:,at:at+128]
+                dest=packed.at[n//(4*depth),n//(2*depth)%2,n//2%depth,n%2]
+                dest[...]=pltpu.roll(tile,turn,1) if turn else tile
+            def write_wide(n,value): packed.at[n//(4*depth),n//(2*depth)%2,n//2%depth,n%2][13:14,:]=value
+            shuffle(lambda t: wide[:,t*128:(t+1)*128],write_wide,pairs,8*depth,128//pairs)
+            def store_small(w,total): small_out[...]=total
+            small_begin,small_ticks,small_finish=reduce_plan([packed],store_small,vector_scratch,depth)
+            small_begin()
         for t in range(pairs+rows//strip,count+LAST_LAG): tick1(t); tick2(t); middle1(t); middle2(t)
         finish()
+        if causal:
+            for small_tick in small_ticks: small_tick()
+            small_finish()
         if not causal:
             memory_grad=dot(dk_all[...],late[1][...],NT)+dot(dv_all[...],late[2][...],NT)
             flag=jnp.where(flag_ref[0]==1,1.0,0.0)
@@ -279,7 +301,7 @@
             for n in range(CROSS_LATE): copies+=leave(n)
         for copy in copies: copy.wait()
 
-def sub_layer_back(q,k,v,g,ctx,lse,limit,flag,causal,normed,source,out_grad,gain,late,before,starts,depth,collective_id,block=256,width=64):
+def sub_layer_back(q,k,v,g,ctx,lse,limit,flag,causal,normed,source,out_grad,gain,late,before,starts,small,depth,collective_id,block=256,width=64):
     rows,d=q.shape; keys=k.shape[0]
     pairs=d//128; per=128//width
     each=d//(8*depth)
@@ -292,6 +314,7 @@
     in_specs=[spec(rows),spec(keys),spec(keys),spec(rows),spec(rows),pl.BlockSpec((1,per,rows),lambda i,a,b:(i,0,0))]
     in_specs+=[once((rows,d)),once(source.shape),once((rows,d)),pl.BlockSpec((rows,256),lambda i,a,b:(0,i//2)),once(gain.shape)]+[any_]*(len(late)+2)
     in_specs+=[pl.BlockSpec(a.shape,lambda i,a,b,n=a.ndim:(0,)*n,pipeline_mode=pl.Buffered(1)) for a in starts]
+    in_specs+=[once(a.shape) for a in small]
     out_specs=[any_]; out_shape=[shape(rows,f32)]
     scratch=[pltpu.VMEM(a.shape,a.dtype) for a in late]+[DMA((len(late)+2*CROSS_LATE,))]
     scratch+=[pltpu.VMEM((d,rows),bf),pltpu.VMEM((8,128) if causal else (d,keys),bf),pltpu.VMEM((d,rows),bf)]
@@ -307,9 +330,13 @@
         out_shape+=[jax.ShapeDtypeStruct((max(CROSS_LATE,1),2,2,depth,2,each,256),bf)]*2
     out_specs+=[pl.BlockSpec(a.shape,lambda i,a,b,n=a.ndim:(0,)*n) for a in starts]
     out_shape+=[jax.ShapeDtypeStruct(a.shape,a.dtype) for a in starts]
+    if causal:
+        out_specs+=[keep((16,128))]
+        out_shape+=[jax.ShapeDtypeStruct((16,128),f32)]
     scratch+=stream_scratch(each,256,depth)*2
     before_late=CROSS_LATE if causal else FFN_LATE
     if before_late: scratch+=reduce_scratch([before[w%2].shape[5:]+(bf,) for w in range(2*before_late)],depth)
+    if causal: scratch+=[pltpu.VMEM((16,d),f32),pltpu.VMEM((2,2,depth,2,16,128),f32)]+reduce_scratch([(16,128,f32)],depth)
     return pl.pallas_call(
         functools.partial(sub_layer_kernel,causal,block,width,pairs,depth),
         grid_spec=pltpu.PrefetchScalarGridSpec(num_scalar_prefetch=2,grid=(pairs,),in_specs=in_specs,out_specs=out_specs,scratch_shapes=scratch),
@@ -317,7 +344,7 @@
         compiler_params=pltpu.CompilerParams(vmem_limit_bytes=62*MIB,collective_id=collective_id,has_side_effects=True),
         cost_estimate=pl.CostEstimate(flops=20*rows*keys*d,bytes_accessed=20*rows*d*2,transcendentals=rows*keys*16),
         name="self_back" if causal else "cross_back",
-    )(limit,flag,q,k,v,g,ctx,lse,normed,source,ctx,out_grad,gain,*late,*before,*starts)
+    )(limit,flag,q,k,v,g,ctx,lse,normed,source,ctx,out_grad,gain,*late,*before,*starts,*small)
 
 MESH=pl.DeviceIdType.MESH
 DMA=pltpu.SemaphoreType.DMA
@@ -554,7 +581,7 @@
 
 def stream_scratch(rows,cols,depth):
     vmem=lambda *lead: pltpu.VMEM(lead+(rows,cols),jnp.bfloat16)
-    return [vmem(2,2,2,depth,2),vmem(SLOTS,2,2,depth),vmem(SLOTS,2,2,depth),vmem(SLOTS,2,depth),vmem(SLOTS,2,depth),vmem(SLOTS,depth),vmem(SLOTS,depth),vmem(SLOTS,depth-1),
+    return [vmem(2,2,2,depth,2),vmem(2,2,2,depth),vmem(2,2,2,depth),vmem(SLOTS,2,depth),vmem(SLOTS,2,depth),vmem(SLOTS,depth),vmem(SLOTS,depth),vmem(SLOTS,depth-1),
       DMA((SLOTS,)),DMA((SLOTS,)),DMA((SLOTS,2)),DMA((SLOTS,2)),DMA((SLOTS,depth-1)),DMA((SLOTS,depth-1))]
 
 def stream_plan(count,odd,store,scratch,depth):
@@ -566,10 +593,11 @@
     def slot(i): return lax.rem(i,SLOTS)
     def core(i):
         s=slot(i)
-        return pltpu.make_async_remote_copy(made.at[lax.rem(i,2),:,:,:,1-c],r0.at[s],c_send.at[s],c_recv.at[s],(dp,z*2+1-c),MESH)
+        return pltpu.make_async_remote_copy(made.at[lax.rem(i,2),:,:,:,1-c],r0.at[lax.rem(i,2)],c_send.at[s],c_recv.at[s],(dp,z*2+1-c),MESH)
     def first(i):
         s=slot(i)
-        src=sum0.at[s,there] if odd else sum0.at[s,:,there]
+        m=lax.rem(i,2)
+        src=sum0.at[m,there] if odd else sum0.at[m,:,there]
         return pltpu.make_async_remote_copy(src,r1.at[s],a_send.at[s,0],a_recv.at[s,0],(turned(dp,2 if odd else 1),fs),MESH)
     def second(i):
         s=slot(i)
@@ -578,16 +606,16 @@
         s=slot(i)
         return pltpu.make_async_remote_copy(sum2.at[s,lax.rem(z+k,depth)],r3.at[s,k-1],z_send.at[s,k-1],z_recv.at[s,k-1],(dp,lax.rem(z+k,depth)*2+c),MESH)
     def step0(i):
-        s=slot(i); m=lax.rem(i,2)
+        m=lax.rem(i,2)
         core(i).wait()
         for a in range(4):
-            sum0[s,a//2,a%2]=made[m,a//2,a%2,:,c]+r0[s,a//2,a%2]
+            sum0[m,a//2,a%2]=made[m,a//2,a%2,:,c]+r0[m,a//2,a%2]
         first(i).start()
     def step1(i):
-        s=slot(i)
+        s=slot(i); m=lax.rem(i,2)
         first(i).wait()
         for a in range(2):
-            sum1[s,a]=(sum0[s,here,a] if odd else sum0[s,a,here])+r1[s,a]
+            sum1[s,a]=(sum0[m,here,a] if odd else sum0[m,a,here])+r1[s,a]
         second(i).start()
     def step2(i):
         s=slot(i)
@@ -671,11 +699,11 @@
 FFN_LATE=0
 CROSS_LATE=0
 
-def ffn_kernel(strip, steps, depth, length_ref, after_ref, cot_ref, w1_ref, w2_ref, b1_ref, vec_ref, wo_ref,
-               mixed_ref, grad_ref, low_ref, ctx_ref, dw1_ref, dw2_ref, db1_ref, dvec_ref, late1_ref, late2_ref, n3, n3t, gf, branch, gn, wo, sem, *refs):
+def ffn_kernel(strip, steps, depth, length_ref, n3, n3t, gf, after_in, cot_in, w1_ref, w2_ref, b1_ref, vec_ref, wo_ref,
+               mixed_ref, grad_ref, low_ref, ctx_ref, dw1_ref, dw2_ref, db1_ref, dvec_ref, late1_ref, late2_ref, mixed, ctx, after_ref, cot_ref, branch, gn, wo, sem, *refs):
     j=pl.program_id(0)
     rows,d=after_ref.shape
-    gain,shift,b2=vec_ref[0:1,:],vec_ref[1:2,:],vec_ref[2:3,:]
+    gain,b2=vec_ref[0:1,:],vec_ref[2:3,:]
     def live(r):
         return (r*strip+lax.broadcasted_iota(jnp.int32,(strip,1),0)<length_ref[0]).astype(jnp.float32)
     if depth:
@@ -692,16 +720,10 @@
     def _():
         if depth: greet(depth)
         pltpu.make_async_copy(wo_ref,wo,sem.at[2]).start()
-        def one(r,total):
-            sl=pl.ds(r*strip,strip)
-            hat,_=normal(after_ref[sl,:])
-            n3[sl,:]=(hat*gain+shift).astype(jnp.bfloat16)
-            top=(cot_ref[sl,:].astype(jnp.float32)*live(r)).astype(jnp.bfloat16)
-            gf[sl,:]=top
-            return total+jnp.sum(top.astype(jnp.float32),axis=0,keepdims=True)
+        pltpu.make_async_copy(after_in,after_ref,sem.at[0]).start()
+        pltpu.make_async_copy(cot_in,cot_ref,sem.at[1]).start()
         dvec_ref[...]=jnp.zeros_like(dvec_ref)
-        dvec_ref[2:3,:]=lax.fori_loop(0,rows//strip,one,jnp.zeros((1,d),jnp.float32))
-        n3t[...]=jnp.transpose(n3[...])
+        dvec_ref[2:3,:]=jnp.sum(gf[...].astype(jnp.float32),axis=0,keepdims=True)
         branch[...]=jnp.zeros_like(branch); gn[...]=jnp.zeros_like(gn)
     if depth:
         tick1(j); tick2(j)
@@ -738,23 +760,25 @@
             sl=pl.ds(r*strip,strip)
             valid=live(r)
             after=after_ref[sl,:]
-            n3[sl,:]=((after+(branch[sl,:]+b2))*valid).astype(jnp.bfloat16)
+            mixed[sl,:]=((after+(branch[sl,:]+b2))*valid).astype(jnp.bfloat16)
             hat,inverse=normal(after)
             grad=gn[sl,:]
             dvec_ref[0:1,:]+=jnp.sum(grad*hat,axis=0,keepdims=True)
             dvec_ref[1:2,:]+=jnp.sum(grad,axis=0,keepdims=True)
             grad=cot_ref[sl,:].astype(jnp.float32)*valid+pull_norm(hat,inverse,gain,grad)
             gn[sl,:]=grad
-            gf[sl,:]=grad.astype(jnp.bfloat16)
-            n3t[sl,:]=dot(gf[sl,:],wo[...],NT).astype(jnp.bfloat16)
+            cot_ref[sl,:]=grad.astype(jnp.bfloat16)
+            ctx[sl,:]=dot(cot_ref[sl,:],wo[...],NT).astype(jnp.bfloat16)
         pltpu.make_async_copy(wo_ref,wo,sem.at[2]).wait()
+        pltpu.make_async_copy(after_in,after_ref,sem.at[0]).wait()
+        pltpu.make_async_copy(cot_in,cot_ref,sem.at[1]).wait()
         for r in range(rows//strip):
             if depth and r%2==0:
                 tick1(steps+r//2); tick2(steps+r//2)
             one(r)
             if depth and r%2==0:
                 middle1(steps+r//2); middle2(steps+r//2)
-        copies=[pltpu.make_async_copy(a,b,sem.at[n]) for n,(a,b) in enumerate(((n3,mixed_ref),(gn,grad_ref),(gf,low_ref),(n3t,ctx_ref)))]
+        copies=[pltpu.make_async_copy(a,b,sem.at[n]) for n,(a,b) in enumerate(((mixed,mixed_ref),(gn,grad_ref),(cot_ref,low_ref),(ctx,ctx_ref)))]
         for copy in copies: copy.start()
         if depth:
             for t in range(steps+rows//strip//2,steps-FFN_LATE+LAST_LAG):
@@ -762,7 +786,7 @@
             for n in range(FFN_LATE): copies+=leave(n)
         for copy in copies: copy.wait()
 
-def feed_forward(after,cot,length,w1,w2,b1,vec,wo,block=512,strip=128,depth=0,collective_id=None):
+def feed_forward(ready,after,cot,length,w1,w2,b1,vec,wo,block=512,strip=128,depth=0,collective_id=None):
     rows,d=after.shape; ff=w1.shape[1]
     steps=ff//block
     once=lambda shape: pl.BlockSpec(shape,lambda j,n:(0,0),pipeline_mode=pl.Buffered(1))
@@ -771,7 +795,7 @@
     wide=pl.BlockSpec((d,block),lambda j,n:(0,j)); line=pl.BlockSpec((1,block),lambda j,n:(0,j))
     tall=pl.BlockSpec((w2.shape[0],block//w2.shape[0],d),lambda j,n:(0,j,0))
     bf=jnp.bfloat16; f32=jnp.float32
-    scratch=[pltpu.VMEM((rows,d),bf),pltpu.VMEM((d,rows),bf),pltpu.VMEM((rows,d),bf),pltpu.VMEM((rows,d),f32),pltpu.VMEM((rows,d),f32),pltpu.VMEM((d,d),bf),DMA((4+2*FFN_LATE,))]
+    scratch=[pltpu.VMEM((rows,d),bf),pltpu.VMEM((rows,d),bf),pltpu.VMEM((rows,d),f32),pltpu.VMEM((rows,d),bf),pltpu.VMEM((rows,d),f32),pltpu.VMEM((rows,d),f32),pltpu.VMEM((d,d),bf),DMA((4+2*FFN_LATE,))]
     if depth:
         each=d//(8*depth); part=block//(8*depth)
         grad_specs=[keep((each,ff)),keep((steps,part,d))]
@@ -786,14 +810,14 @@
         functools.partial(ffn_kernel,strip,steps,depth),
         grid_spec=pltpu.PrefetchScalarGridSpec(
             num_scalar_prefetch=1,grid=(steps,),
-            in_specs=[once((rows,d)),once((rows,d)),wide,tall,line,once(vec.shape),any_],
+            in_specs=[once((rows,d)),once((d,rows)),once((rows,d)),any_,any_,wide,tall,line,once(vec.shape),any_],
             out_specs=[any_]*4+grad_specs+[line,keep((8,d)),any_,any_],
             scratch_shapes=scratch),
         out_shape=[jax.ShapeDtypeStruct((rows,d),bf),jax.ShapeDtypeStruct((rows,d),f32)]+[jax.ShapeDtypeStruct((rows,d),bf)]*2+grad_shapes+[jax.ShapeDtypeStruct((1,ff),f32),jax.ShapeDtypeStruct((8,d),f32)]+late_shapes,
         compiler_params=pltpu.CompilerParams(vmem_limit_bytes=62*MIB,collective_id=collective_id,has_side_effects=depth>0),
         cost_estimate=pl.CostEstimate(flops=12*rows*d*ff,bytes_accessed=4*d*ff*2+rows*d*12,transcendentals=rows*ff),
         name="feed_forward",
-    )(length,after,cot,w1,w2,b1,vec,wo)
+    )(length,*ready,after,cot,w1,w2,b1,vec,wo)
 
 AXES=("dp","fsdp")
 
@@ -858,21 +882,25 @@
     cq=low(dot(n2,cwq)+cbq); ck=low(dot(memory,cwk)); cv=low(dot(memory,cwv)+cbv)
     cctx,clse,_=flash_fwd(cq,ck,cv,text_len,False)
     after_cross=after_self+(dot(cctx,cwo)+cbo)
+    n3=low(layer_norm(after_cross,g3,s3))
+    valid=(jnp.arange(units.shape[0],dtype=jnp.int32)<unit_len[0]).astype(jnp.float32)[:,None]
+    gf=low(cotangent[0].astype(jnp.float32)*valid)
+    ready=(n3,n3.T,gf)
     last=jnp.concatenate([vectors[10:13],jnp.zeros((5,1024),jnp.float32)])
     if depth:
-        mixed,g_cross,gc,g_cctx,dw1,dw2,db1,dvec,*before=feed_forward(after_cross,cotangent[0],unit_len,w1,w2.reshape(devices,4*each,1024),b1,last,cwo,depth=depth,collective_id=3)
-        db1=db1.reshape(steps,devices,part).transpose(1,0,2)
+        mixed,g_cross,gc,g_cctx,dw1,dw2,db1,dvec,*before=feed_forward(ready,after_cross,cotangent[0],unit_len,w1,w2.reshape(devices,4*each,1024),b1,last,cwo,depth=depth,collective_id=3)
     else:
-        mixed,g_cross,gc,g_cctx,dw1,dw2,db1,dvec,*_=feed_forward(after_cross,cotangent[0],unit_len,w1,w2[None],b1,last,cwo)
+        mixed,g_cross,gc,g_cctx,dw1,dw2,db1,dvec,*_=feed_forward(ready,after_cross,cotangent[0],unit_len,w1,w2[None],b1,last,cwo)
         dw1,dw2=reduce_all([dw1,dw2[0]])
     gain1,gain2=vectors[0:1],vectors[5:6]
     if depth:
         g_self,gs,g_ctx,g_dec,g_enc,csums,*starts,left1,left2,dw1,dw2=sub_layer_back(
-            cq,ck,cv,g_cctx,cctx,clse,text_len,task_flag,False,n2,memory,gc,gain2,[cwq,cwk,cwv,wo,after_self,g_cross],before,[dw1,dw2],depth,4)
+            cq,ck,cv,g_cctx,cctx,clse,text_len,task_flag,False,n2,memory,gc,gain2,[cwq,cwk,cwv,wo,after_self,g_cross],before,[dw1,dw2],[],depth,4)
         dw2=dw2.reshape(4*each,1024)
-        g_units,sums,dwq,dwk,dwv,dwo,dcwq,dcwk,dcwv,dcwo=sub_layer_back(
-            q,k,v,g_ctx,ctx,lse,text_len,task_flag,True,n1,memory,gs,gain1,[wq,wk,wv,unit_states[0],g_self],[left1,left2],starts,depth,5)
-        small_grads=[sums[3],sums[4],sums[0],sums[1],sums[2],csums[3],csums[4],csums[0],csums[1],csums[2],dvec[0],dvec[1],dvec[2]]
+        g_units,sums,dwq,dwk,dwv,dwo,dcwq,dcwk,dcwv,dcwo,grads=sub_layer_back(
+            q,k,v,g_ctx,ctx,lse,text_len,task_flag,True,n1,memory,gs,gain1,[wq,wk,wv,unit_states[0],g_self],[left1,left2],starts,[csums,dvec,db1],depth,5)
+        ng=[grads[i,:each] for i in range(13)]
+        db1=grads[13]
     else:
         gcq,gck,gcv=flash_bwd(cq,ck,cv,g_cctx,cctx,clse,text_len,False)
         dcwq,dcwk,dcwv,dcwo=reduce_all([low(dot(n2,gcq,TN)),low(dot(memory,gck,TN)),low(dot(memory,gcv,TN)),low(dot(cctx,gc,TN))])
@@ -887,11 +915,10 @@
         is_dec=(task_flag[0]==1).astype(jnp.float32)
         g_dec,g_enc=g_memory*is_dec,g_memory*(1.0-is_dec)
         small_grads=[dg1,ds1,columns(gq),columns(gv),columns(gs),dg2,ds2,columns(gcq),columns(gcv),columns(gc),dvec[0],dvec[1],dvec[2]]
-    grads=pack_grads(small_grads,db1,devices)
-    grads,=reduce_rows([grads],depth,6) if depth else reduce_all([grads])
-    grads=grads.reshape(1024)
-    ng=[grads[i*each:(i+1)*each] for i in range(13)]
-    db1=grads[13*each:17*each]
+        grads,=reduce_all([pack_grads(small_grads,db1,devices)])
+        grads=grads.reshape(1024)
+        ng=[grads[i*each:(i+1)*each] for i in range(13)]
+        db1=grads[13*each:17*each]
     if depth:
         dw1,mixed,g_units,g_dec,g_enc,dwq,dwk,dwv,dwo,dcwq,dcwk,dcwv,dcwo,dw2=deliver(
             [dw1,mixed,g_units,g_dec,g_enc,dwq,dwk,dwv,dwo,dcwq,dcwk,dcwv,dcwo,dw2],devices,steps)

time: 495 us -> 487 us (0.984)
  waiting for transfers between devices: 9.84 us -> 1.36 us
    pallas_call x1 -> x0, Pallas kernels: 12.9 us -> none  [reduce_rows(): pl.pallas_call(functools.partial(last_kernel, count, depth), in_specs=[pl...]
    pallas_call x2, Pallas kernels: 138 us -> 150 us  [sub_layer_back(): pl.pallas_call(functools.partial(sub_layer_kernel, causal, block, width,...]
    all_gather x1, waiting for transfers between devices: 9.13 us -> 0.65 us  [shards(): w2 = lax.all_gather(ffn_w2, AXES, axis=0, tiled=True)]
  transfers between devices with their start and end apart: 2 -> 2, of which waited for: 1 -> 1; matrix products, arithmetic and copies ran while one was open for 6% -> 7% of each run, Pallas kernels for 30% -> 30%
where the time goes in v5:
time: 487 us; the launch traced here: 484 us
  Pallas kernels  422 us (87%)
  matrix products  19.8 us (4%)
  between operations  16.7 us (3%)
  local copies, waits for them, and re-layouts  15.3 us (3%)
  other arithmetic  9.3 us (2%)
    pallas_call x2, Pallas kernels, sub_layer_back(): pl.pallas_call(functools.partial(sub_layer_kernel, causal, block, width,...  150 us
    pallas_call x1, Pallas kernels, feed_forward(): pl.pallas_call(functools.partial(ffn_kernel, strip, steps, depth), grid_s...  114 us
    pallas_call x2, Pallas kernels, flash_fwd(): pl.pallas_call(functools.partial(fwd_kernel, causal, block, width, count,...  88.4 us
    pallas_call x1, Pallas kernels, gather_first(): pl.pallas_call(functools.partial(first_kernel, count, lines, depth, block...  57.6 us
    dot_general x8, matrix products, dot(): return lax.dot_general(a, b, dims, preferred_element_type=jnp.float32)  19.8 us
  transfers between devices with their start and end apart: 2, of which 1 were waited for; matrix products, arithmetic and copies ran while one was open for 7% of the time, Pallas kernels for 30%

profile of v5, /device:TPU:0, one launch (start us, length us, event | category | flops | bytes accessed | tf_op | source)
XLA Modules:
  0.0 484.4 jit_solution(12966102890336629785)
XLA Ops:
  7.3 2.3 order_columns.1
  12.3 57.6 %gather_first.1 = (bf16[4,4,2,32,1024]{4,3,2,1,0:T(8,128)(2,1)}, bf16[4,4,2,32,1024]{4,3,2,1,0:T(8,128)(2,1)}, bf16[4,4,2,32,1024]{4,3,2,1,0:T(8,128)(2,1)}, f32[16,1024]{1,0:T(8,128)}, f32[1,4096]{1,0:T(1,128)}) custom-call(bf16[32,1024]{1,0:T(8,128)(2,1)} %refs_0_.2, bf16[32,1024]{1,0:T(8,128)(2,1)} %refs_1_.2, bf16[32,1024]{1,0:T(8,128)(2,1)} %refs_2_.2, ...), custom_call_target="tpu_custom_call" | custom-call | tf_op jit(solution)/shard_map/gather_first/pallas_call | solution.py:544
  69.9 0.9 slice.95
  70.8 1.9 convert_reduce_fusion
  73.6 3.7 convolution_convert_fusion.k_ref.refs_1_
  77.3 3.7 add_convert_fusion.3.v_ref.refs_2_
  81.1 3.7 add_convert_fusion.4.q_ref.refs_0_
  84.8 75.1 %attend_causal.1 = (bf16[1024,1024]{1,0:T(8,128)(2,1)S(1)}, f32[8,2,1024]{2,1,0:T(2,128)S(1)}, bf16[4,4,2,32,1024]{4,3,2,1,0:T(8,128)(2,1)S(1)}, bf16[4,4,2,32,1...) custom-call(s32[1]{0:T(128)S(6)} %copy.65.lim_ref, ...), custom_call_target="tpu_custom_call" | custom-call | flops 2147483648 | bytes 8388608 | tf_op jit(solution)/shard_map/attend_causal/pallas_call | solution.py:82
  159.9 2.5 fusion.13
  164.5 1.6 copy-done.21
  168.3 1.3 copy-done.17
  169.6 2.3 add_convert_fusion.1.q_ref.refs_0_
  171.9 13.4 %attend_text.1 = (bf16[1024,1024]{1,0:T(8,128)(2,1)S(1)}, f32[8,2,1024]{2,1,0:T(2,128)S(1)}) custom-call(s32[1]{0:T(128)S(6)} %copy.65.lim_ref, bf16[1024,1024]{1,0:T(8,128)(2,1)S(1)} %add_convert_fusion.1.q_ref.refs_0_, bf16[256,1024]{1,0:T(8,128)(2,1)S(1)} %convolution_convert_fusion.1.k_ref.refs_1_, bf16[256,1024]{1,0:T(8,128)(2,1)S(1)} %fusion.7.v_ref.refs_2_), custom_call_target="tpu_custom_call" | custom-call | flops 1073741824 | bytes 8388608 | tf_op jit(solution)/shard_map/attend_text/pallas_call | solution.py:82
  185.4 2.4 fusion.14
  188.4 2.5 copy-done.19
  191.0 2.6 multiply_convert_fusion
  193.5 4.1 copy.61.n3t
  198.3 2.2 fusion.5.refs_6_
  201.1 114.1 %feed_forward.1 = (bf16[1024,1024]{1,0:T(8,128)(2,1)}, f32[1024,1024]{1,0:T(8,128)}, bf16[1024,1024]{1,0:T(8,128)(2,1)}, bf16[1024,1024]{1,0:T(8,128)(2,1)}, f32...) custom-call(s32[1]{0:T(128)} %copy.64.length_ref, ...), custom_call_target="tpu_custom_call" | custom-call | flops 51539607552 | bytes 46137344 | tf_op jit(solution)/shard_map/feed_forward/pallas_call | solution.py:809
  315.2 64.2 %cross_back.1 = (f32[1024,1024]{1,0:T(8,128)}, bf16[1024,1024]{1,0:T(8,128)(2,1)}, bf16[1024,1024]{1,0:T(8,128)(2,1)}, f32[256,1024]{1,0:T(8,128)}, f32[256,1024...) custom-call(s32[1]{0:T(128)S(6)} %copy.65.lim_ref, ...), custom_call_target="tpu_custom_call" | custom-call | flops 5368709120 | bytes 41943040 | tf_op jit(solution)/shard_map/cross_back/pallas_call | solution.py:340
  379.4 85.7 %self_back.1 = (f32[1024,1024]{1,0:T(8,128)}, f32[8,1024]{1,0:T(8,128)}, f32[32,1024]{1,0:T(8,128)}, f32[32,1024]{1,0:T(8,128)}, f32[32,1024]{1,0:T(8,128)}, /*i...) custom-call(s32[1]{0:T(128)S(6)} %copy.65.lim_ref, ...), custom_call_target="tpu_custom_call" | custom-call | flops 21474836480 | bytes 41943040 | tf_op jit(solution)/shard_map/self_back/pallas_call | solution.py:340
  465.1 1.5 slice_bitcast_fusion
  466.6 1.2 slice_bitcast_fusion.1
  467.8 9.5 %deliver.1 = (f32[32,4096]{1,0:T(8,128)}, bf16[1024,1024]{1,0:T(8,128)(2,1)}, f32[1024,1024]{1,0:T(8,128)}, f32[256,1024]{1,0:T(8,128)}, f32[256,1024]{1,0:T(8,1...) custom-call(f32[32,4096]{1,0:T(8,128)} %get-tuple-element.110.refs_0, ...), custom_call_target="tpu_custom_call" | custom-call | tf_op jit(solution)/shard_map/deliver/pallas_call | solution.py:666
  (83 shorter events, 7.7 us)
Async XLA Ops:
  7.2 65.6 %copy-start.14 = (bf16[1,1024,1024]{2,1,0:T(8,128)(2,1)S(1)}, bf16[1,1024,1024]{2,1,0:T(8,128)(2,1)}, u32[]{:S(2)}) copy-start(bf16[1,1024,1024]{2,1,0:T(8,128)(2,1)} %param.31) | copy-start | bytes 6291460
  7.2 193.2 %all-gather.3.cloned.1.call-start = ((), (), s32[]{:S(2)}) async-start(), calls=%async_computation | async-start | bytes 8650752 | tf_op jit(solution)/shard_map/all_gather | solution.py:862
  9.6 191.5 %all-gather.5.cloned.1.call-start = ((), (), s32[]{:S(2)}) async-start(), calls=%async_computation.1 | async-start | bytes 8650752 | tf_op jit(solution)/shard_map/all_gather | solution.py:863
  69.9 3.6 copy-start.25
  69.9 3.7 copy-start.29
  73.6 94.0 %copy-start.26 = (f32[1,1024]{1,0:T(1,128)}, f32[1,1024]{1,0:T(1,128)S(1)}, u32[]{:S(2)}) copy-start(f32[1,1024]{1,0:T(1,128)S(1)} %get-tuple-element.158.refs_10_) | copy-start | bytes 12292
  73.6 124.7 %copy-start.27 = (f32[1,1024]{1,0:T(1,128)}, f32[1,1024]{1,0:T(1,128)S(1)}, u32[]{:S(2)}) copy-start(f32[1,1024]{1,0:T(1,128)S(1)} %get-tuple-element.163.refs_10_) | copy-start | bytes 12292
  73.6 3.7 copy-start.30
  77.3 3.7 copy-start.28
  81.0 3.8 copy-start.6
  81.0 3.8 copy-start.7
  81.0 3.8 copy-start.8
  81.1 3.8 copy-start.9
  81.1 3.7 copy-start.10
  162.4 22.9 %copy-start.13 = (f32[1024,1024]{1,0:T(8,128)}, f32[1024,1024]{1,0:T(8,128)S(1)}, u32[]{:S(2)}) copy-start(f32[1024,1024]{1,0:T(8,128)S(1)} %get-tuple-element.178.refs_15_) | copy-start | bytes 12582916
  162.4 3.6 copy-start.21
  162.5 4.3 copy-start.22
  164.5 3.8 copy-start.18
  166.8 5.2 %copy-start.3 = (bf16[256,1024]{1,0:T(8,128)(2,1)}, bf16[256,1024]{1,0:T(8,128)(2,1)S(1)}, u32[]{:S(2)}) copy-start(bf16[256,1024]{1,0:T(8,128)(2,1)S(1)} %convolution_convert_fusion.1.k_ref.refs_1_) | copy-start | bytes 1572868
  167.5 4.4 copy-start.4
  171.9 15.9 %copy-start.2 = (bf16[1024,1024]{1,0:T(8,128)(2,1)}, bf16[1024,1024]{1,0:T(8,128)(2,1)S(1)}, u32[]{:S(2)}) copy-start(bf16[1024,1024]{1,0:T(8,128)(2,1)S(1)} %add_convert_fusion.1.q_ref.refs_0_) | copy-start | bytes 6291460
  171.9 13.4 %copy-start.31 = (bf16[4,4,2,32,1024]{4,3,2,1,0:T(8,128)(2,1)S(1)}, bf16[4,4,2,32,1024]{4,3,2,1,0:T(8,128)(2,1)}, u32[]{:S(2)}) copy-start(bf16[4,4,2,32,1024]{4,3,2,1,0:T(8,128)(2,1)} %get-tuple-element.100) | copy-start | bytes 6291460
  187.8 5.7 %copy-start.16 = (f32[1024,1024]{1,0:T(8,128)}, f32[1024,1024]{1,0:T(8,128)S(1)}, u32[]{:S(2)}) copy-start(f32[1024,1024]{1,0:T(8,128)S(1)} %get-tuple-element.180.after_in) | copy-start | bytes 12582916
  193.5 4.7 copy-start.15
  (10 other events, 23.1 us)
Sparse Core Ops, SparseCore 0:
  11.6 104.0 all-gather.2
  118.7 82.3 all-gather.4

commit v6 on v5

--- a/solution.py
+++ b/solution.py
@@ -364,8 +364,8 @@
         pl.semaphore_signal(barrier,inc=1,device_id=device,device_id_type=MESH)
     pl.semaphore_wait(barrier,len(partners))
 
-PIECES=2
-AHEAD=2
+PIECES=4
+AHEAD=1
 
 def gather_sems(count,depth):
     count=PIECES*count

time: 487 us -> 483 us (level)
  Pallas kernels: 422 us -> 413 us
  transfers between devices with their start and end apart: 2 -> 2, of which waited for: 1 -> 1; matrix products, arithmetic and copies ran while one was open for 7% -> 7% of each run, Pallas kernels for 30% -> 29%
where the time goes in v6:
time: 483 us; the launch traced here: 476 us
  Pallas kernels  413 us (86%)
  matrix products  19.8 us (4%)
  between operations  16.7 us (3%)
  local copies, waits for them, and re-layouts  15.3 us (3%)
  other arithmetic  9.3 us (2%)
    pallas_call x2, Pallas kernels, sub_layer_back(): pl.pallas_call(functools.partial(sub_layer_kernel, causal, block, width,...  150 us
    pallas_call x1, Pallas kernels, feed_forward(): pl.pallas_call(functools.partial(ffn_kernel, strip, steps, depth), grid_s...  113 us
    pallas_call x2, Pallas kernels, flash_fwd(): pl.pallas_call(functools.partial(fwd_kernel, causal, block, width, count,...  85.3 us
    pallas_call x1, Pallas kernels, gather_first(): pl.pallas_call(functools.partial(first_kernel, count, lines, depth, block...  53.3 us
    dot_general x8, matrix products, dot(): return lax.dot_general(a, b, dims, preferred_element_type=jnp.float32)  19.8 us
  transfers between devices with their start and end apart: 2, of which 1 were waited for; matrix products, arithmetic and copies ran while one was open for 7% of the time, Pallas kernels for 29%

profile of v6, /device:TPU:0, one launch (start us, length us, event | category | flops | bytes accessed | tf_op | source)
XLA Modules:
  0.0 476.2 jit_solution(3880493806555744045)
XLA Ops:
  7.3 2.3 order_columns.1
  12.3 53.3 %gather_first.1 = (bf16[4,4,2,32,1024]{4,3,2,1,0:T(8,128)(2,1)}, bf16[4,4,2,32,1024]{4,3,2,1,0:T(8,128)(2,1)}, bf16[4,4,2,32,1024]{4,3,2,1,0:T(8,128)(2,1)}, f32[16,1024]{1,0:T(8,128)}, f32[1,4096]{1,0:T(1,128)}) custom-call(bf16[32,1024]{1,0:T(8,128)(2,1)} %refs_0_.2, bf16[32,1024]{1,0:T(8,128)(2,1)} %refs_1_.2, bf16[32,1024]{1,0:T(8,128)(2,1)} %refs_2_.2, ...), custom_call_target="tpu_custom_call" | custom-call | tf_op jit(solution)/shard_map/gather_first/pallas_call | solution.py:544
  66.5 1.9 convert_reduce_fusion
  69.3 3.7 convolution_convert_fusion.k_ref.refs_1_
  73.0 3.7 add_convert_fusion.3.v_ref.refs_2_
  76.8 3.7 add_convert_fusion.4.q_ref.refs_0_
  80.5 71.9 %attend_causal.1 = (bf16[1024,1024]{1,0:T(8,128)(2,1)S(1)}, f32[8,2,1024]{2,1,0:T(2,128)S(1)}, bf16[4,4,2,32,1024]{4,3,2,1,0:T(8,128)(2,1)S(1)}, bf16[4,4,2,32,1...) custom-call(s32[1]{0:T(128)S(6)} %copy.65.lim_ref, ...), custom_call_target="tpu_custom_call" | custom-call | flops 2147483648 | bytes 8388608 | tf_op jit(solution)/shard_map/attend_causal/pallas_call | solution.py:82
  152.5 2.5 fusion.13
  157.0 1.6 copy-done.21
  160.8 1.3 copy-done.17
  162.1 2.3 add_convert_fusion.1.q_ref.refs_0_
  164.5 13.4 %attend_text.1 = (bf16[1024,1024]{1,0:T(8,128)(2,1)S(1)}, f32[8,2,1024]{2,1,0:T(2,128)S(1)}) custom-call(s32[1]{0:T(128)S(6)} %copy.65.lim_ref, bf16[1024,1024]{1,0:T(8,128)(2,1)S(1)} %add_convert_fusion.1.q_ref.refs_0_, bf16[256,1024]{1,0:T(8,128)(2,1)S(1)} %convolution_convert_fusion.1.k_ref.refs_1_, bf16[256,1024]{1,0:T(8,128)(2,1)S(1)} %fusion.7.v_ref.refs_2_), custom_call_target="tpu_custom_call" | custom-call | flops 1073741824 | bytes 8388608 | tf_op jit(solution)/shard_map/attend_text/pallas_call | solution.py:82
  177.9 2.4 fusion.14
  181.0 2.5 copy-done.19
  183.5 2.6 multiply_convert_fusion
  186.1 4.1 copy.61.n3t
  190.8 2.2 fusion.5.refs_6_
  193.0 1.7 all-gather.5.cloned.1.call-done
  194.7 112.7 %feed_forward.1 = (bf16[1024,1024]{1,0:T(8,128)(2,1)}, f32[1024,1024]{1,0:T(8,128)}, bf16[1024,1024]{1,0:T(8,128)(2,1)}, bf16[1024,1024]{1,0:T(8,128)(2,1)}, f32...) custom-call(s32[1]{0:T(128)} %copy.64.length_ref, ...), custom_call_target="tpu_custom_call" | custom-call | flops 51539607552 | bytes 46137344 | tf_op jit(solution)/shard_map/feed_forward/pallas_call | solution.py:809
  307.4 65.4 %cross_back.1 = (f32[1024,1024]{1,0:T(8,128)}, bf16[1024,1024]{1,0:T(8,128)(2,1)}, bf16[1024,1024]{1,0:T(8,128)(2,1)}, f32[256,1024]{1,0:T(8,128)}, f32[256,1024...) custom-call(s32[1]{0:T(128)S(6)} %copy.65.lim_ref, ...), custom_call_target="tpu_custom_call" | custom-call | flops 5368709120 | bytes 41943040 | tf_op jit(solution)/shard_map/cross_back/pallas_call | solution.py:340
  372.8 84.1 %self_back.1 = (f32[1024,1024]{1,0:T(8,128)}, f32[8,1024]{1,0:T(8,128)}, f32[32,1024]{1,0:T(8,128)}, f32[32,1024]{1,0:T(8,128)}, f32[32,1024]{1,0:T(8,128)}, /*i...) custom-call(s32[1]{0:T(128)S(6)} %copy.65.lim_ref, ...), custom_call_target="tpu_custom_call" | custom-call | flops 21474836480 | bytes 41943040 | tf_op jit(solution)/shard_map/self_back/pallas_call | solution.py:340
  456.9 1.5 slice_bitcast_fusion
  458.4 1.2 slice_bitcast_fusion.1
  459.6 9.5 %deliver.1 = (f32[32,4096]{1,0:T(8,128)}, bf16[1024,1024]{1,0:T(8,128)(2,1)}, f32[1024,1024]{1,0:T(8,128)}, f32[256,1024]{1,0:T(8,128)}, f32[256,1024]{1,0:T(8,1...) custom-call(f32[32,4096]{1,0:T(8,128)} %get-tuple-element.110.refs_0, ...), custom_call_target="tpu_custom_call" | custom-call | tf_op jit(solution)/shard_map/deliver/pallas_call | solution.py:666
  (83 shorter events, 7.9 us)
Async XLA Ops:
  7.2 61.3 %copy-start.14 = (bf16[1,1024,1024]{2,1,0:T(8,128)(2,1)S(1)}, bf16[1,1024,1024]{2,1,0:T(8,128)(2,1)}, u32[]{:S(2)}) copy-start(bf16[1,1024,1024]{2,1,0:T(8,128)(2,1)} %param.31) | copy-start | bytes 6291460
  7.2 185.7 %all-gather.3.cloned.1.call-start = ((), (), s32[]{:S(2)}) async-start(), calls=%async_computation | async-start | bytes 8650752 | tf_op jit(solution)/shard_map/all_gather | solution.py:862
  9.6 185.1 %all-gather.5.cloned.1.call-start = ((), (), s32[]{:S(2)}) async-start(), calls=%async_computation.1 | async-start | bytes 8650752 | tf_op jit(solution)/shard_map/all_gather | solution.py:863
  65.6 3.6 copy-start.25
  65.6 3.7 copy-start.29
  69.2 90.8 %copy-start.26 = (f32[1,1024]{1,0:T(1,128)}, f32[1,1024]{1,0:T(1,128)S(1)}, u32[]{:S(2)}) copy-start(f32[1,1024]{1,0:T(1,128)S(1)} %get-tuple-element.158.refs_10_) | copy-start | bytes 12292
  69.3 121.5 %copy-start.27 = (f32[1,1024]{1,0:T(1,128)}, f32[1,1024]{1,0:T(1,128)S(1)}, u32[]{:S(2)}) copy-start(f32[1,1024]{1,0:T(1,128)S(1)} %get-tuple-element.163.refs_10_) | copy-start | bytes 12292
  69.3 3.8 copy-start.30
  73.0 3.7 copy-start.28
  76.7 3.8 copy-start.6
  76.7 3.8 copy-start.7
  76.7 3.8 copy-start.8
  76.7 3.8 copy-start.9
  76.8 3.7 copy-start.10
  155.0 22.9 %copy-start.13 = (f32[1024,1024]{1,0:T(8,128)}, f32[1024,1024]{1,0:T(8,128)S(1)}, u32[]{:S(2)}) copy-start(f32[1024,1024]{1,0:T(8,128)S(1)} %get-tuple-element.178.refs_15_) | copy-start | bytes 12582916
  155.0 3.6 copy-start.21
  155.0 4.3 copy-start.22
  157.0 3.8 copy-start.18
  159.3 5.2 %copy-start.3 = (bf16[256,1024]{1,0:T(8,128)(2,1)}, bf16[256,1024]{1,0:T(8,128)(2,1)S(1)}, u32[]{:S(2)}) copy-start(bf16[256,1024]{1,0:T(8,128)(2,1)S(1)} %convolution_convert_fusion.1.k_ref.refs_1_) | copy-start | bytes 1572868
  160.0 4.4 copy-start.4
  164.5 15.9 %copy-start.2 = (bf16[1024,1024]{1,0:T(8,128)(2,1)}, bf16[1024,1024]{1,0:T(8,128)(2,1)S(1)}, u32[]{:S(2)}) copy-start(bf16[1024,1024]{1,0:T(8,128)(2,1)S(1)} %add_convert_fusion.1.q_ref.refs_0_) | copy-start | bytes 6291460
  164.5 13.4 %copy-start.31 = (bf16[4,4,2,32,1024]{4,3,2,1,0:T(8,128)(2,1)S(1)}, bf16[4,4,2,32,1024]{4,3,2,1,0:T(8,128)(2,1)}, u32[]{:S(2)}) copy-start(bf16[4,4,2,32,1024]{4,3,2,1,0:T(8,128)(2,1)} %get-tuple-element.100) | copy-start | bytes 6291460
  180.4 5.7 %copy-start.16 = (f32[1024,1024]{1,0:T(8,128)}, f32[1024,1024]{1,0:T(8,128)S(1)}, u32[]{:S(2)}) copy-start(f32[1024,1024]{1,0:T(8,128)S(1)} %get-tuple-element.180.after_in) | copy-start | bytes 12582916
  186.1 4.7 copy-start.15
  (10 other events, 23.1 us)
Sparse Core Ops, SparseCore 0:
  11.6 98.9 all-gather.2
  113.6 81.0 all-gather.4
